TPU v7x, 128 devices: a whole 4x4x4 slice. The times are simulated.
128 devices in a mesh: clip: 32 (over y, z, x_lo), seq: 4 (over x_hi, core).
Axes of the slice: x: 4 (x_hi: 2, x_lo: 2; x = x_hi * 2 + x_lo), y: 4, z: 4, core: 2. Of those that a mesh axis runs over, the one named last changes fastest.
Arguments:
- latents: bfloat16 [32, 4, 160, 1152], P('clip', 'seq'), may hold values from -6 to 6
- noise_sample: bfloat16 [32, 4, 160, 1152], P('clip', 'seq'), may hold values from -6 to 6
- timesteps: int32 [32], P('clip'), may hold values from 0 to 999
- text_states: bfloat16 [32, 120, 4096], P('clip'), may hold values from -6 to 6
- text_lengths: int32 [32], P('clip'), may hold values from 91 to 120, as said below
- cotangent: bfloat16 [32, 4, 160, 1152], P('clip', 'seq'), may hold values from -6 to 6
- time_input: bfloat16 [256, 1152], P(('clip', 'seq')), may hold values from -0.375 to 0.375
- time_output: bfloat16 [1152, 6912], P(('clip', 'seq')), may hold values from -0.1875 to 0.1875
- spatial_table: bfloat16 [6, 1152], P(None, ('clip', 'seq')), may hold values from -3 to 3
- spatial_projection: bfloat16 [1152, 3456], P(('clip', 'seq')), may hold values from -0.1875 to 0.1875
- spatial_output: bfloat16 [1152, 1152], P(('clip', 'seq')), may hold values from -0.625 to 0.625
- spatial_up: bfloat16 [1152, 4608], P(('clip', 'seq')), may hold values from -0.1875 to 0.1875
- spatial_down: bfloat16 [4608, 1152], P(('clip', 'seq')), may hold values from -0.09375 to 0.09375
- temporal_table: bfloat16 [6, 1152], P(None, ('clip', 'seq')), may hold values from -3 to 3
- temporal_projection: bfloat16 [1152, 3456], P(('clip', 'seq')), may hold values from -0.1875 to 0.1875
- temporal_output: bfloat16 [1152, 1152], P(('clip', 'seq')), may hold values from -0.25 to 0.25
- cross_query: bfloat16 [1152, 1152], P(('clip', 'seq')), may hold values from -0.1875 to 0.1875
- cross_text: bfloat16 [4096, 2304], P(('clip', 'seq')), may hold values from -0.09375 to 0.09375
- cross_output: bfloat16 [1152, 1152], P(('clip', 'seq')), may hold values from -0.5 to 0.5
- cross_gain: bfloat16 [1152], P(('clip', 'seq')), may hold values from 0.099609375 to 1.8984375
- temporal_up: bfloat16 [1152, 4608], P(('clip', 'seq')), may hold values from -0.1875 to 0.1875
- temporal_down: bfloat16 [4608, 1152], P(('clip', 'seq')), may hold values from -0.09375 to 0.09375
Outputs:
- activations: bfloat16 [32, 4, 160, 1152], P('clip', 'seq')
- latent_grad: float32 [32, 4, 160, 1152], P('clip', 'seq')
- grad_time_input: float32 [256, 1152], P(('clip', 'seq'))
- grad_time_output: float32 [1152, 6912], P(('clip', 'seq'))
- grad_spatial_table: float32 [6, 1152], P(None, ('clip', 'seq'))
- grad_spatial_projection: float32 [1152, 3456], P(('clip', 'seq'))
- grad_spatial_output: float32 [1152, 1152], P(('clip', 'seq'))
- grad_spatial_up: float32 [1152, 4608], P(('clip', 'seq'))
- grad_spatial_down: float32 [4608, 1152], P(('clip', 'seq'))
- grad_temporal_table: float32 [6, 1152], P(None, ('clip', 'seq'))
- grad_temporal_projection: float32 [1152, 3456], P(('clip', 'seq'))
- grad_temporal_output: float32 [1152, 1152], P(('clip', 'seq'))
- grad_cross_query: float32 [1152, 1152], P(('clip', 'seq'))
- grad_cross_text: float32 [4096, 2304], P(('clip', 'seq'))
- grad_cross_output: float32 [1152, 1152], P(('clip', 'seq'))
- grad_cross_gain: float32 [1152], P(('clip', 'seq'))
- grad_temporal_up: float32 [1152, 4608], P(('clip', 'seq'))
- grad_temporal_down: float32 [4608, 1152], P(('clip', 'seq'))
Inputs may be any that keep to these rules, and one draw needn't show every extreme that they name: Each clip's caption uses its first text_lengths tokens; some clip uses all 120.
All inputs are finite; a program needn't handle non-finite values.
Results may differ from a plain program's by a relative error of at most 0.035.
Values may be sent and summed in bfloat16 or wider, within the bound.
No kernel may reach another device: no remote copies, remote signals or barrier semaphores. Data moves between devices by JAX's collectives and lax.ppermute only.
A program may use at most 640 MiB of HBM per device.

v0:
```python
from functools import partial
import math

import jax
import jax.numpy as jnp
from jax import lax
from jax.sharding import PartitionSpec as P

HEADS = 16
HEAD_DIM = 72
FREQ = 256
STEPS = 1000


EPSILON = 1e-06
MASK_FILL = -1000000000.0
SPATIAL_FORMS = ("fphe,fqhe->fhpq", "fhpq,fqhe->fphe", "fhpq,fphe->fqhe")
TEMPORAL_FORMS = ("fphe,gphe->phfg", "phfg,gphe->fphe", "phfg,fphe->gphe")
CROSS_FORMS = ("fphe,lhe->fphl", "fphl,lhe->fphe", "fphl,fphe->lhe")


def noise_table(count):
    beta_values = jnp.linspace(0.0001, 0.02, count, dtype=jnp.float32)
    return jnp.cumprod(1.0 - beta_values)


def time_features(timestep, feature_count):
    half_count = feature_count // 2
    frequency = jnp.exp(-math.log(10000.0) * jnp.arange(half_count, dtype=jnp.float32) / half_count)
    angles = timestep.astype(jnp.float32) * frequency
    return jnp.concatenate([jnp.cos(angles), jnp.sin(angles)])


def normalize(values):
    average = jnp.mean(values, axis=-1, keepdims=True)
    centred = values - average
    inverse_std = lax.rsqrt(jnp.mean(centred * centred, axis=-1, keepdims=True) + EPSILON)
    return (centred * inverse_std, inverse_std)


def norm_back(normal_rows, inverse_std, normal_grad):
    first_mean = jnp.mean(normal_grad, axis=-1, keepdims=True)
    second_mean = jnp.mean(normal_grad * normal_rows, axis=-1, keepdims=True)
    return inverse_std * (normal_grad - first_mean - normal_rows * second_mean)


def row_total(values):
    return jnp.sum(values.reshape(-1, values.shape[-1]), axis=0)


def outer_sum(operand, partner):
    return lax.dot_general(
        operand.reshape(-1, operand.shape[-1]),
        partner.reshape(-1, partner.shape[-1]),
        (((0,), (0,)), ((), ())),
        preferred_element_type=jnp.float32,
    )


def transposed_product(operand, weight):
    return lax.dot_general(
        operand, weight, (((operand.ndim - 1,), (1,)), ((), ())), preferred_element_type=jnp.float32
    )


def attend_forward(queries, key_rows, value_rows, einsum_forms, visible):
    factor = queries.shape[-1] ** (-0.5)
    scores = (
        jnp.einsum(einsum_forms[0], queries, key_rows, preferred_element_type=jnp.float32) * factor
    )
    if visible is not None:
        scores = jnp.where(visible, scores, MASK_FILL)
    row_max = jnp.max(scores, axis=-1, keepdims=True)
    exponent = jnp.exp(scores - row_max)
    denominator = jnp.sum(exponent, axis=-1, keepdims=True)
    probability = (exponent / denominator).astype(jnp.bfloat16)
    mixed_rows = jnp.einsum(
        einsum_forms[1], probability, value_rows, preferred_element_type=jnp.float32
    )
    return (mixed_rows.astype(jnp.bfloat16), row_max + jnp.log(denominator))


def attend_back(queries, key_rows, value_rows, mixed_grad, logsum, einsum_forms, visible):
    factor = queries.shape[-1] ** (-0.5)
    scores = (
        jnp.einsum(einsum_forms[0], queries, key_rows, preferred_element_type=jnp.float32) * factor
    )
    if visible is not None:
        scores = jnp.where(visible, scores, MASK_FILL)
    probability = jnp.exp(scores - logsum)
    prob_grad = jnp.einsum(
        einsum_forms[0], mixed_grad, value_rows, preferred_element_type=jnp.float32
    )
    value_grad = jnp.einsum(
        einsum_forms[2],
        probability.astype(jnp.bfloat16),
        mixed_grad,
        preferred_element_type=jnp.float32,
    )
    score_grad = probability * (
        prob_grad - jnp.sum(probability * prob_grad, axis=-1, keepdims=True)
    )
    score_grad = score_grad.astype(jnp.bfloat16)
    query_grad = (
        jnp.einsum(einsum_forms[1], score_grad, key_rows, preferred_element_type=jnp.float32)
        * factor
    )
    key_grad = (
        jnp.einsum(einsum_forms[2], score_grad, queries, preferred_element_type=jnp.float32)
        * factor
    )
    return (query_grad, key_grad, value_grad)


def attention_forward(hidden_state, modulation, projection, out_weight, einsum_forms):
    normal_rows, inverse_std = normalize(hidden_state)
    normed = (normal_rows * (1.0 + modulation[1]) + modulation[0]).astype(jnp.bfloat16)
    packed = jnp.dot(normed, projection, preferred_element_type=jnp.float32).astype(jnp.bfloat16)
    packed = packed.reshape(hidden_state.shape[:-1] + (3, HEADS, HEAD_DIM))
    queries = packed[..., 0, :, :]
    key_rows = packed[..., 1, :, :]
    value_rows = packed[..., 2, :, :]
    mixed_rows, logsum = attend_forward(queries, key_rows, value_rows, einsum_forms, None)
    mixed_rows = mixed_rows.reshape(hidden_state.shape)
    branch = jnp.dot(mixed_rows, out_weight, preferred_element_type=jnp.float32)
    stored = (
        normal_rows,
        inverse_std,
        normed,
        queries,
        key_rows,
        value_rows,
        logsum,
        mixed_rows,
        branch,
    )
    return (hidden_state + modulation[2] * branch, stored)


def attention_back(incoming, stored, modulation, projection, out_weight, einsum_forms):
    normal_rows, inverse_std, normed, queries, key_rows, value_rows, logsum, mixed_rows, branch = (
        stored
    )
    gate_grad = row_total(incoming * branch)
    branch_grad = (modulation[2] * incoming).astype(jnp.bfloat16)
    out_grad = outer_sum(mixed_rows, branch_grad)
    mixed_grad = (
        transposed_product(branch_grad, out_weight).astype(jnp.bfloat16).reshape(queries.shape)
    )
    query_grad, key_grad, value_grad = attend_back(
        queries, key_rows, value_rows, mixed_grad, logsum, einsum_forms, None
    )
    packed_grad = jnp.stack([query_grad, key_grad, value_grad], axis=-3).astype(jnp.bfloat16)
    packed_grad = packed_grad.reshape(incoming.shape[:-1] + (3 * incoming.shape[-1],))
    projection_grad = outer_sum(normed, packed_grad)
    normed_grad = transposed_product(packed_grad, projection)
    scale_grad = row_total(normed_grad * normal_rows)
    shift_grad = row_total(normed_grad)
    upstream = incoming + norm_back(normal_rows, inverse_std, normed_grad * (1.0 + modulation[1]))
    return (upstream, (projection_grad, out_grad), (shift_grad, scale_grad, gate_grad))


def cross_forward(
    hidden_state, gain_vector, query_weight, text_keys, text_values, out_weight, visible
):
    normal_rows, inverse_std = normalize(hidden_state)
    normed = (normal_rows * gain_vector).astype(jnp.bfloat16)
    queries = jnp.dot(normed, query_weight, preferred_element_type=jnp.float32).astype(jnp.bfloat16)
    queries = queries.reshape(hidden_state.shape[:-1] + (HEADS, HEAD_DIM))
    mixed_rows, logsum = attend_forward(queries, text_keys, text_values, CROSS_FORMS, visible)
    mixed_rows = mixed_rows.reshape(hidden_state.shape)
    branch = jnp.dot(mixed_rows, out_weight, preferred_element_type=jnp.float32)
    return (hidden_state + branch, (normal_rows, inverse_std, normed, queries, logsum, mixed_rows))


def cross_back(
    incoming, stored, gain_vector, query_weight, text_keys, text_values, out_weight, visible
):
    normal_rows, inverse_std, normed, queries, logsum, mixed_rows = stored
    branch_grad = incoming.astype(jnp.bfloat16)
    out_grad = outer_sum(mixed_rows, branch_grad)
    mixed_grad = (
        transposed_product(branch_grad, out_weight).astype(jnp.bfloat16).reshape(queries.shape)
    )
    query_grad, key_grad, value_grad = attend_back(
        queries, text_keys, text_values, mixed_grad, logsum, CROSS_FORMS, visible
    )
    query_grad = query_grad.astype(jnp.bfloat16).reshape(incoming.shape)
    query_weight_grad = outer_sum(normed, query_grad)
    normed_grad = transposed_product(query_grad, query_weight)
    gain_grad = row_total(normed_grad * normal_rows)
    upstream = incoming + norm_back(normal_rows, inverse_std, normed_grad * gain_vector)
    text_terms = jnp.concatenate(
        [key_grad.reshape(key_grad.shape[0], -1), value_grad.reshape(value_grad.shape[0], -1)],
        axis=1,
    )
    return (upstream, gain_grad, query_weight_grad, out_grad, text_terms)


def feed_forward(hidden_state, modulation, up_weight, down_weight):
    normal_rows, inverse_std = normalize(hidden_state)
    normed = (normal_rows * (1.0 + modulation[4]) + modulation[3]).astype(jnp.bfloat16)
    inner_rows = jnp.dot(normed, up_weight, preferred_element_type=jnp.float32)
    activated = jax.nn.gelu(inner_rows, approximate=True).astype(jnp.bfloat16)
    output = jnp.dot(activated, down_weight, preferred_element_type=jnp.float32)
    return (
        hidden_state + modulation[5] * output,
        (normal_rows, inverse_std, normed, inner_rows, activated, output),
    )


def feed_forward_back(incoming, stored, modulation, up_weight, down_weight):
    normal_rows, inverse_std, normed, inner_rows, activated, output = stored
    gate_grad = row_total(incoming * output)
    output_grad = (modulation[5] * incoming).astype(jnp.bfloat16)
    down_grad = outer_sum(activated, output_grad)
    active_grad = transposed_product(output_grad, down_weight)
    smooth_back = jax.vjp(partial(jax.nn.gelu, approximate=True), inner_rows)[1]
    inner_grad = smooth_back(active_grad)[0].astype(jnp.bfloat16)
    up_grad = outer_sum(normed, inner_grad)
    normed_grad = transposed_product(inner_grad, up_weight)
    scale_grad = row_total(normed_grad * normal_rows)
    shift_grad = row_total(normed_grad)
    upstream = incoming + norm_back(normal_rows, inverse_std, normed_grad * (1.0 + modulation[4]))
    return (upstream, (up_grad, down_grad), (shift_grad, scale_grad, gate_grad))


def local(
    latents,
    noise_sample,
    timesteps,
    text_states,
    text_lengths,
    cotangent,
    time_input,
    time_output,
    spatial_table,
    spatial_projection,
    spatial_output,
    spatial_up,
    spatial_down,
    temporal_table,
    temporal_projection,
    temporal_output,
    cross_query,
    cross_text,
    cross_output,
    cross_gain,
    temporal_up,
    temporal_down,
):
    spatial_full = (
        lax.all_gather(time_input, ("clip", "seq"), axis=0, tiled=True),
        lax.all_gather(time_output, ("clip", "seq"), axis=0, tiled=True),
        lax.all_gather(spatial_table, ("clip", "seq"), axis=1, tiled=True),
        lax.all_gather(spatial_projection, ("clip", "seq"), axis=0, tiled=True),
        lax.all_gather(spatial_output, ("clip", "seq"), axis=0, tiled=True),
        lax.all_gather(spatial_up, ("clip", "seq"), axis=0, tiled=True),
        lax.all_gather(spatial_down, ("clip", "seq"), axis=0, tiled=True),
    )
    (
        full_time_input,
        full_time_output,
        full_spatial_table,
        full_spatial_projection,
        full_spatial_output,
        full_spatial_up,
        full_spatial_down,
    ) = spatial_full
    clip_step = timesteps[0]
    alpha_bars = noise_table(STEPS)
    picked = jnp.sum(jnp.where(jnp.arange(STEPS) == clip_step, alpha_bars, 0.0))
    signal_scale = jnp.sqrt(picked)
    hidden_state = signal_scale * latents[0].astype(jnp.float32) + jnp.sqrt(
        1.0 - picked
    ) * noise_sample[0].astype(jnp.float32)
    embedded = time_features(clip_step, FREQ).astype(jnp.bfloat16)
    pre_time = jnp.dot(embedded, full_time_input, preferred_element_type=jnp.float32)
    lifted = jax.nn.silu(pre_time).astype(jnp.bfloat16)
    shared = jnp.dot(lifted, full_time_output, preferred_element_type=jnp.float32).reshape(6, -1)
    spatial_mod = full_spatial_table.astype(jnp.float32) + shared
    hidden_state, spatial_attention = attention_forward(
        hidden_state, spatial_mod, full_spatial_projection, full_spatial_output, SPATIAL_FORMS
    )
    hidden_state, spatial_mlp = feed_forward(
        hidden_state, spatial_mod, full_spatial_up, full_spatial_down
    )
    patch_rows = lax.all_to_all(
        hidden_state.astype(jnp.bfloat16), "seq", split_axis=1, concat_axis=0, tiled=True
    )
    temporal_full = (
        lax.all_gather(temporal_table, ("clip", "seq"), axis=1, tiled=True),
        lax.all_gather(temporal_projection, ("clip", "seq"), axis=0, tiled=True),
        lax.all_gather(temporal_output, ("clip", "seq"), axis=0, tiled=True),
        lax.all_gather(cross_query, ("clip", "seq"), axis=0, tiled=True),
        lax.all_gather(cross_text, ("clip", "seq"), axis=0, tiled=True),
        lax.all_gather(cross_output, ("clip", "seq"), axis=0, tiled=True),
        lax.all_gather(cross_gain, ("clip", "seq"), axis=0, tiled=True),
        lax.all_gather(temporal_up, ("clip", "seq"), axis=0, tiled=True),
        lax.all_gather(temporal_down, ("clip", "seq"), axis=0, tiled=True),
    )
    (
        full_temporal_table,
        full_temporal_projection,
        full_temporal_output,
        full_cross_query,
        full_cross_text,
        full_cross_output,
        full_cross_gain,
        full_temporal_up,
        full_temporal_down,
    ) = temporal_full
    text_share = text_states.shape[1] // lax.axis_size("seq")
    own_text = lax.dynamic_slice_in_dim(
        text_states[0], lax.axis_index("seq") * text_share, text_share, 0
    )
    text_rows = jnp.dot(text_states[0], full_cross_text, preferred_element_type=jnp.float32).astype(
        jnp.bfloat16
    )
    model_width = text_rows.shape[1] // 2
    text_keys = text_rows[:, :model_width].reshape(-1, HEADS, HEAD_DIM)
    text_values = text_rows[:, model_width:].reshape(-1, HEADS, HEAD_DIM)
    visible = jnp.arange(text_states.shape[1]) < text_lengths[0]
    temporal_mod = full_temporal_table.astype(jnp.float32) + shared
    hidden_state = patch_rows.astype(jnp.float32)
    hidden_state, temporal_attention = attention_forward(
        hidden_state, temporal_mod, full_temporal_projection, full_temporal_output, TEMPORAL_FORMS
    )
    hidden_state, cross_stored = cross_forward(
        hidden_state,
        full_cross_gain.astype(jnp.float32),
        full_cross_query,
        text_keys,
        text_values,
        full_cross_output,
        visible,
    )
    hidden_state, temporal_mlp = feed_forward(
        hidden_state, temporal_mod, full_temporal_up, full_temporal_down
    )
    finished = lax.all_to_all(
        hidden_state.astype(jnp.bfloat16), "seq", split_axis=0, concat_axis=1, tiled=True
    )
    activations = finished[None]
    temporal_back = (
        lax.all_gather(temporal_table, ("clip", "seq"), axis=1, tiled=True),
        lax.all_gather(temporal_projection, ("clip", "seq"), axis=0, tiled=True),
        lax.all_gather(temporal_output, ("clip", "seq"), axis=0, tiled=True),
        lax.all_gather(cross_query, ("clip", "seq"), axis=0, tiled=True),
        lax.all_gather(cross_text, ("clip", "seq"), axis=0, tiled=True),
        lax.all_gather(cross_output, ("clip", "seq"), axis=0, tiled=True),
        lax.all_gather(cross_gain, ("clip", "seq"), axis=0, tiled=True),
        lax.all_gather(temporal_up, ("clip", "seq"), axis=0, tiled=True),
        lax.all_gather(temporal_down, ("clip", "seq"), axis=0, tiled=True),
    )
    (
        back_temporal_table,
        back_temporal_projection,
        back_temporal_output,
        back_cross_query,
        back_cross_text,
        back_cross_output,
        back_cross_gain,
        back_temporal_up,
        back_temporal_down,
    ) = temporal_back
    incoming = lax.all_to_all(cotangent[0], "seq", split_axis=1, concat_axis=0, tiled=True).astype(
        jnp.float32
    )
    incoming, (temporal_up_grad, temporal_down_grad), temporal_mlp_mod = feed_forward_back(
        incoming, temporal_mlp, temporal_mod, back_temporal_up, back_temporal_down
    )
    incoming, gain_grad, cross_query_grad, cross_output_grad, text_terms = cross_back(
        incoming,
        cross_stored,
        back_cross_gain.astype(jnp.float32),
        back_cross_query,
        text_keys,
        text_values,
        back_cross_output,
        visible,
    )
    incoming, (temporal_projection_grad, temporal_output_grad), temporal_attention_mod = (
        attention_back(
            incoming,
            temporal_attention,
            temporal_mod,
            back_temporal_projection,
            back_temporal_output,
            TEMPORAL_FORMS,
        )
    )
    temporal_mod_grad = jnp.stack(temporal_attention_mod + temporal_mlp_mod)
    text_sum = lax.psum_scatter(
        text_terms.astype(jnp.bfloat16), "seq", scatter_dimension=0, tiled=True
    )
    cross_text_grad = outer_sum(own_text, text_sum)
    temporal_grads = (
        lax.psum_scatter(temporal_mod_grad, ("clip", "seq"), scatter_dimension=1, tiled=True),
        lax.psum_scatter(
            temporal_projection_grad, ("clip", "seq"), scatter_dimension=0, tiled=True
        ),
        lax.psum_scatter(temporal_output_grad, ("clip", "seq"), scatter_dimension=0, tiled=True),
        lax.psum_scatter(cross_query_grad, ("clip", "seq"), scatter_dimension=0, tiled=True),
        lax.psum_scatter(cross_text_grad, ("clip", "seq"), scatter_dimension=0, tiled=True),
        lax.psum_scatter(cross_output_grad, ("clip", "seq"), scatter_dimension=0, tiled=True),
        lax.psum_scatter(gain_grad, ("clip", "seq"), scatter_dimension=0, tiled=True),
        lax.psum_scatter(temporal_up_grad, ("clip", "seq"), scatter_dimension=0, tiled=True),
        lax.psum_scatter(temporal_down_grad, ("clip", "seq"), scatter_dimension=0, tiled=True),
    )
    frame_grad = lax.all_to_all(
        incoming.astype(jnp.bfloat16), "seq", split_axis=0, concat_axis=1, tiled=True
    ).astype(jnp.float32)
    spatial_back = (
        lax.all_gather(time_input, ("clip", "seq"), axis=0, tiled=True),
        lax.all_gather(time_output, ("clip", "seq"), axis=0, tiled=True),
        lax.all_gather(spatial_table, ("clip", "seq"), axis=1, tiled=True),
        lax.all_gather(spatial_projection, ("clip", "seq"), axis=0, tiled=True),
        lax.all_gather(spatial_output, ("clip", "seq"), axis=0, tiled=True),
        lax.all_gather(spatial_up, ("clip", "seq"), axis=0, tiled=True),
        lax.all_gather(spatial_down, ("clip", "seq"), axis=0, tiled=True),
    )
    (
        back_time_input,
        back_time_output,
        back_spatial_table,
        back_spatial_projection,
        back_spatial_output,
        back_spatial_up,
        back_spatial_down,
    ) = spatial_back
    frame_grad, (spatial_up_grad, spatial_down_grad), spatial_mlp_mod = feed_forward_back(
        frame_grad, spatial_mlp, spatial_mod, back_spatial_up, back_spatial_down
    )
    frame_grad, (spatial_projection_grad, spatial_output_grad), spatial_attention_mod = (
        attention_back(
            frame_grad,
            spatial_attention,
            spatial_mod,
            back_spatial_projection,
            back_spatial_output,
            SPATIAL_FORMS,
        )
    )
    spatial_mod_grad = jnp.stack(spatial_attention_mod + spatial_mlp_mod)
    shared_grad = (spatial_mod_grad + temporal_mod_grad).reshape(-1)
    time_output_grad = jnp.outer(lifted.astype(jnp.float32), shared_grad)
    lifted_grad = jnp.dot(
        back_time_output,
        shared_grad,
        precision=lax.Precision.HIGHEST,
        preferred_element_type=jnp.float32,
    )
    silu_back = jax.vjp(jax.nn.silu, pre_time)[1]
    pre_grad = silu_back(lifted_grad)[0]
    time_input_grad = jnp.outer(embedded.astype(jnp.float32), pre_grad)
    spatial_grads = (
        lax.psum_scatter(time_input_grad, ("clip", "seq"), scatter_dimension=0, tiled=True),
        lax.psum_scatter(time_output_grad, ("clip", "seq"), scatter_dimension=0, tiled=True),
        lax.psum_scatter(spatial_mod_grad, ("clip", "seq"), scatter_dimension=1, tiled=True),
        lax.psum_scatter(spatial_projection_grad, ("clip", "seq"), scatter_dimension=0, tiled=True),
        lax.psum_scatter(spatial_output_grad, ("clip", "seq"), scatter_dimension=0, tiled=True),
        lax.psum_scatter(spatial_up_grad, ("clip", "seq"), scatter_dimension=0, tiled=True),
        lax.psum_scatter(spatial_down_grad, ("clip", "seq"), scatter_dimension=0, tiled=True),
    )
    latent_grad = (signal_scale * frame_grad)[None]
    return (activations, latent_grad) + tuple(spatial_grads) + tuple(temporal_grads)


def solution(mesh):
    in_specs = (
        P("clip", "seq", None, None),
        P("clip", "seq", None, None),
        P("clip"),
        P("clip", None, None),
        P("clip"),
        P("clip", "seq", None, None),
        P(("clip", "seq"), None),
        P(("clip", "seq"), None),
        P(None, ("clip", "seq")),
        P(("clip", "seq"), None),
        P(("clip", "seq"), None),
        P(("clip", "seq"), None),
        P(("clip", "seq"), None),
        P(None, ("clip", "seq")),
        P(("clip", "seq"), None),
        P(("clip", "seq"), None),
        P(("clip", "seq"), None),
        P(("clip", "seq"), None),
        P(("clip", "seq"), None),
        P(("clip", "seq")),
        P(("clip", "seq"), None),
        P(("clip", "seq"), None),
    )
    out_specs = (
        P("clip", "seq", None, None),
        P("clip", "seq", None, None),
        P(("clip", "seq"), None),
        P(("clip", "seq"), None),
        P(None, ("clip", "seq")),
        P(("clip", "seq"), None),
        P(("clip", "seq"), None),
        P(("clip", "seq"), None),
        P(("clip", "seq"), None),
        P(None, ("clip", "seq")),
        P(("clip", "seq"), None),
        P(("clip", "seq"), None),
        P(("clip", "seq"), None),
        P(("clip", "seq"), None),
        P(("clip", "seq"), None),
        P(("clip", "seq")),
        P(("clip", "seq"), None),
        P(("clip", "seq"), None),
    )
    return jax.shard_map(local, mesh=mesh, in_specs=in_specs, out_specs=out_specs, check_vma=False)
```

profile of v0, /device:TPU:0, one launch (start us, length us, event | category | flops | bytes accessed | tf_op | source)
XLA Modules:
  0.0 5063.5 jit_solution(13451172410848165696)
XLA Ops:
  30.3 180.9 %all-gather.1 = bf16[128,2,1152]{2,1,0:T(2,128)(2,1)S(1)} all-gather(bf16[1,2,1152]{2,1,0:T(2,128)(2,1)S(1)} %bitcast.406), channel_id=1, replica_groups=mesh['clip'=32,'seq'=4] {'clip','seq'}, dimensions={0}, use_global_device_ids=true | all-gather | bytes 594432 | tf_op jit(solution)/shard_map/all_gather | solution.py:253
  213.6 62.3 %all-reduce.1 = bf16[1152]{0:T(1024)(128)(2,1)S(1)} all-reduce(bf16[1152]{0:T(1024)(128)(2,1)S(1)} %dynamic-update-slice), channel_id=1, replica_groups=mesh['clip'=32,'seq'=4] {'clip','seq'}, use_global_device_ids=true, to_apply=%add.1 | all-reduce | flops 1152 | bytes 4608
  276.5 173.9 %all-gather = bf16[128,9,6]{1,2,0:T(8,128)(2,1)S(1)} all-gather(bf16[1,9,6]{1,2,0:T(8,128)(2,1)S(1)} %bitcast.407), channel_id=1, replica_groups=mesh['clip'=32,'seq'=4] {'clip','seq'}, dimensions={0}, use_global_device_ids=true | all-gather | bytes 13932 | tf_op jit(solution)/shard_map/all_gather | solution.py:255
  450.7 171.3 %all-gather.7 = bf16[128,9,6]{1,2,0:T(8,128)(2,1)S(1)} all-gather(bf16[1,9,6]{1,2,0:T(8,128)(2,1)S(1)} %bitcast.408), channel_id=1, replica_groups=mesh['clip'=32,'seq'=4] {'clip','seq'}, dimensions={0}, use_global_device_ids=true | all-gather | bytes 13932 | tf_op jit(solution)/shard_map/all_gather | solution.py:292
  641.5 173.2 %all-gather.45.cloned.1.call-done = bf16[128,9,1152]{2,1,0:T(8,128)(2,1)} async-done(((bf16[1,9,1152]{2,1,0:T(8,128)(2,1)}), bf16[128,9,1152]{2,1,0:T(8,128)(2,1)}) %all-gather.45.cloned.1.call-update) | async-done | bytes 2654224 | tf_op jit(solution)/shard_map/all_gather | solution.py:297
  820.4 205.2 %all-gather.31.cloned.1.call-done = bf16[128,9,3456]{2,1,0:T(8,128)(2,1)} async-done(((bf16[1,9,3456]{2,1,0:T(8,128)(2,1)}), bf16[128,9,3456]{2,1,0:T(8,128)(2,1)}) %all-gather.31.cloned.1.call-update) | async-done | bytes 7962640 | tf_op jit(solution)/shard_map/all_gather | solution.py:256
  1040.1 196.3 %all-gather.39.cloned.1.call-done = bf16[128,9,3456]{2,1,0:T(8,128)(2,1)} async-done(((bf16[1,9,3456]{2,1,0:T(8,128)(2,1)}), bf16[128,9,3456]{2,1,0:T(8,128)(2,1)}) %all-gather.39.cloned.1.call-update) | async-done | bytes 7962640 | tf_op jit(solution)/shard_map/all_gather | solution.py:293
  1250.8 204.4 %all-gather.35.cloned.1.call-done = bf16[128,9,4608]{2,1,0:T(8,128)(2,1)} async-done(((bf16[1,9,4608]{2,1,0:T(8,128)(2,1)}), bf16[128,9,4608]{2,1,0:T(8,128)(2,1)}) %all-gather.35.cloned.1.call-update) | async-done | bytes 10616848 | tf_op jit(solution)/shard_map/all_gather | solution.py:258
  1455.2 17.4 reshape.946
  1472.7 191.1 %all-gather.37.cloned.1.call-done = bf16[128,36,1152]{2,1,0:T(8,128)(2,1)} async-done(((bf16[1,36,1152]{2,1,0:T(8,128)(2,1)}), bf16[128,36,1152]{2,1,0:T(8,128)(2,1)}) %all-gather.37.cloned.1.call-update) | async-done | bytes 10616848 | tf_op jit(solution)/shard_map/all_gather | solution.py:259
  1680.1 202.2 %all-gather.47.cloned.1.call-done = bf16[128,9,4608]{2,1,0:T(8,128)(2,1)} async-done(((bf16[1,9,4608]{2,1,0:T(8,128)(2,1)}), bf16[128,9,4608]{2,1,0:T(8,128)(2,1)}) %all-gather.47.cloned.1.call-update) | async-done | bytes 10616848 | tf_op jit(solution)/shard_map/all_gather | solution.py:299
  1882.3 17.4 reshape.977
  1899.8 191.2 %all-gather.49.cloned.1.call-done = bf16[128,36,1152]{2,1,0:T(8,128)(2,1)} async-done(((bf16[1,36,1152]{2,1,0:T(8,128)(2,1)}), bf16[128,36,1152]{2,1,0:T(8,128)(2,1)}) %all-gather.49.cloned.1.call-update) | async-done | bytes 10616848 | tf_op jit(solution)/shard_map/all_gather | solution.py:300
  2107.4 215.1 %all-gather.29.cloned.1.call-done = bf16[128,9,6912]{2,1,0:T(8,128)(2,1)} async-done(((bf16[1,9,6912]{2,1,0:T(8,128)(2,1)}), bf16[128,9,6912]{2,1,0:T(8,128)(2,1)}) %all-gather.29.cloned.1.call-update) | async-done | bytes 15925264 | tf_op jit(solution)/shard_map/all_gather | solution.py:254
  2322.4 22.5 reshape.940
  2424.7 118.3 %all-gather.27.cloned.1.call-done = bf16[4096,2304]{1,0:T(8,128)(2,1)} async-done(((bf16[32,2304]{1,0:T(8,128)(2,1)}), bf16[4096,2304]{1,0:T(8,128)(2,1)}) %all-gather.27.cloned.1.call-update) | async-done | bytes 18874384 | tf_op jit(solution)/shard_map/all_gather | solution.py:296
  2815.5 914.6 %fusion.105 = (f32[48,1152]{1,0:T(8,128)S(1)}, f32[48,1152]{1,0:T(8,128)S(1)}) fusion(f32[4608,1152]{1,0:T(8,128)} %fusion.102, f32[4608,1152]{1,0:T(8,128)} %convolution_bitcast_fusion), kind=kCustom, calls=%all-reduce-scatter.2 | all-reduce-scatter fusion | flops 14155777 | bytes 42909696
  3807.9 29.5 collective-permute-start.16
  3952.1 19.7 collective-permute-start.56
  4006.5 20.2 collective-permute-start.48
  4087.4 73.8 %all-reduce.20 = (f32[6,1152]{1,0:T(8,128)S(1)}, f32[6,1152]{1,0:T(8,128)S(1)}, f32[1152]{0:T(1024)S(1)}) all-reduce(f32[6,1152]{1,0:T(8,128)S(1)} %stack.80, f32[6,1152]{1,0:T(8,128)S(1)} %stack.87, f32[1152]{0:T(1024)S(1)} %copy-done.155), channel_id=4, replica_groups=mesh['clip'=32,'seq'=4] {'clip','seq'}, use_global_device_ids=true, to_apply=%region_46.47.clone | all-reduce | flops 14976 | bytes 119808
  4179.1 56.3 %concatenate.27 = f32[1572,1152]{1,0:T(8,128)} concatenate(f32[36,1152]{1,0:T(8,128)} %collective-permute-done.31, f32[48,1152]{1,0:T(8,128)} %copy-done.70, f32[48,1152]{1,0:T(8,128)} %copy-done.71, f32[48,1152]{1,0:T(8,128)} %copy-done.72, f32[48,1152]{1,0:T(8,128)} %copy-done.73, f32[48,1152]{1,0:T(8,128)} %copy-done.74, f32[48,1152]{1,0:T(8,128)} %copy-done.75, ...), dimensions={0} | concatenate | bytes 14487552
  4235.5 54.7 %concatenate.28 = f32[1572,1152]{1,0:T(8,128)} concatenate(f32[36,1152]{1,0:T(8,128)} %collective-permute-done.63, f32[48,1152]{1,0:T(8,128)S(1)} %copy-done.100, f32[48,1152]{1,0:T(8,128)S(1)} %copy-done.103, f32[48,1152]{1,0:T(8,128)S(1)} %copy-done.106, f32[48,1152]{1,0:T(8,128)S(1)} %copy-done.108, f32[48,1152]{1,0:T(8,128)S(1)} %copy-done.110, f32[48,1152]{1,0:T(8,128)S(1)} %copy-done.112, ...), dimensions={0} | concatenate | bytes 14487552
  4309.7 746.2 %reduce-scatter.9.cloned.1.call-done = f32[32,2304]{1,0:T(8,128)} async-done(((f32[4096,2304]{1,0:T(8,128)}), f32[32,2304]{1,0:T(8,128)}) %reduce-scatter.9.cloned.1.call-update) | async-done | bytes 294928 | tf_op jit(solution)/shard_map/reduce_scatter | solution.py:405
  (795 shorter events, 784.6 us)
Async XLA Ops:
  7.2 617.1 %all-gather.33.cloned.1.call-start = ((), (), s32[]{:S(2)}) async-start(), calls=%async_computation.9 | async-start | bytes 4755456 | tf_op jit(solution)/shard_map/all_gather | solution.py:257
  7.9 622.1 %all-gather.41.cloned.1.call-start = ((), (), s32[]{:S(2)}) async-start(), calls=%async_computation.13 | async-start | bytes 4755456 | tf_op jit(solution)/shard_map/all_gather | solution.py:294
  8.7 627.1 %all-gather.43.cloned.1.call-start = ((), (), s32[]{:S(2)}) async-start(), calls=%async_computation.14 | async-start | bytes 4755456 | tf_op jit(solution)/shard_map/all_gather | solution.py:295
  9.4 805.2 %all-gather.45.cloned.1.call-start = ((), (), s32[]{:S(2)}) async-start(), calls=%async_computation.15 | async-start | bytes 4755456 | tf_op jit(solution)/shard_map/all_gather | solution.py:297
  10.0 1015.6 %all-gather.31.cloned.1.call-start = ((), (), s32[]{:S(2)}) async-start(), calls=%async_computation.8 | async-start | bytes 14266368 | tf_op jit(solution)/shard_map/all_gather | solution.py:256
  10.6 1225.7 %all-gather.39.cloned.1.call-start = ((), (), s32[]{:S(2)}) async-start(), calls=%async_computation.12 | async-start | bytes 14266368 | tf_op jit(solution)/shard_map/all_gather | solution.py:293
  11.2 1444.1 %all-gather.35.cloned.1.call-start = ((), (), s32[]{:S(2)}) async-start(), calls=%async_computation.10 | async-start | bytes 19021824 | tf_op jit(solution)/shard_map/all_gather | solution.py:258
  11.9 1651.8 %all-gather.37.cloned.1.call-start = ((), (), s32[]{:S(2)}) async-start(), calls=%async_computation.11 | async-start | bytes 11888640 | tf_op jit(solution)/shard_map/all_gather | solution.py:259
  12.7 1869.7 %all-gather.47.cloned.1.call-start = ((), (), s32[]{:S(2)}) async-start(), calls=%async_computation.16 | async-start | bytes 19021824 | tf_op jit(solution)/shard_map/all_gather | solution.py:299
  13.4 2077.6 %all-gather.49.cloned.1.call-start = ((), (), s32[]{:S(2)}) async-start(), calls=%async_computation.17 | async-start | bytes 11888640 | tf_op jit(solution)/shard_map/all_gather | solution.py:300
  14.0 2308.4 %all-gather.29.cloned.1.call-start = ((), (), s32[]{:S(2)}) async-start(), calls=%async_computation.7 | async-start | bytes 28532736 | tf_op jit(solution)/shard_map/all_gather | solution.py:254
  14.7 2528.3 %all-gather.27.cloned.1.call-start = ((), (), s32[]{:S(2)}) async-start(), calls=%async_computation.5 | async-start | bytes 19021824 | tf_op jit(solution)/shard_map/all_gather | solution.py:296
  21.1 601.9 %all-to-all-start.2 = ((bf16[4,2,23040]{2,1,0:T(2,128)(2,1)}), bf16[4,2,23040]{2,1,0:T(2,128)(2,1)S(1)}, u32[]{:S(2)}, u32[]{:S(2)}) async-start(bf16[4,2,23040]{2,1,0:T(2,128)(2,1)} %reshape.1022), calls=%async_computation.2 | async-start | bytes 737280 | tf_op jit(solution)/shard_map/all_to_all | solution.py:367
  2383.4 392.2 %all-reduce.27.cloned.1.call-start = ((), (), s32[]{:S(2)}) async-start(), calls=%async_computation.18 | async-start | bytes 1179648
  2669.0 1624.4 %all-reduce.29.cloned.1.call-start = ((), (), s32[]{:S(2)}) async-start(), calls=%async_computation.19 | async-start | bytes 42467328
  2683.9 1611.3 %all-reduce.31.cloned.1.call-start = ((), (), s32[]{:S(2)}) async-start(), calls=%async_computation.20 | async-start | bytes 214695936
  2773.8 2282.2 %reduce-scatter.9.cloned.1.call-start = ((), (), s32[]{:S(2)}) async-start(), calls=%async_computation.6 | async-start | bytes 38043648 | tf_op jit(solution)/shard_map/reduce_scatter | solution.py:405
  3989.3 98.0 %all-to-all-start.1 = ((bf16[4,40,1152]{2,1,0:T(8,128)(2,1)}), bf16[4,40,1152]{2,1,0:T(8,128)(2,1)S(1)}, u32[]{:S(2)}, u32[]{:S(2)}) async-start(bf16[4,40,1152]{2,1,0:T(8,128)(2,1)} %get-tuple-element.85), calls=%async_computation.1 | async-start | bytes 737280 | tf_op jit(solution)/shard_map/all_to_all | solution.py:341
  4052.2 109.5 %collective-permute-start.41 = (f32[48,1152]{1,0:T(8,128)S(1)}, f32[48,1152]{1,0:T(8,128)}, u32[]{:S(2)}, u32[]{:S(2)}) collective-permute-start(f32[48,1152]{1,0:T(8,128)S(1)} %get-tuple-element.64), channel_id=1, source_target_pairs={{0,10},{1,11},{2,12},{3,13},{4,14},{5,15},{6,16},{7,17},{8,18},{9,... | collective-permute-start | bytes 663560
  4054.2 109.5 %collective-permute-start.40 = (f32[48,1152]{1,0:T(8,128)S(1)}, f32[48,1152]{1,0:T(8,128)}, u32[]{:S(2)}, u32[]{:S(2)}) collective-permute-start(f32[48,1152]{1,0:T(8,128)S(1)} %get-tuple-element.64), channel_id=1, source_target_pairs={{0,9},{1,10},{2,11},{3,12},{4,13},{5,14},{6,15},{7,16},{8,17},{9,1... | collective-permute-start | bytes 663560
  4068.1 99.1 %collective-permute-start.39 = (f32[48,1152]{1,0:T(8,128)S(1)}, f32[48,1152]{1,0:T(8,128)}, u32[]{:S(2)}, u32[]{:S(2)}) collective-permute-start(f32[48,1152]{1,0:T(8,128)S(1)} %get-tuple-element.64), channel_id=1, source_target_pairs={{0,8},{1,9},{2,10},{3,11},{4,12},{5,13},{6,14},{7,15},{8,16},{9,17... | collective-permute-start | bytes 663560
  4075.9 96.2 %collective-permute-start.38 = (f32[48,1152]{1,0:T(8,128)S(1)}, f32[48,1152]{1,0:T(8,128)}, u32[]{:S(2)}, u32[]{:S(2)}) collective-permute-start(f32[48,1152]{1,0:T(8,128)S(1)} %get-tuple-element.64), channel_id=1, source_target_pairs={{0,7},{1,8},{2,9},{3,10},{4,11},{5,12},{6,13},{7,14},{8,15},{9,16}... | collective-permute-start | bytes 663560
  4082.9 92.9 %collective-permute-start.37 = (f32[48,1152]{1,0:T(8,128)S(1)}, f32[48,1152]{1,0:T(8,128)}, u32[]{:S(2)}, u32[]{:S(2)}) collective-permute-start(f32[48,1152]{1,0:T(8,128)S(1)} %get-tuple-element.64), channel_id=1, source_target_pairs={{0,6},{1,7},{2,8},{3,9},{4,10},{5,11},{6,12},{7,13},{8,14},{9,15},... | collective-permute-start | bytes 663560
  4161.7 73.7 %collective-permute-start.36 = (f32[48,1152]{1,0:T(8,128)S(1)}, f32[48,1152]{1,0:T(8,128)}, u32[]{:S(2)}, u32[]{:S(2)}) collective-permute-start(f32[48,1152]{1,0:T(8,128)S(1)} %get-tuple-element.64), channel_id=1, source_target_pairs={{0,5},{1,6},{2,7},{3,8},{4,9},{5,10},{6,11},{7,12},{8,13},{9,14},{... | collective-permute-start | bytes 663560
  (261 other events, 20186.7 us)
Sparse Core Ops, SparseCore 0:
  9.8 205.2 all-gather.32
  216.8 198.1 all-gather.40
  416.7 198.1 all-gather.42
  616.5 198.1 all-gather.44
  816.2 209.3 all-gather.30
  1027.2 209.1 all-gather.38
  1238.1 217.1 all-gather.34
  1457.0 206.7 all-gather.36
  1665.5 216.8 all-gather.46
  1883.9 207.0 all-gather.48
  2092.7 229.6 all-gather.28
  2324.0 219.0 all-gather.26
  2657.6 42.3 all-reduce.26
  2705.4 286.6 all-reduce.28
  2998.3 1261.7 all-reduce.30
  4263.1 792.8 reduce-scatter.8
where the time goes:
time: 5080 us; the launch traced here: 5060 us
  waiting for transfers between devices  2510 us (49%)
  blocking collectives  1580 us (31%)
  local copies, waits for them, and re-layouts  341 us (7%)
  starting transfers between devices  331 us (7%)
  matrix products  237 us (5%)
    unnamed x3, blocking collectives  1050 us
    reduce_scatter x1, waiting for transfers between devices, local(): lax.psum_scatter(cross_text_grad, ('clip', 'seq'), scatter_dimension=0, t...  746 us
    unnamed x67, starting transfers between devices  314 us
    unnamed x444, local copies, waits for them, and re-layouts  293 us
    all_gather x1, waiting for transfers between devices, local(): lax.all_gather(time_output, ('clip', 'seq'), axis=0, tiled=True)  215 us
    all_gather x1, waiting for transfers between devices, local(): lax.all_gather(spatial_projection, ('clip', 'seq'), axis=0, tiled=True)  205 us
    all_gather x1, waiting for transfers between devices, local(): lax.all_gather(spatial_up, ('clip', 'seq'), axis=0, tiled=True)  204 us
    all_gather x1, waiting for transfers between devices, local(): lax.all_gather(temporal_up, ('clip', 'seq'), axis=0, tiled=True)  202 us
  transfers between devices with their start and end apart: 84, of which 17 were waited for; matrix products, arithmetic and copies ran while one was open for 28% of the time, Pallas kernels for 0%

commit v1 on v0

v1 whole, which is shorter than its diff:
```python
from functools import partial
import math

import jax
import jax.numpy as jnp
from jax import lax
from jax.sharding import Mesh, PartitionSpec as P

HEADS = 16
HEAD_DIM = 72
FREQ = 256
STEPS = 1000
D = 1152
FFN = 4608
EPSILON = 1e-06
MASK_FILL = -1000000000.0

CLIP = ("y", "z", "xl")
SEQ = ("xh", "c")
GROUP = ("xl", "xh", "c")
RING = ("xh", "xl")
ALL = ("y", "z", "xl", "xh", "c")
X_PLACE = (0, 2, 1, 3)

bf16 = jnp.bfloat16
f32 = jnp.float32

SPATIAL_FORMS = ("fphe,fqhe->fhpq", "fhpq,fqhe->fphe", "fhpq,fphe->fqhe")
TEMPORAL_FORMS = ("fphe,gphe->phfg", "phfg,gphe->fphe", "phfg,fphe->gphe")
CROSS_FORMS = ("fphe,lhe->fphl", "fphl,lhe->fphe", "fphl,fphe->lhe")


def fetch(value, axis, step):
    if axis == "x":
        pairs = [(X_PLACE[(i + step) % 4], X_PLACE[i]) for i in range(4)]
        return lax.ppermute(value, ("xl", "xh"), pairs)
    return lax.ppermute(value, axis, [((i + step) % 4, i) for i in range(4)])


def swap(value, axis):
    return lax.ppermute(value, axis, [(0, 1), (1, 0)])


def place_of(axis):
    if axis == "x":
        return lax.axis_index("xh") * 2 + lax.axis_index("xl")
    return lax.axis_index(axis)


def place(blocks, axis, pos):
    shape = blocks[0].shape
    out = jnp.zeros(shape[:pos] + (4,) + shape[pos:], blocks[0].dtype)
    own = place_of(axis)
    for step, block in enumerate(blocks):
        out = lax.dynamic_update_index_in_dim(out, block, lax.rem(own + step, 4), pos)
    return out


def place_down(blocks, axis):
    wide = []
    for block in blocks:
        halves = block.reshape(4, 2, 2, 72, 640)
        wide.append(jnp.concatenate([halves[:, :, 0], halves[:, :, 1, :, :512]], axis=3))
    return place(wide, axis, 1)


def ring_blocks(value, axis):
    return [value] + [fetch(value, axis, step) for step in (1, 3, 2)]


def in_order(blocks):
    return [blocks[0], blocks[1], blocks[3], blocks[2]]


def gather(value, axis, pos):
    return place(in_order(ring_blocks(value, axis)), axis, pos)


def pick(value, axis, step, pos):
    return lax.dynamic_index_in_dim(
        value, lax.rem(place_of(axis) + step, 4), pos, keepdims=False
    )


def scatter_sum(value, axis, pos):
    total = pick(value, axis, 0, pos).astype(f32)
    for step in (1, 3, 2):
        total = total + fetch(pick(value, axis, step, pos), axis, 4 - step).astype(f32)
    return total.astype(bf16)


def by_core(first, second, axis, dim):
    own_first = lax.axis_index(axis) == 0
    return jnp.concatenate(
        [jnp.where(own_first, first, second), jnp.where(own_first, second, first)], axis=dim
    )


def pair_sum(partial_rows):
    mine = partial_rows.astype(bf16)
    return mine.astype(f32) + swap(mine, "c").astype(f32)


def down_pairs(other):
    pairs = []
    for d in range(128):
        y1, y0, z1, z0 = (d >> 6) & 1, (d >> 5) & 1, (d >> 4) & 1, (d >> 3) & 1
        xl, xh, core = (d >> 2) & 1, (d >> 1) & 1, d & 1
        half = 1 - core if other else core
        target = 0
        for bit in (z0, xl, xh, half, z1, y0, y1):
            target = 2 * target + bit
        pairs.append((d, target))
    return pairs


def send_down(shards):
    core = lax.axis_index("c")
    low = shards[:, :, :640]
    high = jnp.pad(shards[:, :, 640:], ((0, 0), (0, 0), (0, 128)))
    first = lax.ppermute(jnp.where(core == 0, low, high), ALL, down_pairs(False))
    second = lax.ppermute(jnp.where(core == 0, high, low), ALL, down_pairs(True))
    half = lax.axis_index("z") % 2
    return jnp.concatenate(
        [jnp.where(half == 0, first, second), jnp.where(half == 0, second, first)], axis=1
    )


def return_down(blocks):
    half = lax.axis_index("z") % 2
    top, bottom = blocks[:, :36], blocks[:, 36:]
    back = [[(b, a) for a, b in down_pairs(other)] for other in (False, True)]
    first = lax.ppermute(jnp.where(half == 0, top, bottom), ALL, back[0])
    second = lax.ppermute(jnp.where(half == 0, bottom, top), ALL, back[1])
    core = lax.axis_index("c")
    low = jnp.where(core == 0, first, second)
    high = jnp.where(core == 0, second, first)
    return jnp.concatenate([low, high[:, :, :512]], axis=2)


def to_pieces(shard, groups):
    rows = shard.shape[0]
    value = shard.reshape(rows, groups, 2, 2, 2, -1)
    value = value.transpose(4, 3, 2, 0, 1, 5)
    return value.reshape(8, rows, -1)


def from_pieces(value, groups):
    rows = value.shape[1]
    value = value.reshape(2, 2, 2, rows, groups, -1)
    value = value.transpose(3, 4, 2, 1, 0, 5)
    return value.reshape(rows, -1)


def swap_group(value, axes):
    return lax.all_to_all(value, axes, split_axis=0, concat_axis=0, tiled=True)


def widen(value, width):
    return jnp.pad(value, [(0, 0)] * (value.ndim - 1) + [(0, width - value.shape[-1])])


def noise_table(count):
    beta_values = jnp.linspace(0.0001, 0.02, count, dtype=f32)
    return jnp.cumprod(1.0 - beta_values)


def time_features(timesteps, feature_count):
    half_count = feature_count // 2
    frequency = jnp.exp(-math.log(10000.0) * jnp.arange(half_count, dtype=f32) / half_count)
    angles = timesteps.astype(f32)[:, None] * frequency
    return jnp.concatenate([jnp.cos(angles), jnp.sin(angles)], axis=1)


def normalize(values):
    average = jnp.mean(values, axis=-1, keepdims=True)
    centred = values - average
    inverse_std = lax.rsqrt(jnp.mean(centred * centred, axis=-1, keepdims=True) + EPSILON)
    return (centred * inverse_std, inverse_std)


def norm_back(normal_rows, inverse_std, normal_grad):
    first_mean = jnp.mean(normal_grad, axis=-1, keepdims=True)
    second_mean = jnp.mean(normal_grad * normal_rows, axis=-1, keepdims=True)
    return inverse_std * (normal_grad - first_mean - normal_rows * second_mean)


def product(operand, weight):
    return jnp.dot(operand, weight, preferred_element_type=f32)


def product_back(operand, weight):
    return lax.dot_general(operand, weight, (((1,), (1,)), ((), ())), preferred_element_type=f32)


def outer_sum(operand, partner):
    return lax.dot_general(operand, partner, (((0,), (0,)), ((), ())), preferred_element_type=f32)


def attend_forward(queries, key_rows, value_rows, einsum_forms, visible):
    factor = HEAD_DIM ** (-0.5)
    scores = jnp.einsum(einsum_forms[0], queries, key_rows, preferred_element_type=f32) * factor
    if visible is not None:
        scores = jnp.where(visible, scores, MASK_FILL)
    row_max = jnp.max(scores, axis=-1, keepdims=True)
    exponent = jnp.exp(scores - row_max)
    denominator = jnp.sum(exponent, axis=-1, keepdims=True)
    probability = (exponent / denominator).astype(bf16)
    mixed_rows = jnp.einsum(einsum_forms[1], probability, value_rows, preferred_element_type=f32)
    return (mixed_rows.astype(bf16), row_max + jnp.log(denominator))


def attend_back(queries, key_rows, value_rows, mixed_grad, logsum, einsum_forms, visible):
    factor = HEAD_DIM ** (-0.5)
    scores = jnp.einsum(einsum_forms[0], queries, key_rows, preferred_element_type=f32) * factor
    if visible is not None:
        scores = jnp.where(visible, scores, MASK_FILL)
    probability = jnp.exp(scores - logsum)
    prob_grad = jnp.einsum(einsum_forms[0], mixed_grad, value_rows, preferred_element_type=f32)
    value_grad = jnp.einsum(
        einsum_forms[2], probability.astype(bf16), mixed_grad, preferred_element_type=f32
    )
    score_grad = probability * (
        prob_grad - jnp.sum(probability * prob_grad, axis=-1, keepdims=True)
    )
    score_grad = score_grad.astype(bf16)
    query_grad = (
        jnp.einsum(einsum_forms[1], score_grad, key_rows, preferred_element_type=f32) * factor
    )
    key_grad = (
        jnp.einsum(einsum_forms[2], score_grad, queries, preferred_element_type=f32) * factor
    )
    return (query_grad, key_grad, value_grad)


def both_columns(own):
    return by_core(own, swap(own, "c"), "c", 1)


def own_columns(value):
    half = value.shape[1] // 2
    return jnp.where(lax.axis_index("c") == 0, value[:, :half], value[:, half:])


def own_rows(value):
    half = value.shape[0] // 2
    return lax.dynamic_slice_in_dim(value, lax.axis_index("c") * half, half, 0)


def side_by_side(pieces, start, stop):
    return jnp.concatenate([pieces[j][:, start:stop] for j in range(4)], axis=1)


def heads_of(rows, lead):
    return rows.reshape(lead + (HEADS // 2, HEAD_DIM))


def attention_forward(hidden_state, modulation, weights, out_full, forms, lead):
    normal_rows, inverse_std = normalize(hidden_state)
    normed = (normal_rows * (1.0 + modulation[1]) + modulation[0]).astype(bf16)
    packed = [product(normed, weights[j]).astype(bf16) for j in range(4)]
    queries = heads_of(side_by_side(packed, 0, 144), lead)
    key_rows = heads_of(side_by_side(packed, 144, 288), lead)
    value_rows = heads_of(side_by_side(packed, 288, 432), lead)
    mixed_own, logsum = attend_forward(queries, key_rows, value_rows, forms, None)
    mixed_rows = both_columns(mixed_own.reshape(-1, D // 2))
    branch = product(mixed_rows, out_full)
    stored = (
        normal_rows,
        inverse_std,
        normed,
        queries,
        key_rows,
        value_rows,
        logsum,
        mixed_rows,
        branch,
    )
    return (hidden_state + modulation[2] * branch, stored)


def attention_back(incoming, stored, modulation, weights, out_full, forms):
    normal_rows, inverse_std, normed, queries, key_rows, value_rows, logsum, mixed_rows, branch = (
        stored
    )
    gate_grad = jnp.sum(incoming * branch, axis=0)
    branch_grad = (modulation[2] * incoming).astype(bf16)
    out_grad = outer_sum(mixed_rows, own_columns(branch_grad)).astype(bf16)
    mixed_grad = product_back(branch_grad, own_rows(out_full)).astype(bf16).reshape(queries.shape)
    parts = attend_back(queries, key_rows, value_rows, mixed_grad, logsum, forms, None)
    parts = [part.astype(bf16).reshape(-1, D // 2) for part in parts]
    packed_grad = [
        jnp.concatenate([part[:, 144 * j : 144 * j + 144] for part in parts], axis=1)
        for j in range(4)
    ]
    projection_grad = [outer_sum(normed, packed_grad[j]).astype(bf16) for j in range(4)]
    normed_grad = sum(product_back(packed_grad[j], weights[j][:, :432]) for j in range(4))
    normed_grad = pair_sum(normed_grad)
    scale_grad = jnp.sum(normed_grad * normal_rows, axis=0)
    shift_grad = jnp.sum(normed_grad, axis=0)
    upstream = incoming + norm_back(normal_rows, inverse_std, normed_grad * (1.0 + modulation[1]))
    return (upstream, projection_grad, out_grad, (shift_grad, scale_grad, gate_grad))


def cross_forward(hidden_state, gain_vector, query_weight, text_keys, text_values, out_full, visible, lead):
    normal_rows, inverse_std = normalize(hidden_state)
    normed = (normal_rows * gain_vector).astype(bf16)
    queries = heads_of(product(normed, query_weight).astype(bf16), lead)
    mixed_own, logsum = attend_forward(queries, text_keys, text_values, CROSS_FORMS, visible)
    mixed_rows = both_columns(mixed_own.reshape(-1, D // 2))
    branch = product(mixed_rows, out_full)
    return (hidden_state + branch, (normal_rows, inverse_std, normed, queries, logsum, mixed_rows))


def cross_back(incoming, stored, gain_vector, query_weight, text_keys, text_values, out_full, visible):
    normal_rows, inverse_std, normed, queries, logsum, mixed_rows = stored
    branch_grad = incoming.astype(bf16)
    out_grad = outer_sum(mixed_rows, own_columns(branch_grad)).astype(bf16)
    mixed_grad = product_back(branch_grad, own_rows(out_full)).astype(bf16).reshape(queries.shape)
    query_grad, key_grad, value_grad = attend_back(
        queries, text_keys, text_values, mixed_grad, logsum, CROSS_FORMS, visible
    )
    query_grad = query_grad.astype(bf16).reshape(-1, D // 2)
    query_weight_grad = outer_sum(normed, query_grad).astype(bf16)
    normed_grad = pair_sum(product_back(query_grad, query_weight))
    gain_grad = jnp.sum(normed_grad * normal_rows, axis=0)
    upstream = incoming + norm_back(normal_rows, inverse_std, normed_grad * gain_vector)
    key_grad = key_grad.reshape(key_grad.shape[0], -1)
    value_grad = value_grad.reshape(value_grad.shape[0], -1)
    return (upstream, gain_grad, query_weight_grad, out_grad, key_grad, value_grad)


def feed_forward(hidden_state, modulation, up_pieces, down):
    normal_rows, inverse_std = normalize(hidden_state)
    normed = (normal_rows * (1.0 + modulation[4]) + modulation[3]).astype(bf16)
    inner = [product(normed, up_pieces[j]) for j in range(4)]
    activated = [jax.nn.gelu(rows, approximate=True).astype(bf16)[:, :576] for rows in inner]
    activated = jnp.concatenate(activated, axis=1)
    output = pair_sum(product(activated, down))
    return (
        hidden_state + modulation[5] * output,
        (normal_rows, inverse_std, normed, inner, activated, output),
    )


def feed_forward_back(incoming, stored, modulation, up_pieces, down):
    normal_rows, inverse_std, normed, inner, activated, output = stored
    gate_grad = jnp.sum(incoming * output, axis=0)
    output_grad = (modulation[5] * incoming).astype(bf16)
    down_grad = outer_sum(activated, output_grad).astype(bf16)
    active_grad = product_back(output_grad, down)
    inner_grad = []
    for j in range(4):
        smooth_back = jax.vjp(partial(jax.nn.gelu, approximate=True), inner[j])[1]
        piece = widen(active_grad[:, 576 * j : 576 * j + 576], 640)
        inner_grad.append(smooth_back(piece)[0].astype(bf16))
    up_grad = jnp.stack([outer_sum(normed, inner_grad[j]).astype(bf16) for j in range(4)])
    normed_grad = pair_sum(sum(product_back(inner_grad[j], up_pieces[j]) for j in range(4)))
    scale_grad = jnp.sum(normed_grad * normal_rows, axis=0)
    shift_grad = jnp.sum(normed_grad, axis=0)
    upstream = incoming + norm_back(normal_rows, inverse_std, normed_grad * (1.0 + modulation[4]))
    return (upstream, up_grad, down_grad, (shift_grad, scale_grad, gate_grad))


def scatter_down(grad):
    grad = grad.reshape(4, 4, 2, 72, D)
    low, high = grad[..., :640], widen(grad[..., 640:], 640)
    grad = jnp.stack([low, high], axis=3)

    def part(step):
        return pick(grad, "y", step, 1).reshape(4, 4, 72, 640)

    total = part(0).astype(f32)
    for step in (1, 3, 2):
        total = total + fetch(part(step), "y", 4 - step).astype(f32)
    return scatter_sum(total.astype(bf16), "z", 1)


def local(
    latents,
    noise_sample,
    timesteps,
    text_states,
    text_lengths,
    cotangent,
    time_input,
    time_output,
    spatial_table,
    spatial_projection,
    spatial_output,
    spatial_up,
    spatial_down,
    temporal_table,
    temporal_projection,
    temporal_output,
    cross_query,
    cross_text,
    cross_output,
    cross_gain,
    temporal_up,
    temporal_down,
):
    core, far = lax.axis_index("c"), lax.axis_index("xh")
    clip = (lax.axis_index("y") * 4 + lax.axis_index("z")) * 2 + lax.axis_index("xl")
    me = clip * 4 + far * 2 + core

    sent = jnp.concatenate(
        [
            to_pieces(spatial_up, 1),
            to_pieces(spatial_projection, 3),
            to_pieces(spatial_output, 1),
            to_pieces(temporal_up, 1),
            to_pieces(temporal_projection, 3),
            to_pieces(temporal_output, 1),
            to_pieces(cross_query, 1),
            to_pieces(cross_output, 1),
        ],
        axis=2,
    )
    mine = swap_group(sent, GROUP).reshape(72, 2592)
    s_up = widen(mine[:, :576], 640)
    s_att = widen(mine[:, 576:1152], 640)
    t_up = widen(mine[:, 1152:1728], 640)
    t_att = widen(mine[:, 1728:2592], 896)
    downs = send_down(jnp.stack([spatial_down, temporal_down]))

    first_y = gather(jnp.concatenate([s_up, t_att], axis=1), "y", 0)
    first_x = gather(jnp.concatenate([s_att, downs[0], t_up, downs[1]], axis=1), "x", 0)

    s_up = gather(first_y[..., :640], "z", 1)
    s_up = lax.all_gather(s_up.reshape(D, 640), RING, axis=0, tiled=False)
    s_att = gather(gather(first_x[..., :640], "y", 1), "z", 2).reshape(4, D, 640)
    s_down = ring_blocks(gather(first_x[..., 640:1280], "z", 1), "y")
    s_down = place_down(in_order(s_down), "y").reshape(FFN // 2, D)

    t_att = gather(first_y[..., 640:], "z", 1)
    t_att = lax.all_gather(t_att.reshape(D, 896), RING, axis=0, tiled=False)
    t_up = gather(gather(first_x[..., 1280:1920], "y", 1), "z", 2).reshape(4, D, 640)
    t_down = ring_blocks(gather(first_x[..., 1920:], "z", 1), "y")
    t_down = place_down(in_order(t_down), "y").reshape(FFN // 2, D)

    words = cross_text.reshape(32, 2, 2, 2, 288).transpose(3, 2, 0, 1, 4).reshape(4, 32, 576)
    words = widen(swap_group(words, SEQ).reshape(128, 576), 640)
    words = by_core(words, swap(words, "xl"), "xl", 0)
    words = gather(words, "y", 0)
    words = lax.all_gather(words, "z", axis=0, tiled=False).reshape(4096, 640)

    split_steps = jnp.stack([timesteps // 32, timesteps % 32], axis=1).reshape(-1).astype(bf16)
    note = jnp.concatenate(
        [
            time_input.reshape(-1),
            spatial_table.reshape(-1),
            temporal_table.reshape(-1),
            cross_gain,
            split_steps,
            jnp.zeros((9,), bf16),
        ]
    )
    notes = swap_group(jnp.broadcast_to(note, (128, 2432)), ALL)
    full_time_input = notes[:, :2304].reshape(FREQ, D)
    tables = notes[:, 2304:2412].reshape(128, 12, 9).transpose(1, 0, 2).reshape(2, 6, D)
    full_gain = notes[:, 2412:2421].reshape(D).astype(f32)
    steps = notes[::4, 2421:2423].astype(f32)
    steps = (steps[:, 0] * 32.0 + steps[:, 1]).astype(jnp.int32)

    embedded = time_features(steps, FREQ).astype(bf16)
    pre_time = product(embedded, full_time_input)
    lifted = jax.nn.silu(pre_time).astype(bf16)
    own_lifted = lax.dynamic_slice_in_dim(lifted, me * 9, 9, 1)
    shares = swap_group(product(own_lifted, time_output).reshape(128, 1728), ALL)
    shared = jnp.sum(shares, axis=0)
    shared = by_core(shared, swap(shared, "c"), "c", 0)
    shared = by_core(shared, swap(shared, "xh"), "xh", 0).reshape(6, D)
    spatial_mod = tables[0].astype(f32) + shared
    temporal_mod = tables[1].astype(f32) + shared

    alpha_bars = noise_table(STEPS)
    picked = jnp.sum(jnp.where(jnp.arange(STEPS) == timesteps[0], alpha_bars, 0.0))
    signal_scale = jnp.sqrt(picked)

    frames = jnp.stack([latents[0, 0], noise_sample[0, 0]])
    other = swap(frames, "c")

    def noised(pair):
        return signal_scale * pair[0].astype(f32) + jnp.sqrt(1.0 - picked) * pair[1].astype(f32)

    hidden_state = by_core(noised(frames), noised(other), "c", 0)

    s_out = both_columns(side_by_side(s_att, 432, 576))
    hidden_state, spatial_attention = attention_forward(
        hidden_state, spatial_mod, s_att, s_out, SPATIAL_FORMS, (2, 160)
    )
    hidden_state, spatial_mlp = feed_forward(hidden_state, spatial_mod, s_up, s_down)

    def to_patches(rows):
        halves = rows.reshape(2, 2, 80, D)
        keep = lax.dynamic_index_in_dim(halves, far, 1, keepdims=False)
        give = lax.dynamic_index_in_dim(halves, 1 - far, 1, keepdims=False)
        return jnp.concatenate([keep, swap(give, "xh")], axis=0).reshape(320, D)

    patch_rows = to_patches(hidden_state.astype(bf16))
    own_cotangent = cotangent[0, 0]
    incoming = to_patches(by_core(own_cotangent, swap(own_cotangent, "c"), "c", 0)).astype(f32)

    text_order = text_states[0].reshape(120, 4, 4, 2, 128).transpose(0, 2, 1, 3, 4)
    text_order = text_order.reshape(120, 4096)
    text_rows = product(text_order, words)[:, :576].astype(bf16)
    other_text = swap(text_rows, "xh")
    text_keys = by_core(text_rows[:, :288], other_text[:, :288], "xh", 1).reshape(120, 8, 72)
    text_values = by_core(text_rows[:, 288:], other_text[:, 288:], "xh", 1).reshape(120, 8, 72)
    visible = jnp.arange(120) < text_lengths[0]

    t_out = both_columns(side_by_side(t_att, 432, 576))
    x_query = side_by_side(t_att, 576, 720)
    x_out = both_columns(side_by_side(t_att, 720, 864))
    hidden_state = patch_rows.astype(f32)
    hidden_state, temporal_attention = attention_forward(
        hidden_state, temporal_mod, t_att, t_out, TEMPORAL_FORMS, (4, 80)
    )
    hidden_state, cross_stored = cross_forward(
        hidden_state, full_gain, x_query, text_keys, text_values, x_out, visible, (4, 80)
    )
    hidden_state, temporal_mlp = feed_forward(hidden_state, temporal_mod, t_up, t_down)

    finished = hidden_state.astype(bf16).reshape(4, 80, D)
    keep = lax.dynamic_index_in_dim(finished, core, 0, keepdims=False)
    give = lax.dynamic_index_in_dim(finished, 2 + core, 0, keepdims=False)
    activations = by_core(keep, swap(give, "xh"), "xh", 0)[None, None]

    incoming, t_up_grad, t_down_grad, t_mlp_mod = feed_forward_back(
        incoming, temporal_mlp, temporal_mod, t_up, t_down
    )
    incoming, gain_grad, x_query_grad, x_out_grad, key_grad, value_grad = cross_back(
        incoming, cross_stored, full_gain, x_query, text_keys, text_values, x_out, visible
    )
    key_grad, value_grad = key_grad.astype(bf16), value_grad.astype(bf16)

    def text_half(which):
        def half(value):
            return lax.dynamic_slice_in_dim(value, which * 288, 288, 1)

        return jnp.concatenate([half(key_grad), half(value_grad)], axis=1)

    text_grad = text_half(far).astype(f32) + swap(text_half(1 - far), "xh").astype(f32)
    words_grad = outer_sum(text_order, widen(text_grad.astype(bf16), 640)).astype(bf16)
    words_grad = lax.psum_scatter(
        words_grad.reshape(4, 4 * 2 * 128, 640), "z", scatter_dimension=0, tiled=False
    )
    words_grad = scatter_sum(words_grad.reshape(4, 2, 128, 640), "y", 0)
    near = lax.axis_index("xl")
    words_grad = lax.dynamic_index_in_dim(words_grad, near, 0, keepdims=False).astype(f32) + swap(
        lax.dynamic_index_in_dim(words_grad, 1 - near, 0, keepdims=False), "xl"
    ).astype(f32)
    words_grad = swap_group(words_grad.astype(bf16)[:, :576].reshape(4, 32, 576), SEQ)
    words_grad = words_grad.reshape(2, 2, 32, 2, 288).transpose(2, 3, 1, 0, 4).reshape(32, 2304)

    incoming, t_proj_grad, t_out_grad, t_att_mod = attention_back(
        incoming, temporal_attention, temporal_mod, t_att, t_out, TEMPORAL_FORMS
    )
    t_mod_grad = jnp.stack(t_att_mod + t_mlp_mod)

    def piece(value, j):
        return value[:, 144 * j : 144 * j + 144]

    t_att_grad = jnp.stack(
        [
            widen(
                jnp.concatenate(
                    [t_proj_grad[j], piece(t_out_grad, j), piece(x_query_grad, j), piece(x_out_grad, j)],
                    axis=1,
                ),
                896,
            )
            for j in range(4)
        ]
    )

    def scatter_ring(grad):
        return lax.psum_scatter(grad, RING, scatter_dimension=0, tiled=False)

    def finish(up_grad, att_grad, down_grad):
        width = att_grad.shape[-1]
        if width == 640:
            ring, rest = up_grad, att_grad
        else:
            ring, rest = att_grad, up_grad
        down = scatter_down(down_grad)
        rest = scatter_sum(rest.reshape(4, 4, 4, 72, 640), "z", 2)
        rest = scatter_sum(rest, "y", 1)
        both = scatter_sum(jnp.concatenate([rest, down], axis=2), "x", 0)
        ring = scatter_ring(ring).reshape(4, 4, 72, -1)
        ring = scatter_sum(scatter_sum(ring, "z", 1), "y", 0)
        rest, down = both[:, :640], both[:, 640:]
        down = return_down(down[None])[0].astype(f32)
        up, att = (ring, rest) if width == 640 else (rest, ring)
        return up, att, down

    t_up_done, t_att_done, t_down_done = finish(t_up_grad, t_att_grad, t_down_grad)

    back = incoming.astype(bf16).reshape(4, 80, D)
    theirs = swap(back[2:], "xh")
    frame_grad = by_core(back[:2], theirs, "xh", 1).reshape(320, D).astype(f32)
    frame_grad, s_up_grad, s_down_grad, s_mlp_mod = feed_forward_back(
        frame_grad, spatial_mlp, spatial_mod, s_up, s_down
    )
    frame_grad, s_proj_grad, s_out_grad, s_att_mod = attention_back(
        frame_grad, spatial_attention, spatial_mod, s_att, s_out, SPATIAL_FORMS
    )
    latent_grad = signal_scale * lax.dynamic_index_in_dim(frame_grad.reshape(2, 160, D), core, 0)
    s_mod_grad = jnp.stack(s_att_mod + s_mlp_mod)
    s_att_grad = jnp.stack(
        [
            widen(jnp.concatenate([s_proj_grad[j], piece(s_out_grad, j)], axis=1), 640)
            for j in range(4)
        ]
    )
    s_up_done, s_att_done, s_down_done = finish(s_up_grad, s_att_grad, s_down_grad)

    returned = jnp.concatenate(
        [s_up_done[:, :576], s_att_done[:, :576], t_up_done[:, :576], t_att_done[:, :864]], axis=1
    )
    returned = swap_group(returned.reshape(8, 9, 2592), GROUP).astype(f32)
    s_up_grad = from_pieces(returned[..., :576], 1)
    s_proj_grad = from_pieces(returned[..., 576:1008], 3)
    s_out_grad = from_pieces(returned[..., 1008:1152], 1)
    t_up_grad = from_pieces(returned[..., 1152:1728], 1)
    t_proj_grad = from_pieces(returned[..., 1728:2160], 3)
    t_out_grad = from_pieces(returned[..., 2160:2304], 1)
    x_query_grad = from_pieces(returned[..., 2304:2448], 1)
    x_out_grad = from_pieces(returned[..., 2448:], 1)

    shared_grad = (s_mod_grad + t_mod_grad).reshape(4, 1728)
    shared_grad = shared_grad + swap(shared_grad, "xh")
    quarter = lax.dynamic_index_in_dim(shared_grad, far * 2 + core, 0, keepdims=False)
    table_part = jnp.stack([s_mod_grad, t_mod_grad]).reshape(12, 128, 9).transpose(1, 0, 2)
    table_part = jnp.concatenate([table_part.reshape(128, 108), gain_grad.reshape(128, 9)], axis=1)
    table_part = jnp.where(core == 0, table_part, 0.0)
    letter = jnp.concatenate(
        [jnp.broadcast_to(quarter, (128, 1728)), table_part, jnp.zeros((128, 75), f32)], axis=1
    )
    letters = swap_group(letter, ALL)
    all_shared = letters[:, :1728].reshape(32, 6 * D)
    table_sum = jnp.sum(letters[:, 1728:1845], axis=0)
    s_table_grad = table_sum[:54].reshape(6, 9)
    t_table_grad = table_sum[54:108].reshape(6, 9)
    cross_gain_grad = table_sum[108:]

    def exact(a, b, dims):
        return lax.dot_general(
            a, b, (dims, ((), ())), precision=lax.Precision.HIGHEST, preferred_element_type=f32
        )

    time_output_grad = exact(own_lifted.astype(f32), all_shared, ((0,), (0,)))
    lifted_grad = exact(all_shared, time_output.astype(f32), ((1,), (1,)))
    own_pre = lax.dynamic_slice_in_dim(pre_time, me * 9, 9, 1)
    own_pre_grad = jax.vjp(jax.nn.silu, own_pre)[1](lifted_grad)[0]
    card = jnp.broadcast_to(widen(own_pre_grad.reshape(288), 384), (128, 384))
    cards = swap_group(card, ALL)[:, :288].reshape(128, 32, 9)
    pre_grad = cards.transpose(1, 0, 2).reshape(32, D)
    own_embedded = lax.dynamic_slice_in_dim(embedded, me * 2, 2, 1).astype(f32)
    time_input_grad = exact(own_embedded, pre_grad, ((0,), (0,)))

    return (
        activations,
        latent_grad[None],
        time_input_grad,
        time_output_grad,
        s_table_grad,
        s_proj_grad,
        s_out_grad,
        s_up_grad,
        s_down_done,
        t_table_grad,
        t_proj_grad,
        t_out_grad,
        x_query_grad,
        words_grad.astype(f32),
        x_out_grad,
        cross_gain_grad,
        t_up_grad,
        t_down_done,
    )


def solution(mesh):
    fine = Mesh(mesh.devices.reshape(4, 4, 2, 2, 2), ALL)
    frames = P(CLIP, SEQ, None, None)
    rows = P(ALL, None)
    columns = P(None, ALL)
    in_specs = (
        frames,
        frames,
        P(CLIP),
        P(CLIP, None, None),
        P(CLIP),
        frames,
        rows,
        rows,
        columns,
        rows,
        rows,
        rows,
        rows,
        columns,
        rows,
        rows,
        rows,
        rows,
        rows,
        P(ALL),
        rows,
        rows,
    )
    out_specs = (
        frames,
        frames,
        rows,
        rows,
        columns,
        rows,
        rows,
        rows,
        rows,
        columns,
        rows,
        rows,
        rows,
        rows,
        rows,
        P(ALL),
        rows,
        rows,
    )
    return jax.shard_map(local, mesh=fine, in_specs=in_specs, out_specs=out_specs, check_vma=False)
```

time: 5080 us -> 1310 us (0.26)
  waiting for transfers between devices: 2510 us -> 379 us
  blocking collectives: 1580 us -> 0 us
  other arithmetic: 43.9 us -> 164 us
  starting transfers between devices: 331 us -> 246 us
  matrix products: 237 us -> 159 us
    all_gather x12 -> x3, waiting for transfers between devices: 1700 us -> 0.01 us  [the longest x1 0.01 us: local(): words = lax.all_gather(words, 'z', axis=0, tiled=False).reshape(4096, 640)]
    unnamed x3 -> x0, blocking collectives: 1050 us -> none
    reduce_scatter x1 -> x3, waiting for transfers between devices: 746 us -> 0.02 us  [the longest x1 0.02 us: local(): lax.psum_scatter(words_grad.reshape(4, 4 * 2 * 128, 640), 'z', scatter_di...]
    all_gather x3 -> x0, blocking collectives: 526 us -> none  [the longest x1 181 us: local(): lax.all_gather(time_input, ('clip', 'seq'), axis=0, tiled=True)]
    ppermute x0 -> x116, waiting for transfers between devices: none -> 357 us  [the longest x75 308 us: fetch(): return lax.ppermute(value, axis, [((i + step) % 4, i) for i in range(4)])]
    unnamed x67 -> x0, starting transfers between devices: 314 us -> none
    unnamed x444 -> x657, local copies, waits for them, and re-layouts: 293 us -> 63.9 us
    ppermute x0 -> x116, starting transfers between devices: none -> 188 us  [the longest x75 143 us: fetch(): return lax.ppermute(value, axis, [((i + step) % 4, i) for i in range(4)])]
  transfers between devices with their start and end apart: 84 -> 130, of which waited for: 17 -> 49; matrix products, arithmetic and copies ran while one was open for 28% -> 42% of each run, Pallas kernels for 0% -> 0%
where the time goes in v1:
time: 1310 us; the launch traced here: 1300 us
  waiting for transfers between devices  379 us (29%)
  local copies, waits for them, and re-layouts  331 us (25%)
  starting transfers between devices  246 us (19%)
  other arithmetic  164 us (13%)
  matrix products  159 us (12%)
  between operations  22.5 us (2%)
    ppermute x75, waiting for transfers between devices, fetch(): return lax.ppermute(value, axis, [((i + step) % 4, i) for i in range(4)])  308 us
    ppermute x75, starting transfers between devices, fetch(): return lax.ppermute(value, axis, [((i + step) % 4, i) for i in range(4)])  143 us
    unnamed x657, local copies, waits for them, and re-layouts  63.9 us
    all_to_all x8, starting transfers between devices, swap_group(): return lax.all_to_all(value, axes, split_axis=0, concat_axis=0, tiled=True)  57.1 us
    dot_general x25, matrix products, product(): return jnp.dot(operand, weight, preferred_element_type=f32)  44.2 us
    dot_general x23, matrix products, outer_sum(): lax.dot_general(operand, partner, (((0,), (0,)), ((), ())), preferred_ele...  43.8 us
    ppermute x26, waiting for transfers between devices, swap(): return lax.ppermute(value, axis, [(0, 1), (1, 0)])  43.7 us
    dot_general x22, matrix products, product_back(): lax.dot_general(operand, weight, (((1,), (1,)), ((), ())), preferred_elem...  39.6 us
  transfers between devices with their start and end apart: 130, of which 49 were waited for; matrix products, arithmetic and copies ran while one was open for 42% of the time, Pallas kernels for 0%

profile of v1, /device:TPU:0, one launch (start us, length us, event | category | flops | bytes accessed | tf_op | source)
XLA Modules:
  0.0 1300.9 jit_solution(652592265373501179)
XLA Ops:
  17.5 11.7 all-to-all-done.2
  51.0 14.6 %collective-permute-done.19 = bf16[4,72,640]{2,1,0:T(8,128)(2,1)S(1)} collective-permute-done((bf16[4,72,640]{2,1,0:T(8,128)(2,1)}, bf16[4,72,640]{2,1,0:T(8,128)(2,1)S(1)}, u32[]{:S(2)}, u32[]{:S(2)}) %collective-permute-start.19) | collective-permute-done | bytes 368672 | tf_op jit(solution)/shard_map/ppermute | solution.py:37
  99.0 7.9 all-to-all-start
  109.1 20.5 %collective-permute-done.35 = bf16[128,640]{1,0:T(8,128)(2,1)S(1)} collective-permute-done((bf16[128,640]{1,0:T(8,128)(2,1)S(1)}, bf16[128,640]{1,0:T(8,128)(2,1)S(1)}, u32[]{:S(2)}, u32[]{:S(2)}) %collective-permute-start.35) | collective-permute-done | bytes 163872 | tf_op jit(solution)/shard_map/ppermute | solution.py:41
  166.9 10.1 all-to-all-start.1
  220.8 8.6 collective-permute-done.9
  237.9 12.0 collective-permute-done.22
  251.1 10.7 collective-permute-start.48
  265.0 12.8 collective-permute-done.48
  281.4 9.3 collective-permute-done.50
  341.8 16.0 %collective-permute-done.45 = bf16[4,4,72,640]{3,2,1,0:T(8,128)(2,1)} collective-permute-done((bf16[4,4,72,640]{3,2,1,0:T(8,128)(2,1)}, bf16[4,4,72,640]{3,2,1,0:T(8,128)(2,1)}, u32[]{:S(2)}, u32[]{:S(2)}) %collective-permute-start.45) | collective-permute-done | bytes 1474592 | tf_op jit(solution)/shard_map/ppermute | solution.py:37
  368.2 21.6 %collective-permute-done.11 = bf16[4,4,72,640]{3,2,1,0:T(8,128)(2,1)} collective-permute-done((bf16[4,4,72,640]{3,2,1,0:T(8,128)(2,1)}, bf16[4,4,72,640]{3,2,1,0:T(8,128)(2,1)}, u32[]{:S(2)}, u32[]{:S(2)}) %collective-permute-start.11) | collective-permute-done | bytes 1474592 | tf_op jit(solution)/shard_map/ppermute | solution.py:37
  402.4 28.8 %collective-permute-done.13 = bf16[4,4,72,640]{3,2,1,0:T(8,128)(2,1)S(1)} collective-permute-done((bf16[4,4,72,640]{3,2,1,0:T(8,128)(2,1)}, bf16[4,4,72,640]{3,2,1,0:T(8,128)(2,1)S(1)}, u32[]{:S(2)}, u32[]{:S(2)}) %collective-permute-start.13) | collective-permute-done | bytes 1474592 | tf_op jit(solution)/shard_map/ppermute | solution.py:37
  467.5 10.1 collective-permute-done.51
  484.6 14.7 %collective-permute-done.53 = bf16[4,4,72,640]{3,2,1,0:T(8,128)(2,1)S(1)} collective-permute-done((bf16[4,4,72,640]{3,2,1,0:T(8,128)(2,1)}, bf16[4,4,72,640]{3,2,1,0:T(8,128)(2,1)S(1)}, u32[]{:S(2)}, u32[]{:S(2)}) %collective-permute-start.53) | collective-permute-done | bytes 1474592 | tf_op jit(solution)/shard_map/ppermute | solution.py:37
  700.5 14.5 %collective-permute-start.87 = (bf16[4,4,72,640]{3,2,0,1:T(8,128)(2,1)}, bf16[4,4,72,640]{3,2,0,1:T(8,128)(2,1)}, u32[]{:S(2)}, u32[]{:S(2)}) collective-permute-start(bf16[4,4,72,640]{3,2,0,1:T(8,128)(2,1)} %bitcast.841), channel_id=1, source_target_pairs={{8,0},{16,8},{24,16},{0,24},{9,1},{17,9},{25,17},{1,25},{10,2},{18... | collective-permute-start | bytes 4423688 | tf_op jit(solution)/shard_map/ppermute | solution.py:37
  827.7 8.8 collective-permute-done.61
  869.5 41.6 %collective-permute-done.91 = bf16[4,72,640]{2,1,0:T(8,128)(2,1)} collective-permute-done((bf16[4,72,640]{2,1,0:T(8,128)(2,1)}, bf16[4,72,640]{2,1,0:T(8,128)(2,1)}, u32[]{:S(2)}, u32[]{:S(2)}) %collective-permute-start.91) | collective-permute-done | bytes 368672 | tf_op jit(solution)/shard_map/ppermute | solution.py:37
  1079.3 12.0 collective-permute-done.73
  1098.4 9.8 all-to-all-start.4
  1108.2 24.5 %collective-permute-done.72 = bf16[4,4,72,640]{3,2,1,0:T(8,128)(2,1)} collective-permute-done((bf16[4,4,72,640]{3,2,1,0:T(8,128)(2,1)}, bf16[4,4,72,640]{3,2,1,0:T(8,128)(2,1)}, u32[]{:S(2)}, u32[]{:S(2)}) %collective-permute-start.72) | collective-permute-done | bytes 1474592 | tf_op jit(solution)/shard_map/ppermute | solution.py:37
  1157.4 10.1 all-to-all-start.5
  1233.7 9.3 collective-permute-done.65
  1275.6 9.3 all-to-all-done.6
  (1487 shorter events, 929.1 us)
Async XLA Ops:
  17.4 513.2 %all-gather.4.cloned.1.call-start = ((), (), s32[]{:S(2)}) async-start(), calls=%async_computation.11 | async-start | bytes 7372800 | tf_op jit(solution)/shard_map/all_gather | solution.py:431
  71.2 126.1 %collective-permute-start = (bf16[2,160,1152]{2,1,0:T(8,128)(2,1)}, bf16[2,160,1152]{2,1,0:T(8,128)(2,1)}, u32[]{:S(2)}, u32[]{:S(2)}) collective-permute-start(bf16[2,160,1152]{2,1,0:T(8,128)(2,1)} %pad_maximum_fusion.19), channel_id=1, source_target_pairs={{0,1},{1,0},{2,3},{3,2},{4,5},{5,4},{6,7},{7,6},{8,9},{9,8},{10,11... | collective-permute-start | bytes 2211848 | tf_op jit(solution)/shard_map/ppermute | solution.py:41
  107.0 444.0 %all-gather.8.cloned.1.call-start = ((), (), s32[]{:S(2)}) async-start(), calls=%async_computation.13 | async-start | bytes 6553600 | tf_op jit(solution)/shard_map/all_gather | solution.py:446
  151.1 188.9 %collective-permute-start.57 = (bf16[2,80,1152]{2,1,0:T(8,128)(2,1)}, bf16[2,80,1152]{2,1,0:T(8,128)(2,1)}, u32[]{:S(2)}, u32[]{:S(2)}) collective-permute-start(bf16[2,80,1152]{2,1,0:T(8,128)(2,1)} %get-tuple-element.183), channel_id=1, source_target_pairs={{0,2},{2,0},{1,3},{3,1},{4,6},{6,4},{5,7},{7,5},{8,10},{10,8},{9,1... | collective-permute-start | bytes 1105928 | tf_op jit(solution)/shard_map/ppermute | solution.py:41
  166.9 156.2 %all-to-all-start.1 = ((f32[128,1,1728]{2,1,0:T(1,128)}), f32[128,1,1728]{2,1,0:T(1,128)S(1)}, u32[]{:S(2)}, u32[]{:S(2)}) async-start(f32[128,1,1728]{2,1,0:T(1,128)} %all_to_all.51), calls=%async_computation.1 | async-start | bytes 1835008 | tf_op jit(solution)/shard_map/all_to_all | solution.py:156
  177.0 397.6 %all-gather.6.cloned.1.call-start = ((), (), s32[]{:S(2)}) async-start(), calls=%async_computation.12 | async-start | bytes 10321920 | tf_op jit(solution)/shard_map/all_gather | solution.py:437
  179.8 114.2 %collective-permute-start.30 = (bf16[4,72,896]{2,1,0:T(8,128)(2,1)}, bf16[4,72,896]{2,1,0:T(8,128)(2,1)S(1)}, u32[]{:S(2)}, u32[]{:S(2)}) collective-permute-start(bf16[4,72,896]{2,1,0:T(8,128)(2,1)} %slice.1030), channel_id=1, source_target_pairs={{8,0},{16,8},{24,16},{0,24},{9,1},{17,9},{25,17},{1,25},{10,2},{18... | collective-permute-start | bytes 1548296 | tf_op jit(solution)/shard_map/ppermute | solution.py:37
  183.6 111.6 %collective-permute-start.31 = (bf16[4,72,896]{2,1,0:T(8,128)(2,1)}, bf16[4,72,896]{2,1,0:T(8,128)(2,1)S(1)}, u32[]{:S(2)}, u32[]{:S(2)}) collective-permute-start(bf16[4,72,896]{2,1,0:T(8,128)(2,1)} %slice.1030), channel_id=1, source_target_pairs={{16,0},{24,8},{0,16},{8,24},{17,1},{25,9},{1,17},{9,25},{18,2},{26... | collective-permute-start | bytes 1548296 | tf_op jit(solution)/shard_map/ppermute | solution.py:37
  295.3 94.4 %collective-permute-start.11 = (bf16[4,4,72,640]{3,2,1,0:T(8,128)(2,1)}, bf16[4,4,72,640]{3,2,1,0:T(8,128)(2,1)}, u32[]{:S(2)}, u32[]{:S(2)}) collective-permute-start(bf16[4,4,72,640]{3,2,1,0:T(8,128)(2,1)} %bitcast_dynamic-update-slice_fusion.31), channel_id=1, source_target_pairs={{8,0},{16,8},{24,16},{0,24},{9,1},{17,9},{25,17},{1,25},{10,2},{18... | collective-permute-start | bytes 4423688 | tf_op jit(solution)/shard_map/ppermute | solution.py:37
  307.2 878.6 %reduce-scatter.8.cloned.1.call-start = ((), (), s32[]{:S(2)}) async-start(), calls=%async_computation.16 | async-start | bytes 6553600 | tf_op jit(solution)/shard_map/reduce_scatter | solution.py:546
  357.7 73.5 %collective-permute-start.13 = (bf16[4,4,72,640]{3,2,1,0:T(8,128)(2,1)}, bf16[4,4,72,640]{3,2,1,0:T(8,128)(2,1)S(1)}, u32[]{:S(2)}, u32[]{:S(2)}) collective-permute-start(bf16[4,4,72,640]{3,2,1,0:T(8,128)(2,1)} %bitcast_dynamic-update-slice_fusion.31), channel_id=1, source_target_pairs={{24,0},{0,8},{8,16},{16,24},{25,1},{1,9},{9,17},{17,25},{26,2},{2,... | collective-permute-start | bytes 4423688 | tf_op jit(solution)/shard_map/ppermute | solution.py:37
  362.9 99.9 %collective-permute-start.25 = (bf16[4,4,72,640]{3,2,1,0:T(8,128)(2,1)}, bf16[4,4,72,640]{3,2,1,0:T(8,128)(2,1)}, u32[]{:S(2)}, u32[]{:S(2)}) collective-permute-start(bf16[4,4,72,640]{3,2,1,0:T(8,128)(2,1)} %bitcast_dynamic-update-slice_fusion.20), channel_id=1, source_target_pairs={{32,0},{64,32},{96,64},{0,96},{33,1},{65,33},{97,65},{1,97},{34,2}... | collective-permute-start | bytes 4423688 | tf_op jit(solution)/shard_map/ppermute | solution.py:37
  389.7 74.8 %collective-permute-start.26 = (bf16[4,4,72,640]{3,2,1,0:T(8,128)(2,1)}, bf16[4,4,72,640]{3,2,1,0:T(8,128)(2,1)}, u32[]{:S(2)}, u32[]{:S(2)}) collective-permute-start(bf16[4,4,72,640]{3,2,1,0:T(8,128)(2,1)} %bitcast_dynamic-update-slice_fusion.20), channel_id=1, source_target_pairs={{64,0},{96,32},{0,64},{32,96},{65,1},{97,33},{1,65},{33,97},{66,2}... | collective-permute-start | bytes 4423688 | tf_op jit(solution)/shard_map/ppermute | solution.py:37
  399.7 77.8 %collective-permute-start.51 = (bf16[4,4,72,640]{3,2,1,0:T(8,128)(2,1)}, bf16[4,4,72,640]{3,2,1,0:T(8,128)(2,1)}, u32[]{:S(2)}, u32[]{:S(2)}) collective-permute-start(bf16[4,4,72,640]{3,2,1,0:T(8,128)(2,1)} %bitcast_dynamic-update-slice_fusion.12), channel_id=1, source_target_pairs={{32,0},{64,32},{96,64},{0,96},{33,1},{65,33},{97,65},{1,97},{34,2}... | collective-permute-start | bytes 4423688 | tf_op jit(solution)/shard_map/ppermute | solution.py:37
  696.6 160.0 %collective-permute-start.88 = (bf16[4,4,72,640]{3,2,0,1:T(8,128)(2,1)}, bf16[4,4,72,640]{3,2,0,1:T(8,128)(2,1)}, u32[]{:S(2)}, u32[]{:S(2)}) collective-permute-start(bf16[4,4,72,640]{3,2,0,1:T(8,128)(2,1)} %bitcast.840), channel_id=1, source_target_pairs={{16,0},{24,8},{0,16},{8,24},{17,1},{25,9},{1,17},{9,25},{18,2},{26... | collective-permute-start | bytes 4423688 | tf_op jit(solution)/shard_map/ppermute | solution.py:37
  700.5 157.3 %collective-permute-start.87 = (bf16[4,4,72,640]{3,2,0,1:T(8,128)(2,1)}, bf16[4,4,72,640]{3,2,0,1:T(8,128)(2,1)}, u32[]{:S(2)}, u32[]{:S(2)}) collective-permute-start(bf16[4,4,72,640]{3,2,0,1:T(8,128)(2,1)} %bitcast.841), channel_id=1, source_target_pairs={{8,0},{16,8},{24,16},{0,24},{9,1},{17,9},{25,17},{1,25},{10,2},{18... | collective-permute-start | bytes 4423688 | tf_op jit(solution)/shard_map/ppermute | solution.py:37
  716.2 141.5 %collective-permute-start.86 = (bf16[4,4,72,640]{3,2,0,1:T(8,128)(2,1)}, bf16[4,4,72,640]{3,2,0,1:T(8,128)(2,1)}, u32[]{:S(2)}, u32[]{:S(2)}) collective-permute-start(bf16[4,4,72,640]{3,2,0,1:T(8,128)(2,1)} %bitcast.842), channel_id=1, source_target_pairs={{24,0},{0,8},{8,16},{16,24},{25,1},{1,9},{9,17},{17,25},{26,2},{2,... | collective-permute-start | bytes 4423688 | tf_op jit(solution)/shard_map/ppermute | solution.py:37
  772.4 82.1 %collective-permute-start.55 = (bf16[80,1152]{1,0:T(8,128)(2,1)}, bf16[80,1152]{1,0:T(8,128)(2,1)}, u32[]{:S(2)}, u32[]{:S(2)}) collective-permute-start(bf16[80,1152]{1,0:T(8,128)(2,1)} %dynamic-slice_bitcast_fusion.28), channel_id=1, source_target_pairs={{0,2},{2,0},{1,3},{3,1},{4,6},{6,4},{5,7},{7,5},{8,10},{10,8},{9,1... | collective-permute-start | bytes 552968 | tf_op jit(solution)/shard_map/ppermute | solution.py:41
  785.7 426.1 %reduce-scatter.4.cloned.1.call-start = ((), (), s32[]{:S(2)}) async-start(), calls=%async_computation.14 | async-start | bytes 7372800 | tf_op jit(solution)/shard_map/reduce_scatter | solution.py:579
  836.5 86.0 %collective-permute-start.94 = (bf16[4,4,72,640]{3,2,0,1:T(8,128)(2,1)}, bf16[4,4,72,640]{3,2,0,1:T(8,128)(2,1)}, u32[]{:S(2)}, u32[]{:S(2)}) collective-permute-start(bf16[4,4,72,640]{3,2,0,1:T(8,128)(2,1)} %bitcast.267), channel_id=1, source_target_pairs={{64,0},{96,32},{0,64},{32,96},{65,1},{97,33},{1,65},{33,97},{66,2}... | collective-permute-start | bytes 4423688 | tf_op jit(solution)/shard_map/ppermute | solution.py:37
  854.4 364.6 %reduce-scatter.6.cloned.1.call-start = ((), (), s32[]{:S(2)}) async-start(), calls=%async_computation.15 | async-start | bytes 10321920 | tf_op jit(solution)/shard_map/reduce_scatter | solution.py:579
  1057.8 74.9 %collective-permute-start.72 = (bf16[4,4,72,640]{3,2,1,0:T(8,128)(2,1)}, bf16[4,4,72,640]{3,2,1,0:T(8,128)(2,1)}, u32[]{:S(2)}, u32[]{:S(2)}) collective-permute-start(bf16[4,4,72,640]{3,2,1,0:T(8,128)(2,1)} %get-tuple-element.75), channel_id=1, source_target_pairs={{8,0},{16,8},{24,16},{0,24},{9,1},{17,9},{25,17},{1,25},{10,2},{18... | collective-permute-start | bytes 4423688 | tf_op jit(solution)/shard_map/ppermute | solution.py:37
  1059.3 73.4 %collective-permute-start.71 = (bf16[4,4,72,640]{3,2,1,0:T(8,128)(2,1)}, bf16[4,4,72,640]{3,2,1,0:T(8,128)(2,1)}, u32[]{:S(2)}, u32[]{:S(2)}) collective-permute-start(bf16[4,4,72,640]{3,2,1,0:T(8,128)(2,1)} %get-tuple-element.73), channel_id=1, source_target_pairs={{24,0},{0,8},{8,16},{16,24},{25,1},{1,9},{9,17},{17,25},{26,2},{2,... | collective-permute-start | bytes 4423688 | tf_op jit(solution)/shard_map/ppermute | solution.py:37
  1064.8 76.9 %collective-permute-start.79 = (bf16[4,4,72,640]{3,2,0,1:T(8,128)(2,1)}, bf16[4,4,72,640]{3,2,0,1:T(8,128)(2,1)}, u32[]{:S(2)}, u32[]{:S(2)}) collective-permute-start(bf16[4,4,72,640]{3,2,0,1:T(8,128)(2,1)} %bitcast.240), channel_id=1, source_target_pairs={{64,0},{96,32},{0,64},{32,96},{65,1},{97,33},{1,65},{33,97},{66,2}... | collective-permute-start | bytes 4423688 | tf_op jit(solution)/shard_map/ppermute | solution.py:37
  (430 other events, 5360.6 us)
Sparse Core Ops, SparseCore 0:
  70.2 74.4 all-gather.3
  153.7 99.2 all-gather.7
  307.3 83.3 all-gather.5
  785.8 53.6 reduce-scatter.7
  854.6 59.6 reduce-scatter.3
  975.2 82.6 reduce-scatter.5

commit v2 on v1

v2 whole, which is shorter than its diff:
```python
from functools import partial
import math

import jax
import jax.numpy as jnp
from jax import lax
from jax.experimental import pallas as pl
from jax.experimental.pallas import tpu as pltpu
from jax.sharding import Mesh, PartitionSpec as P

HEADS = 16
HEAD_DIM = 72
FREQ = 256
STEPS = 1000
D = 1152
FFN = 4608
EPSILON = 1e-06
MASK_FILL = -1000000000.0

CLIP = ("y", "z", "xl")
SEQ = ("xh", "c")
GROUP = ("xl", "xh", "c")
RING = ("xh", "xl")
ALL = ("y", "z", "xl", "xh", "c")
X_PLACE = (0, 2, 1, 3)

bf16 = jnp.bfloat16
f32 = jnp.float32


def fetch(value, axis, step):
    if axis == "x":
        pairs = [(X_PLACE[(i + step) % 4], X_PLACE[i]) for i in range(4)]
        return lax.ppermute(value, ("xl", "xh"), pairs)
    return lax.ppermute(value, axis, [((i + step) % 4, i) for i in range(4)])


def swap(value, axis):
    return lax.ppermute(value, axis, [(0, 1), (1, 0)])


def place_of(axis):
    if axis == "x":
        return lax.axis_index("xh") * 2 + lax.axis_index("xl")
    return lax.axis_index(axis)


def turn(step, row, which, rows):
    return jnp.where(step == which, row, jnp.where(step < which, 0, rows - 1))


def place_kernel(widths, own_ref, *refs):
    blocks, outs = refs[:4], refs[4:]
    for which in range(4):

        @pl.when(pl.program_id(0) == which)
        def _():
            start = 0
            for width, out in zip(widths, outs):
                out[...] = blocks[which][..., start : start + width].reshape(out.shape)
                start += width


def place(blocks, axis, pos, widths):
    lead, last = blocks[0].shape[:pos], blocks[0].shape[pos:]
    rows = math.prod(lead)
    group = min(rows, 4)
    rows //= group
    flat = [block.reshape((rows, group) + last) for block in blocks]
    zeros = (0,) * len(last)
    whole = (group,) + last

    def in_map(which):
        return lambda step, row, own: (turn(step, row, which, rows), 0) + zeros

    def out_map(step, row, own):
        return (row, 0, lax.rem(own[0] + step, 4)) + zeros

    outs = pl.pallas_call(
        partial(place_kernel, widths),
        out_shape=[
            jax.ShapeDtypeStruct((rows, group, 4) + last[:-1] + (width,), bf16) for width in widths
        ],
        grid_spec=pltpu.PrefetchScalarGridSpec(
            num_scalar_prefetch=1,
            grid=(4, rows),
            in_specs=[pl.BlockSpec((1,) + whole, in_map(which)) for which in range(4)],
            out_specs=[
                pl.BlockSpec((1, group, 1) + last[:-1] + (width,), out_map) for width in widths
            ],
        ),
        compiler_params=pltpu.CompilerParams(vmem_limit_bytes=40 * 2**20),
        cost_estimate=pl.CostEstimate(flops=0, bytes_accessed=0, transcendentals=0),
    )(place_of(axis).reshape(1), *flat)
    return [out.reshape(lead + out.shape[2:]) for out in outs]


def ring_blocks(value, axis):
    return [value] + [fetch(value, axis, step) for step in (1, 3, 2)]


def in_order(blocks):
    return [blocks[0], blocks[1], blocks[3], blocks[2]]


def after(values, earlier):
    return lax.optimization_barrier((values, earlier))[0]


def fetch_rings(jobs, earlier):
    values = after([value for value, _ in jobs], earlier)
    blocks = [[value] for value, _ in jobs]
    for step in (1, 3, 2):
        for n, (_, axis) in enumerate(jobs):
            blocks[n].append(fetch(values[n], axis, step))
    blocks = lax.optimization_barrier(blocks)
    return [in_order(own) for own in blocks], [own[1] for own in blocks]


def sum_rings(jobs, earlier):
    sent = [
        [pick(value, axis, step, pos) for step in (1, 3, 2)] for value, axis, pos in jobs
    ]
    sent = after(sent, earlier)
    arrived = [
        [fetch(own[k], axis, 4 - step) for k, step in enumerate((1, 3, 2))]
        for own, (_, axis, _) in zip(sent, jobs)
    ]
    arrived = lax.optimization_barrier(arrived)
    totals = []
    for own, (value, axis, pos) in zip(arrived, jobs):
        total = pick(value, axis, 0, pos).astype(f32)
        for block in own:
            total = total + block.astype(f32)
        totals.append(total.astype(bf16))
    return totals, [own[0] for own in arrived]


def pick(value, axis, step, pos):
    return lax.dynamic_index_in_dim(
        value, lax.rem(place_of(axis) + step, 4), pos, keepdims=False
    )


def by_core(first, second, axis, dim):
    own_first = lax.axis_index(axis) == 0
    return jnp.concatenate(
        [jnp.where(own_first, first, second), jnp.where(own_first, second, first)], axis=dim
    )


def down_pairs(other):
    pairs = []
    for d in range(128):
        y1, y0, z1, z0 = (d >> 6) & 1, (d >> 5) & 1, (d >> 4) & 1, (d >> 3) & 1
        xl, xh, core = (d >> 2) & 1, (d >> 1) & 1, d & 1
        half = 1 - core if other else core
        target = 0
        for bit in (z0, xl, xh, half, z1, y0, y1):
            target = 2 * target + bit
        pairs.append((d, target))
    return pairs


def send_down(shards):
    core = lax.axis_index("c")
    low = shards[:, :, :640]
    high = jnp.pad(shards[:, :, 640:], ((0, 0), (0, 0), (0, 128)))
    first = lax.ppermute(jnp.where(core == 0, low, high), ALL, down_pairs(False))
    second = lax.ppermute(jnp.where(core == 0, high, low), ALL, down_pairs(True))
    half = lax.axis_index("z") % 2
    return jnp.concatenate(
        [jnp.where(half == 0, first, second), jnp.where(half == 0, second, first)], axis=1
    )


def return_down(blocks):
    half = lax.axis_index("z") % 2
    top, bottom = blocks[:, :36], blocks[:, 36:]
    back = [[(b, a) for a, b in down_pairs(other)] for other in (False, True)]
    first = lax.ppermute(jnp.where(half == 0, top, bottom), ALL, back[0])
    second = lax.ppermute(jnp.where(half == 0, bottom, top), ALL, back[1])
    core = lax.axis_index("c")
    low = jnp.where(core == 0, first, second)
    high = jnp.where(core == 0, second, first)
    return jnp.concatenate([low, high[:, :, :512]], axis=2)


def to_pieces(shard, groups):
    rows = shard.shape[0]
    value = shard.reshape(rows, groups, 2, 2, 2, -1)
    value = value.transpose(4, 3, 2, 0, 1, 5)
    return value.reshape(8, rows, -1)


def from_pieces(value, groups):
    rows = value.shape[1]
    value = value.reshape(2, 2, 2, rows, groups, -1)
    value = value.transpose(3, 4, 2, 1, 0, 5)
    return value.reshape(rows, -1)


def swap_group(value, axes):
    return lax.all_to_all(value, axes, split_axis=0, concat_axis=0, tiled=True)


def widen(value, width):
    return jnp.pad(value, [(0, 0)] * (value.ndim - 1) + [(0, width - value.shape[-1])])


def noise_table(count):
    beta_values = jnp.linspace(0.0001, 0.02, count, dtype=f32)
    return jnp.cumprod(1.0 - beta_values)


def time_features(timesteps, feature_count):
    half_count = feature_count // 2
    frequency = jnp.exp(-math.log(10000.0) * jnp.arange(half_count, dtype=f32) / half_count)
    angles = timesteps.astype(f32)[:, None] * frequency
    return jnp.concatenate([jnp.cos(angles), jnp.sin(angles)], axis=1)


def normalize(values):
    average = jnp.mean(values, axis=-1, keepdims=True)
    centred = values - average
    inverse_std = lax.rsqrt(jnp.mean(centred * centred, axis=-1, keepdims=True) + EPSILON)
    return (centred * inverse_std, inverse_std)


def norm_back(normal_rows, inverse_std, normal_grad):
    first_mean = jnp.mean(normal_grad, axis=-1, keepdims=True)
    second_mean = jnp.mean(normal_grad * normal_rows, axis=-1, keepdims=True)
    return inverse_std * (normal_grad - first_mean - normal_rows * second_mean)


def product(operand, weight):
    return jnp.dot(operand, weight, preferred_element_type=f32)


def product_back(operand, weight):
    return lax.dot_general(operand, weight, (((1,), (1,)), ((), ())), preferred_element_type=f32)


def outer_sum(operand, partner):
    return lax.dot_general(operand, partner, (((0,), (0,)), ((), ())), preferred_element_type=f32)


def apart(own):
    other = swap(own, "c")
    first = lax.axis_index("c") == 0
    low, high = jnp.where(first, own, other), jnp.where(first, other, own)
    return jnp.concatenate([low[j] for j in range(4)] + [high[j] for j in range(4)], axis=1)


def windows(value, start):
    rows = value.shape[0]
    pieces = jnp.swapaxes(value.reshape(rows, 4, 144), 0, 1)
    return jnp.pad(pieces, ((0, 0), (0, 0), (start, 112 - start)))


def norm_value(values):
    centred = values - jnp.mean(values, axis=-1, keepdims=True)
    return centred * lax.rsqrt(jnp.mean(centred * centred, axis=-1, keepdims=True) + EPSILON)


def softmax_value(queries, keys, bias):
    scores = product_back(queries, keys) * HEAD_DIM ** (-0.5)
    if bias is not None:
        scores = scores + bias
    exponent = jnp.exp(scores - jnp.max(scores, axis=-1, keepdims=True))
    return exponent / jnp.sum(exponent, axis=-1, keepdims=True)


def head_back(queries, keys, values, mixed_grad, bias):
    factor = HEAD_DIM ** (-0.5)
    probability = softmax_value(queries, keys, bias)
    prob_grad = product_back(mixed_grad, values)
    value_grad = outer_sum(probability.astype(bf16), mixed_grad)
    inner = jnp.sum(probability * prob_grad, axis=-1, keepdims=True)
    score_grad = (probability * (prob_grad - inner)).astype(bf16)
    return product(score_grad, keys) * factor, outer_sum(score_grad, queries) * factor, value_grad


def whole(shape):
    return pl.BlockSpec(shape, lambda j: (0,) * len(shape))


def part(shape):
    return pl.BlockSpec((1,) + shape, lambda j: (j,) + (0,) * len(shape))


def shaped(shape, dtype=bf16):
    return jax.ShapeDtypeStruct(shape, dtype)


def by_piece(kernel, out_shape, in_specs, out_specs, scratch, args):
    return pl.pallas_call(
        kernel,
        out_shape=out_shape,
        grid=(4,),
        in_specs=in_specs,
        out_specs=out_specs,
        scratch_shapes=scratch,
        compiler_params=pltpu.CompilerParams(vmem_limit_bytes=48 * 2**20),
        cost_estimate=pl.CostEstimate(flops=0, bytes_accessed=0, transcendentals=0),
    )(*args)


def first_piece(action):
    pl.when(pl.program_id(0) == 0)(action)


def last_piece(action):
    pl.when(pl.program_id(0) == 3)(action)


def self_kernel(groups, x_ref, shift_ref, scale_ref, weight_ref, *refs):
    bias_ref = refs[0] if groups == 1 else None
    normed_ref, packed_ref, mixed_ref = refs[-3:]

    @first_piece
    def _():
        normed = norm_value(x_ref[...]) * (1.0 + scale_ref[...]) + shift_ref[...]
        normed_ref[...] = normed.astype(bf16)

    packed = product(normed_ref[...], weight_ref[0]).astype(bf16)
    packed_ref[0] = packed
    rows = 320 // groups
    for group in range(groups):
        mixed = []
        for head in range(2):
            queries, keys, values = (
                packed[group * rows : group * rows + rows, start : start + 72]
                for start in (72 * head, 144 + 72 * head, 288 + 72 * head)
            )
            bias = None if bias_ref is None else bias_ref[...]
            probability = softmax_value(queries, keys, bias).astype(bf16)
            mixed.append(product(probability, values))
        mixed_ref[0, group * rows : group * rows + rows, :] = jnp.concatenate(
            mixed, axis=1
        ).astype(bf16)


def self_forward(groups, hidden_state, shift, scale, weights, bias):
    specs = [whole((320, D)), whole((1, D)), whole((1, D)), part((D, 640))]
    args = [hidden_state, shift[None], scale[None], weights]
    if groups == 1:
        specs.append(whole((320, 320)))
        args.append(bias)
    return by_piece(
        partial(self_kernel, groups),
        [shaped((320, D)), shaped((4, 320, 640)), shaped((4, 320, 144))],
        specs,
        [whole((320, D)), part((320, 640)), part((320, 144))],
        [],
        args,
    )


def self_back_kernel(groups, extras, *refs):
    packed_ref, mixed_grad_ref, weight_ref, normed_ref = refs[:4]
    pairs = refs[4 : 4 + 2 * extras]
    bias_ref = refs[4 + 2 * extras] if groups == 1 else None
    grad_ref, normed_grad_ref, total_ref = refs[-3:]
    packed, mixed_grad = packed_ref[0], mixed_grad_ref[0]
    rows = 320 // groups
    strips = []
    for group in range(groups):
        at = group * rows
        parts = []
        for head in range(2):
            queries, keys, values = (
                packed[at : at + rows, start : start + 72]
                for start in (72 * head, 144 + 72 * head, 288 + 72 * head)
            )
            bias = None if bias_ref is None else bias_ref[...]
            own_grad = mixed_grad[at : at + rows, 72 * head : 72 * head + 72]
            parts.append(head_back(queries, keys, values, own_grad, bias))
        line = [parts[head][which] for which in range(3) for head in range(2)]
        line.append(jnp.zeros((rows, 208), f32))
        strips.append(jnp.concatenate(line, axis=1).astype(bf16))
    packed_grad = strips[0] if groups == 1 else jnp.concatenate(strips, axis=0)
    width = weight_ref.shape[2]
    grad = outer_sum(normed_ref[...], packed_grad)
    if width > 640:
        grad = jnp.concatenate([grad, jnp.zeros((D, width - 640), f32)], axis=1)
    for n in range(extras):
        start = (384, 512, 640)[n]
        own = outer_sum(pairs[2 * n][...], pairs[2 * n + 1][0])
        lines = [grad[:, :start], grad[:, start : start + 256] + own, grad[:, start + 256 :]]
        grad = jnp.concatenate([line for line in lines if line.shape[1] > 0], axis=1)
    grad_ref[0] = grad.astype(bf16)
    back = product_back(packed_grad, weight_ref[0, :, :640])

    @first_piece
    def _():
        total_ref[...] = back

    @pl.when(pl.program_id(0) > 0)
    def _():
        total_ref[...] += back

    @last_piece
    def _():
        normed_grad_ref[...] = total_ref[...].astype(bf16)


def self_back(groups, packed, mixed_grad, weights, normed, pairs, bias):
    width = weights.shape[-1]
    specs = [part((320, 640)), part((320, 144)), part((D, width)), whole((320, D))]
    args = [packed, mixed_grad, weights, normed]
    for rows, window in pairs:
        specs += [whole((320, D)), part((320, 256))]
        args += [rows, window]
    if groups == 1:
        specs.append(whole((320, 320)))
        args.append(bias)
    return by_piece(
        partial(self_back_kernel, groups, len(pairs)),
        [shaped((4, D, width)), shaped((320, D))],
        specs,
        [part((D, width)), whole((320, D))],
        [pltpu.VMEM((320, D), f32)],
        args,
    )


def out_kernel(start, mixed_ref, weight_ref, out_ref):
    low = start // 128 * 128
    value = product(mixed_ref[...], weight_ref[0, :, low : low + 256])
    out_ref[0] = value[:, start - low : start - low + 144].astype(bf16)


def out_forward(mixed_rows, weights, start):
    return by_piece(
        partial(out_kernel, start),
        shaped((4, 320, 144)),
        [whole((320, D)), part(weights.shape[1:])],
        part((320, 144)),
        [],
        [mixed_rows, weights],
    )


def out_back_kernel(low, window_ref, weight_ref, out_ref, total_ref):
    back = product_back(window_ref[0], weight_ref[0, :, low : low + 256])

    @first_piece
    def _():
        total_ref[...] = back

    @pl.when(pl.program_id(0) > 0)
    def _():
        total_ref[...] += back

    @last_piece
    def _():
        for n in range(8):
            out_ref[n] = total_ref[:, 144 * n : 144 * n + 144].astype(bf16)


def out_back(window, weights, low):
    halves = by_piece(
        partial(out_back_kernel, low),
        shaped((8, 320, 144)),
        [part((320, 256)), part(weights.shape[1:])],
        whole((8, 320, 144)),
        [pltpu.VMEM((320, D), f32)],
        [window, weights],
    ).reshape(2, 4, 320, 144)
    core = lax.axis_index("c")
    keep = lax.dynamic_index_in_dim(halves, core, 0, keepdims=False)
    give = lax.dynamic_index_in_dim(halves, 1 - core, 0, keepdims=False)
    return (keep.astype(f32) + swap(give, "c").astype(f32)).astype(bf16)


def cross_kernel(x_ref, gain_ref, weight_ref, key_ref, value_ref, bias_ref, normed_ref, query_ref, mixed_ref):
    @first_piece
    def _():
        normed_ref[...] = (norm_value(x_ref[...]) * gain_ref[...]).astype(bf16)

    queries = product(normed_ref[...], weight_ref[0, :, :256]).astype(bf16)[:, 64:208]
    query_ref[0] = queries
    keys, values = key_ref[0], value_ref[0]
    mixed = []
    for head in range(2):
        own = slice(72 * head, 72 * head + 72)
        probability = softmax_value(queries[:, own], keys[:, own], bias_ref[...])
        mixed.append(product(probability.astype(bf16), values[:, own]))
    mixed_ref[0] = jnp.concatenate(mixed, axis=1).astype(bf16)


def cross_forward(hidden_state, gain, weights, keys, values, bias):
    return by_piece(
        cross_kernel,
        [shaped((320, D)), shaped((4, 320, 144)), shaped((4, 320, 144))],
        [whole((320, D)), whole((1, D)), part((D, 384))]
        + [part((128, 144)), part((128, 144)), whole((1, 128))],
        [whole((320, D)), part((320, 144)), part((320, 144))],
        [],
        [hidden_state, gain[None], weights, keys, values, bias],
    )


def cross_back_kernel(
    query_ref, key_ref, value_ref, grad_ref, weight_ref, bias_ref, window_ref, key_out, value_out, normed_ref, total_ref
):
    queries, keys, values, mixed_grad = query_ref[0], key_ref[0], value_ref[0], grad_ref[0]
    parts = []
    for head in range(2):
        own = slice(72 * head, 72 * head + 72)
        parts.append(
            head_back(queries[:, own], keys[:, own], values[:, own], mixed_grad[:, own], bias_ref[...])
        )
    zeros = jnp.zeros((320, 64), f32)
    window = jnp.concatenate(
        [zeros, parts[0][0], parts[1][0], zeros[:, :48]], axis=1
    ).astype(bf16)
    window_ref[0] = window
    key_out[0] = jnp.concatenate([parts[0][1], parts[1][1]], axis=1).astype(bf16)
    value_out[0] = jnp.concatenate([parts[0][2], parts[1][2]], axis=1).astype(bf16)
    back = product_back(window, weight_ref[0, :, :256])

    @first_piece
    def _():
        total_ref[...] = back

    @pl.when(pl.program_id(0) > 0)
    def _():
        total_ref[...] += back

    @last_piece
    def _():
        normed_ref[...] = total_ref[...].astype(bf16)


def cross_back(queries, keys, values, mixed_grad, weights, bias):
    return by_piece(
        cross_back_kernel,
        [shaped((4, 320, 256)), shaped((4, 128, 144)), shaped((4, 128, 144)), shaped((320, D))],
        [part((320, 144)), part((128, 144)), part((128, 144)), part((320, 144)), part((D, 384)), whole((1, 128))],
        [part((320, 256)), part((128, 144)), part((128, 144)), whole((320, D))],
        [pltpu.VMEM((320, D), f32)],
        [queries, keys, values, mixed_grad, weights, bias],
    )


GELU_SCALE = math.sqrt(2.0 / math.pi)


def down_halves(down_ref):
    blocks = [(y, 2 * z) for y in range(4) for z in range(2)]
    low = jnp.concatenate([down_ref[0, y, z] for y, z in blocks], axis=0)
    high = jnp.concatenate([down_ref[0, y, z + 1, :, :512] for y, z in blocks], axis=0)
    return low, high


def feed_kernel(x_ref, shift_ref, scale_ref, up_ref, down_ref, normed_ref, inner_ref, active_ref, out_ref, total_ref):
    @first_piece
    def _():
        normed = norm_value(x_ref[...]) * (1.0 + scale_ref[...]) + shift_ref[...]
        normed_ref[...] = normed.astype(bf16)

    inner = product(normed_ref[...], up_ref[0])
    inner_ref[0] = inner
    bent = jnp.tanh(GELU_SCALE * (inner + 0.044715 * inner * inner * inner))
    active = (0.5 * inner * (1.0 + bent)).astype(bf16)[:, :576]
    active_ref[0] = active
    low, high = down_halves(down_ref)

    @first_piece
    def _():
        total_ref[:, :640] = product(active, low)
        total_ref[:, 640:] = product(active, high)

    @pl.when(pl.program_id(0) > 0)
    def _():
        total_ref[:, :640] += product(active, low)
        total_ref[:, 640:] += product(active, high)

    @last_piece
    def _():
        out_ref[...] = total_ref[...].astype(bf16)


def feed_forward(hidden_state, shift, scale, up, down):
    return by_piece(
        feed_kernel,
        [shaped((320, D)), shaped((4, 320, 640), f32), shaped((4, 320, 576)), shaped((320, D))],
        [whole((320, D)), whole((1, D)), whole((1, D)), part((D, 640)), part((4, 4, 72, 640))],
        [whole((320, D)), part((320, 640)), part((320, 576)), whole((320, D))],
        [pltpu.VMEM((320, D), f32)],
        [hidden_state, shift[None], scale[None], up, down],
    )


def feed_back_kernel(
    grad_ref, inner_ref, active_ref, normed_ref, up_ref, down_ref, up_out, down_out, normed_grad_ref, total_ref
):
    low, high = down_halves(down_ref)
    low_grad, high_grad = grad_ref[:, :640], grad_ref[:, 640:]
    low_out = outer_sum(active_ref[0], low_grad).astype(bf16)
    high_out = outer_sum(active_ref[0], high_grad).astype(bf16)
    for block in range(8):
        rows = slice(72 * block, 72 * block + 72)
        down_out[0, block // 2, block % 2 * 2] = low_out[rows]
        down_out[0, block // 2, block % 2 * 2 + 1, :, :512] = high_out[rows]
        down_out[0, block // 2, block % 2 * 2 + 1, :, 512:] = jnp.zeros((72, 128), bf16)
    inner = inner_ref[0]
    active_grad = product_back(low_grad, low) + product_back(high_grad, high)
    active_grad = jnp.concatenate([active_grad, jnp.zeros((320, 64), f32)], axis=1)
    square = inner * inner
    bent = jnp.tanh(GELU_SCALE * inner * (1.0 + 0.044715 * square))
    slope = 0.5 * (1.0 + bent) + 0.5 * inner * (1.0 - bent * bent) * GELU_SCALE * (
        1.0 + 0.134145 * square
    )
    inner_grad = (active_grad * slope).astype(bf16)
    up_out[0] = outer_sum(normed_ref[...], inner_grad).astype(bf16)
    back = product_back(inner_grad, up_ref[0])

    @first_piece
    def _():
        total_ref[...] = back

    @pl.when(pl.program_id(0) > 0)
    def _():
        total_ref[...] += back

    @last_piece
    def _():
        normed_grad_ref[...] = total_ref[...].astype(bf16)


def feed_back(output_grad, inner, active, normed, up, down):
    return by_piece(
        feed_back_kernel,
        [shaped((4, D, 640)), shaped((4, 4, 4, 72, 640)), shaped((320, D))],
        [whole((320, D)), part((320, 640)), part((320, 576)), whole((320, D))]
        + [part((D, 640)), part((4, 4, 72, 640))],
        [part((D, 640)), part((4, 4, 72, 640)), whole((320, D))],
        [pltpu.VMEM((320, D), f32)],
        [output_grad, inner, active, normed, up, down],
    )


def both_cores(partial_rows):
    return partial_rows.astype(f32) + swap(partial_rows, "c").astype(f32)


def attention_block(groups, hidden_state, modulation, weights, bias):
    normed, packed, mixed = self_forward(
        groups, hidden_state, modulation[0], modulation[1], weights, bias
    )
    mixed_rows = apart(mixed)
    branch = apart(out_forward(mixed_rows, weights, 432)).astype(f32)
    stored = (hidden_state, normed, packed, mixed_rows, branch)
    return (hidden_state + modulation[2] * branch, stored)


def attention_block_back(groups, incoming, stored, modulation, weights, pairs, bias, earlier):
    hidden_state, normed, packed, mixed_rows, branch = stored
    gate_grad = jnp.sum(incoming * branch, axis=0)
    branch_grad = (modulation[2] * incoming).astype(bf16)
    window = windows(own_columns(branch_grad), 48)
    mixed_grad = after(out_back(window, weights, 384), earlier)
    weight_grad, normed_grad = self_back(
        groups, packed, mixed_grad, weights, normed, [(mixed_rows, window)] + pairs, bias
    )
    normed_grad = both_cores(normed_grad)
    normal_rows, inverse_std = normalize(hidden_state)
    scale_grad = jnp.sum(normed_grad * normal_rows, axis=0)
    shift_grad = jnp.sum(normed_grad, axis=0)
    upstream = incoming + norm_back(normal_rows, inverse_std, normed_grad * (1.0 + modulation[1]))
    return (upstream, weight_grad, (shift_grad, scale_grad, gate_grad))


def feed_block(hidden_state, modulation, up, down):
    normed, inner, active, output = feed_forward(
        hidden_state, modulation[3], modulation[4], up, down
    )
    output = both_cores(output)
    return (hidden_state + modulation[5] * output, (hidden_state, normed, inner, active, output))


def feed_block_back(incoming, stored, modulation, up, down):
    hidden_state, normed, inner, active, output = stored
    gate_grad = jnp.sum(incoming * output, axis=0)
    output_grad = (modulation[5] * incoming).astype(bf16)
    up_grad, down_grad, normed_grad = feed_back(output_grad, inner, active, normed, up, down)
    normed_grad = both_cores(normed_grad)
    normal_rows, inverse_std = normalize(hidden_state)
    scale_grad = jnp.sum(normed_grad * normal_rows, axis=0)
    shift_grad = jnp.sum(normed_grad, axis=0)
    upstream = incoming + norm_back(normal_rows, inverse_std, normed_grad * (1.0 + modulation[4]))
    return (upstream, up_grad, down_grad, (shift_grad, scale_grad, gate_grad))


def scatter_ring(grad):
    return lax.psum_scatter(grad, RING, scatter_dimension=0, tiled=False)


def own_columns(value):
    half = value.shape[1] // 2
    return jnp.where(lax.axis_index("c") == 0, value[:, :half], value[:, half:])


def local(
    latents,
    noise_sample,
    timesteps,
    text_states,
    text_lengths,
    cotangent,
    time_input,
    time_output,
    spatial_table,
    spatial_projection,
    spatial_output,
    spatial_up,
    spatial_down,
    temporal_table,
    temporal_projection,
    temporal_output,
    cross_query,
    cross_text,
    cross_output,
    cross_gain,
    temporal_up,
    temporal_down,
):
    core, far = lax.axis_index("c"), lax.axis_index("xh")
    clip = (lax.axis_index("y") * 4 + lax.axis_index("z")) * 2 + lax.axis_index("xl")
    me = clip * 4 + far * 2 + core

    sent = jnp.concatenate(
        [
            to_pieces(spatial_up, 1),
            to_pieces(spatial_projection, 3),
            to_pieces(spatial_output, 1),
            to_pieces(temporal_up, 1),
            to_pieces(temporal_projection, 3),
            to_pieces(temporal_output, 1),
            to_pieces(cross_query, 1),
            to_pieces(cross_output, 1),
        ],
        axis=2,
    )
    words = cross_text.reshape(4, 8, 2, 2, 2, 288).transpose(4, 3, 1, 0, 2, 5).reshape(4, 8, 2304)
    words = jnp.pad(words, ((0, 0), (0, 1), (0, 0)))
    near = lax.axis_index("xl")
    words = jnp.stack([jnp.where(near == 0, words, 0), jnp.where(near == 1, words, 0)])
    sent = jnp.concatenate([sent, words.reshape(8, 9, 2304)], axis=2)
    mine = swap_group(sent, GROUP)
    words = lax.dynamic_slice_in_dim(mine[:, :8, 2592:], near * 4, 4, 0)
    words = words.reshape(4, 8, 4, 576).transpose(0, 2, 1, 3).reshape(128, 576)
    words = widen(words, 640)
    mine = mine[..., :2592].reshape(72, 2592)
    shards = jnp.stack([spatial_down, temporal_down])
    s_up = widen(mine[:, :576], 640)
    s_att = widen(mine[:, 576:1152], 640)
    t_up = widen(mine[:, 1152:1728], 640)
    t_att = widen(mine[:, 1728:2592], 896)
    downs = send_down(shards)

    split_steps = jnp.stack([timesteps // 32, timesteps % 32], axis=1).reshape(-1).astype(bf16)
    note = jnp.concatenate(
        [
            time_input.reshape(-1),
            spatial_table.reshape(-1),
            temporal_table.reshape(-1),
            cross_gain,
            split_steps,
            jnp.zeros((9,), bf16),
        ]
    )
    notes = swap_group(jnp.broadcast_to(note, (128, 2432)), ALL)
    full_time_input = notes[:, :2304].reshape(FREQ, D)

    near_words = by_core(words, swap(words, "xl"), "xl", 0)
    rings, first_done = fetch_rings(
        [
            (jnp.concatenate([s_up, t_att, s_att], axis=1), "y"),
            (jnp.concatenate([downs[0], downs[1], t_up], axis=1), "z"),
        ],
        (),
    )
    up_att, s_att = place(rings[0], "y", 0, (1536, 640))
    s_down, down_up = place(rings[1], "z", 0, (640, 1280))
    rings, second_done = fetch_rings(
        [
            (up_att, "z"),
            (jnp.concatenate([s_att, s_down], axis=2), "x"),
            (down_up, "y"),
            (near_words, "y"),
        ],
        (first_done, full_time_input),
    )
    steps = notes[::4, 2421:2423].astype(f32)
    steps = (steps[:, 0] * 32.0 + steps[:, 1]).astype(jnp.int32)
    embedded = time_features(steps, FREQ).astype(bf16)
    pre_time = product(embedded, full_time_input)
    lifted = jax.nn.silu(pre_time).astype(bf16)
    own_lifted = lax.dynamic_slice_in_dim(lifted, me * 9, 9, 1)
    shares = after(product(own_lifted, time_output), first_done)
    shares = swap_group(shares.reshape(128, 1728), ALL)
    shares, rings = lax.optimization_barrier((shares, rings))
    s_up, t_att = place(rings[0], "z", 1, (640, 896))
    s_att, s_down = place(rings[1], "x", 0, (640, 640))
    t_down, t_up = place(rings[2], "y", 0, (640, 640))
    (words,) = place(rings[3], "y", 0, (640,))
    t_att = lax.all_gather(t_att.reshape(D, 896), RING, axis=0, tiled=False)
    words = lax.all_gather(words.reshape(1024, 640), "z", axis=0, tiled=False).reshape(4096, 640)
    t_up = lax.all_gather(t_up.reshape(D, 640), RING, axis=0, tiled=False)
    t_down = lax.all_gather(t_down.reshape(D, 640), RING, axis=0, tiled=False)
    t_down = t_down.reshape(4, 4, 4, 72, 640)

    tables = notes[:, 2304:2412].reshape(128, 12, 9).transpose(1, 0, 2).reshape(2, 6, D)
    full_gain = notes[:, 2412:2421].reshape(D).astype(f32)
    shared = jnp.sum(shares, axis=0)
    shared = by_core(shared, swap(shared, "c"), "c", 0)
    shared = by_core(shared, swap(shared, "xh"), "xh", 0).reshape(6, D)
    rings, _ = fetch_rings([(s_att, "z"), (s_down, "y"), (s_up, "x")], (second_done, shared))
    (s_att,) = place(rings[0], "z", 2, (640,))
    s_att = s_att.reshape(4, D, 640)
    (s_down,) = place(rings[1], "y", 1, (640,))
    (s_up,) = place(rings[2], "x", 0, (640,))
    s_up = s_up.reshape(4, D, 640)

    spatial_mod = tables[0].astype(f32) + shared
    temporal_mod = tables[1].astype(f32) + shared

    alpha_bars = noise_table(STEPS)
    picked = jnp.sum(jnp.where(jnp.arange(STEPS) == timesteps[0], alpha_bars, 0.0))
    signal_scale = jnp.sqrt(picked)

    frames = jnp.stack([latents[0, 0], noise_sample[0, 0]])
    other = swap(frames, "c")

    def noised(pair):
        return signal_scale * pair[0].astype(f32) + jnp.sqrt(1.0 - picked) * pair[1].astype(f32)

    hidden_state = by_core(noised(frames), noised(other), "c", 0)

    hidden_state, spatial_attention = attention_block(2, hidden_state, spatial_mod, s_att, None)
    hidden_state, spatial_mlp = feed_block(hidden_state, spatial_mod, s_up, s_down)

    def to_patches(rows):
        halves = rows.reshape(2, 2, 80, D)
        keep = lax.dynamic_index_in_dim(halves, far, 1, keepdims=False)
        give = lax.dynamic_index_in_dim(halves, 1 - far, 1, keepdims=False)
        return jnp.concatenate([keep, swap(give, "xh")], axis=0).reshape(320, D)

    patch_rows = to_patches(hidden_state.astype(bf16))
    own_cotangent = cotangent[0, 0]
    incoming = to_patches(by_core(own_cotangent, swap(own_cotangent, "c"), "c", 0)).astype(f32)

    text_order = text_states[0].reshape(120, 4, 4, 2, 128).transpose(0, 2, 1, 3, 4)
    text_order = text_order.reshape(120, 4096)
    text_rows = product(text_order, words)[:, :576].astype(bf16)
    other_text = swap(text_rows, "xh")
    def text_pieces(value):
        pieces = jnp.swapaxes(value.reshape(120, 4, 144), 0, 1)
        return jnp.pad(pieces, ((0, 0), (0, 8), (0, 0)))

    text_keys = text_pieces(by_core(text_rows[:, :288], other_text[:, :288], "xh", 1))
    text_values = text_pieces(by_core(text_rows[:, 288:], other_text[:, 288:], "xh", 1))
    text_bias = jnp.where(jnp.arange(128) < text_lengths[0], 0.0, MASK_FILL)[None]
    row = jnp.arange(320) % 80
    patch_bias = jnp.where(row[:, None] == row[None], 0.0, MASK_FILL)

    t_cross = t_att[..., 512:]
    hidden_state = patch_rows.astype(f32)
    hidden_state, temporal_attention = attention_block(
        1, hidden_state, temporal_mod, t_att, patch_bias
    )
    cross_state = hidden_state
    cross_normed, cross_queries, cross_mixed = cross_forward(
        cross_state, full_gain, t_cross, text_keys, text_values, text_bias
    )
    cross_mixed = apart(cross_mixed)
    hidden_state = cross_state + apart(out_forward(cross_mixed, t_cross, 208)).astype(f32)
    hidden_state, temporal_mlp = feed_block(hidden_state, temporal_mod, t_up, t_down)

    finished = hidden_state.astype(bf16).reshape(4, 80, D)
    keep = lax.dynamic_index_in_dim(finished, core, 0, keepdims=False)
    give = lax.dynamic_index_in_dim(finished, 2 + core, 0, keepdims=False)
    activations = by_core(keep, swap(give, "xh"), "xh", 0)[None, None]

    incoming, t_up_grad, t_down_grad, t_mlp_mod = feed_block_back(
        incoming, temporal_mlp, temporal_mod, t_up, t_down
    )
    t_up_grad = scatter_ring(t_up_grad).reshape(4, 4, 72, 640)
    t_down_grad = scatter_ring(t_down_grad.reshape(4, D, 640)).reshape(4, 4, 72, 640)
    cross_grad = incoming.astype(bf16)
    out_window = windows(own_columns(cross_grad), 80)
    cross_mixed_grad = out_back(out_window, t_cross, 128)
    query_window, key_grad, value_grad, normed_grad = cross_back(
        cross_queries, text_keys, text_values, cross_mixed_grad, t_cross, text_bias
    )
    normed_grad = both_cores(normed_grad)
    normal_rows, inverse_std = normalize(cross_state)
    gain_grad = jnp.sum(normed_grad * normal_rows, axis=0)
    incoming = incoming + norm_back(normal_rows, inverse_std, normed_grad * full_gain)
    key_grad = jnp.swapaxes(key_grad[:, :120], 0, 1).reshape(120, 576)
    value_grad = jnp.swapaxes(value_grad[:, :120], 0, 1).reshape(120, 576)

    def text_half(which):
        def half(value):
            return lax.dynamic_slice_in_dim(value, which * 288, 288, 1)

        return jnp.concatenate([half(key_grad), half(value_grad)], axis=1)

    text_grad = text_half(far).astype(f32) + swap(text_half(1 - far), "xh").astype(f32)
    words_grad = outer_sum(text_order, widen(text_grad.astype(bf16), 640)).astype(bf16)
    words_grad = words_grad.reshape(4, 1024, 640)
    words_grad = lax.psum_scatter(words_grad, "z", scatter_dimension=0, tiled=False)
    words_grad = words_grad.reshape(4, 256, 640)
    words_grad = lax.psum_scatter(words_grad, "y", scatter_dimension=0, tiled=False)
    words_grad = words_grad.reshape(2, 128, 640)
    words_grad = lax.dynamic_index_in_dim(words_grad, near, 0, keepdims=False).astype(f32) + swap(
        lax.dynamic_index_in_dim(words_grad, 1 - near, 0, keepdims=False), "xl"
    ).astype(f32)
    words_grad = words_grad.astype(bf16)

    incoming, t_att_grad, t_att_mod = attention_block_back(
        1,
        incoming,
        temporal_attention,
        temporal_mod,
        t_att,
        [(cross_normed, query_window), (cross_mixed, out_window)],
        patch_bias,
        text_grad,
    )
    t_mod_grad = jnp.stack(t_att_mod + t_mlp_mod)

    back = incoming.astype(bf16).reshape(4, 80, D)
    theirs = swap(back[2:], "xh")
    t_att_grad = scatter_ring(t_att_grad).reshape(4, 4, 72, 896)


    frame_grad = by_core(back[:2], theirs, "xh", 1).reshape(320, D).astype(f32)
    frame_grad, s_up_grad, s_down_grad, s_mlp_mod = feed_block_back(
        frame_grad, spatial_mlp, spatial_mod, s_up, s_down
    )
    s_up_grad = s_up_grad.reshape(4, 4, 4, 72, 640)
    (s_up_grad, s_down_grad), s_done = sum_rings(
        [(s_up_grad, "z", 2), (s_down_grad, "y", 1)], ()
    )
    frame_grad, s_att_grad, s_att_mod = attention_block_back(
        2, frame_grad, spatial_attention, spatial_mod, s_att, [], None, s_done
    )
    latent_grad = signal_scale * lax.dynamic_index_in_dim(frame_grad.reshape(2, 160, D), core, 0)
    s_mod_grad = jnp.stack(s_att_mod + s_mlp_mod)
    s_att_grad = s_att_grad.reshape(4, 4, 4, 72, 640)
    (att_x_y, att_x_z, att_y_z), done = sum_rings(
        [
            (s_att_grad[..., :256], "z", 2),
            (s_att_grad[..., 256:512], "y", 1),
            (s_att_grad[..., 512:], "x", 0),
        ],
        (),
    )
    up_att = jnp.concatenate([t_up_grad, t_att_grad], axis=3)
    down_att = jnp.concatenate([t_down_grad, att_y_z], axis=3)
    up_x_y = jnp.concatenate([s_up_grad, att_x_y], axis=3)
    down_x_z = jnp.concatenate([s_down_grad, att_x_z], axis=3)
    (up_att, down_att, up_x_y, down_x_z), done = sum_rings(
        [(up_att, "z", 1), (down_att, "y", 0), (up_x_y, "y", 1), (down_x_z, "x", 0)], done
    )
    down = jnp.concatenate([down_att, down_x_z], axis=2)
    (up_att, down, up_x), done = sum_rings(
        [(up_att, "y", 0), (down, "z", 0), (up_x_y, "x", 0)], done
    )
    downs = return_down(jnp.stack([down[:, 768:1408], down[:, :640]])).astype(f32)
    s_down_done, t_down_done = downs[0], downs[1]
    words_grad = swap_group(words_grad[:, :576].reshape(4, 32, 576), SEQ)
    words_grad = words_grad.reshape(2, 2, 32, 2, 288).transpose(2, 3, 1, 0, 4).reshape(32, 2304)

    returned = jnp.concatenate(
        [
            up_x[:, :576],
            up_x[:, 640:],
            down[:, 1408:],
            down[:, 640:704],
            up_att[:, :576],
            up_att[:, 640:1504],
        ],
        axis=1,
    )
    returned = swap_group(returned.reshape(8, 9, 2592), GROUP).astype(f32)
    s_up_grad = from_pieces(returned[..., :576], 1)
    s_proj_grad = from_pieces(returned[..., 576:1008], 3)
    s_out_grad = from_pieces(returned[..., 1008:1152], 1)
    t_up_grad = from_pieces(returned[..., 1152:1728], 1)
    t_proj_grad = from_pieces(returned[..., 1728:2160], 3)
    t_out_grad = from_pieces(returned[..., 2160:2304], 1)
    x_query_grad = from_pieces(returned[..., 2304:2448], 1)
    x_out_grad = from_pieces(returned[..., 2448:], 1)

    shared_grad = (s_mod_grad + t_mod_grad).reshape(4, 1728)
    shared_grad = shared_grad + swap(shared_grad, "xh")
    quarter = lax.dynamic_index_in_dim(shared_grad, far * 2 + core, 0, keepdims=False)
    table_part = jnp.stack([s_mod_grad, t_mod_grad]).reshape(12, 128, 9).transpose(1, 0, 2)
    table_part = jnp.concatenate([table_part.reshape(128, 108), gain_grad.reshape(128, 9)], axis=1)
    table_part = jnp.where(core == 0, table_part, 0.0)
    letter = jnp.concatenate(
        [jnp.broadcast_to(quarter, (128, 1728)), table_part, jnp.zeros((128, 75), f32)], axis=1
    )
    letters = swap_group(letter, ALL)
    all_shared = letters[:, :1728].reshape(32, 6 * D)
    table_sum = jnp.sum(letters[:, 1728:1845], axis=0)
    s_table_grad = table_sum[:54].reshape(6, 9)
    t_table_grad = table_sum[54:108].reshape(6, 9)
    cross_gain_grad = table_sum[108:]

    def exact(a, b, dims):
        return lax.dot_general(
            a, b, (dims, ((), ())), precision=lax.Precision.HIGHEST, preferred_element_type=f32
        )

    time_output_grad = exact(own_lifted.astype(f32), all_shared, ((0,), (0,)))
    lifted_grad = exact(all_shared, time_output.astype(f32), ((1,), (1,)))
    own_pre = lax.dynamic_slice_in_dim(pre_time, me * 9, 9, 1)
    own_pre_grad = jax.vjp(jax.nn.silu, own_pre)[1](lifted_grad)[0]
    card = jnp.broadcast_to(widen(own_pre_grad.reshape(288), 384), (128, 384))
    cards = swap_group(card, ALL)[:, :288].reshape(128, 32, 9)
    pre_grad = cards.transpose(1, 0, 2).reshape(32, D)
    own_embedded = lax.dynamic_slice_in_dim(embedded, me * 2, 2, 1).astype(f32)
    time_input_grad = exact(own_embedded, pre_grad, ((0,), (0,)))

    return (
        activations,
        latent_grad[None],
        time_input_grad,
        time_output_grad,
        s_table_grad,
        s_proj_grad,
        s_out_grad,
        s_up_grad,
        s_down_done,
        t_table_grad,
        t_proj_grad,
        t_out_grad,
        x_query_grad,
        words_grad.astype(f32),
        x_out_grad,
        cross_gain_grad,
        t_up_grad,
        t_down_done,
    )


def solution(mesh):
    fine = Mesh(mesh.devices.reshape(4, 4, 2, 2, 2), ALL)
    frames = P(CLIP, SEQ, None, None)
    rows = P(ALL, None)
    columns = P(None, ALL)
    in_specs = (
        frames,
        frames,
        P(CLIP),
        P(CLIP, None, None),
        P(CLIP),
        frames,
        rows,
        rows,
        columns,
        rows,
        rows,
        rows,
        rows,
        columns,
        rows,
        rows,
        rows,
        rows,
        rows,
        P(ALL),
        rows,
        rows,
    )
    out_specs = (
        frames,
        frames,
        rows,
        rows,
        columns,
        rows,
        rows,
        rows,
        rows,
        columns,
        rows,
        rows,
        rows,
        rows,
        rows,
        P(ALL),
        rows,
        rows,
    )
    return jax.shard_map(local, mesh=fine, in_specs=in_specs, out_specs=out_specs, check_vma=False)
```

time: 1310 us -> 1160 us (0.89)
  Pallas kernels: 0 us -> 185 us
  matrix products: 159 us -> 13.9 us
  local copies, waits for them, and re-layouts: 331 us -> 243 us
  other arithmetic: 164 us -> 117 us
  waiting for transfers between devices: 379 us -> 338 us
  starting transfers between devices: 246 us -> 224 us
    pallas_call x0 -> x25, Pallas kernels: none -> 185 us  [the longest x16 158 us: by_piece(): pl.pallas_call(kernel, out_shape=out_shape, grid=(4,), in_specs=in_specs,...]
    ppermute x75 -> x48, waiting for transfers between devices: 308 us -> 192 us  [fetch(): return lax.ppermute(value, axis, [((i + step) % 4, i) for i in range(4)])]
    dot_general x40 -> x0, matrix products: 68.5 us -> none  [the longest x22 39.6 us: product_back(): lax.dot_general(operand, weight, (((1,), (1,)), ((), ())), preferred_elem...]
    ppermute x75 -> x48, starting transfers between devices: 143 us -> 79.8 us  [fetch(): return lax.ppermute(value, axis, [((i + step) % 4, i) for i in range(4)])]
    ppermute x9 -> x15, waiting for transfers between devices: 5.29 us -> 53.8 us  [fetch(): return lax.ppermute(value, ('xl', 'xh'), pairs)]
    dot_general x23 -> x1, matrix products: 43.8 us -> 3.97 us  [outer_sum(): lax.dot_general(operand, partner, (((0,), (0,)), ((), ())), preferred_ele...]
    dynamic_update_slice x40 -> x0, local copies, waits for them, and re-layouts: 38 us -> none  [place(): lax.dynamic_update_index_in_dim(out, block, lax.rem(own + step, 4), pos)]
    dot_general x25 -> x3, matrix products: 44.2 us -> 7.07 us  [product(): return jnp.dot(operand, weight, preferred_element_type=f32)]
  transfers between devices with their start and end apart: 130 -> 112, of which waited for: 49 -> 38; matrix products, arithmetic and copies ran while one was open for 42% -> 23% of each run, Pallas kernels for 0% -> 12%
where the time goes in v2:
time: 1160 us; the launch traced here: 1140 us
  waiting for transfers between devices  338 us (29%)
  local copies, waits for them, and re-layouts  243 us (21%)
  starting transfers between devices  224 us (19%)
  Pallas kernels  185 us (16%)
  other arithmetic  117 us (10%)
  between operations  20.2 us (2%)
  matrix products  13.9 us (1%)
    ppermute x48, waiting for transfers between devices, fetch(): return lax.ppermute(value, axis, [((i + step) % 4, i) for i in range(4)])  192 us
    pallas_call x16, Pallas kernels, by_piece(): pl.pallas_call(kernel, out_shape=out_shape, grid=(4,), in_specs=in_specs,...  158 us
    ppermute x48, starting transfers between devices, fetch(): return lax.ppermute(value, axis, [((i + step) % 4, i) for i in range(4)])  79.8 us
    unnamed x402, local copies, waits for them, and re-layouts  67.5 us
    all_to_all x7, starting transfers between devices, swap_group(): return lax.all_to_all(value, axes, split_axis=0, concat_axis=0, tiled=True)  59 us
    all_to_all x7, waiting for transfers between devices, swap_group(): return lax.all_to_all(value, axes, split_axis=0, concat_axis=0, tiled=True)  55.4 us
    ppermute x15, waiting for transfers between devices, fetch(): return lax.ppermute(value, ('xl', 'xh'), pairs)  53.8 us
    ppermute x29, starting transfers between devices, swap(): return lax.ppermute(value, axis, [(0, 1), (1, 0)])  42.8 us
  transfers between devices with their start and end apart: 112, of which 38 were waited for; matrix products, arithmetic and copies ran while one was open for 23% of the time, Pallas kernels for 12%

profile of v2, /device:TPU:0, one launch (start us, length us, event | category | flops | bytes accessed | tf_op | source)
XLA Modules:
  0.0 1141.2 jit_solution(6213631385170200827)
XLA Ops:
  42.0 13.9 %all-to-all-start = ((bf16[128,2,1216]{2,1,0:T(2,128)(2,1)}), bf16[128,2,1216]{2,1,0:T(2,128)(2,1)}, u32[]{:S(2)}, u32[]{:S(2)}) async-start(bf16[128,2,1216]{2,1,0:T(2,128)(2,1)} %reshape.1017), calls=%async_computation | async-start | bytes 1310720 | tf_op jit(solution)/shard_map/all_to_all | solution.py:204
  79.8 12.1 %collective-permute-done.7 = bf16[72,1920]{1,0:T(8,128)(2,1)S(1)} collective-permute-done((bf16[72,1920]{1,0:T(8,128)(2,1)S(1)}, bf16[72,1920]{1,0:T(8,128)(2,1)S(1)}, u32[]{:S(2)}, u32[]{:S(2)}) %collective-permute-start.7) | collective-permute-done | bytes 276512 | tf_op jit(solution)/shard_map/ppermute | solution.py:35
  146.9 18.8 %all-to-all-done.2 = f32[128,1,1728]{2,1,0:T(1,128)} async-done(((f32[128,1,1728]{2,1,0:T(1,128)}), f32[128,1,1728]{2,1,0:T(1,128)}, u32[]{:S(2)}, u32[]{:S(2)}) %all-to-all-start.2) | async-done | bytes 884768 | tf_op jit(solution)/shard_map/all_to_all | solution.py:204
  171.4 15.6 %collective-permute-done.18 = bf16[4,72,1280]{2,1,0:T(8,128)(2,1)} collective-permute-done((bf16[4,72,1280]{2,1,0:T(8,128)(2,1)S(1)}, bf16[4,72,1280]{2,1,0:T(8,128)(2,1)}, u32[]{:S(2)}, u32[]{:S(2)}) %collective-permute-start.18) | collective-permute-done | bytes 737312 | tf_op jit(solution)/shard_map/ppermute | solution.py:35
  244.9 28.2 %collective-permute-done.24.refs_1_ = bf16[4,4,72,640]{3,2,1,0:T(8,128)(2,1)} collective-permute-done((bf16[4,4,72,640]{3,2,1,0:T(8,128)(2,1)}, bf16[4,4,72,640]{3,2,1,0:T(8,128)(2,1)}, u32[]{:S(2)}, u32[]{:S(2)}) %collective-permute-start.24) | collective-permute-done | bytes 1474592 | tf_op jit(solution)/shard_map/ppermute | solution.py:35
  287.0 22.9 %collective-permute-done.28 = bf16[4,4,72,640]{3,2,1,0:T(8,128)(2,1)} collective-permute-done((bf16[4,4,72,640]{3,2,1,0:T(8,128)(2,1)}, bf16[4,4,72,640]{3,2,1,0:T(8,128)(2,1)}, u32[]{:S(2)}, u32[]{:S(2)}) %collective-permute-start.28) | collective-permute-done | bytes 1474592 | tf_op jit(solution)/shard_map/ppermute | solution.py:35
  309.9 28.5 %collective-permute-done.30 = bf16[4,4,72,640]{3,2,1,0:T(8,128)(2,1)} collective-permute-done((bf16[4,4,72,640]{3,2,1,0:T(8,128)(2,1)S(1)}, bf16[4,4,72,640]{3,2,1,0:T(8,128)(2,1)}, u32[]{:S(2)}, u32[]{:S(2)}) %collective-permute-start.30) | collective-permute-done | bytes 1474592 | tf_op jit(solution)/shard_map/ppermute | solution.py:34
  355.0 10.8 shard_map.354
  406.2 10.7 shard_map.358
  426.6 10.9 collective-permute-done.36
  540.7 10.7 shard_map.365
  551.4 18.1 %shard_map.366 = (bf16[4,1152,640]{2,1,0:T(8,128)(2,1)}, bf16[4,4,4,72,640]{4,3,2,1,0:T(8,128)(2,1)}, bf16[320,1152]{1,0:T(8,128)(2,1)}) custom-call(bf16[320,1152]{1,0:T(8,128)(2,1)S(1)} %copy-done.28, f32[4,320,640]{2,1,0:T(8,128)} %get-tuple-element.274.inner_ref, bf16[4,320,576]{2,1,0:T(8,128)(2,1)S(1)} %get-tuple-element.275.active_ref, ...), custom_call_target="tpu_custom_call" | custom-call | tf_op jit(solution)/shard_map/pallas_call | solution.py:297
  662.6 21.2 %shard_map.370 = (bf16[4,1152,896]{2,1,0:T(8,128)(2,1)}, bf16[320,1152]{1,0:T(8,128)(2,1)S(1)}) custom-call(bf16[4,320,640]{2,1,0:T(8,128)(2,1)} %copy-done.39, bf16[4,320,144]{2,1,0:T(8,128)(2,1)S(1)} %fusion.20.refs_1_, bf16[4,1152,896]{2,1,0:T(8,128)(2,1)} %all-gather.5.cloned.1.call-done.weight_ref.refs_2_, bf16[320,1152]{1,0:T(8,128)(2,1)S(1)} %copy-done.54, ...), custom_call_target="tpu_custom_call" | custom-call | tf_op jit(solution)/shard_map/pallas_call | solution.py:297
  697.7 11.4 collective-permute-done.52
  710.8 17.6 %shard_map.371 = (bf16[4,1152,640]{2,1,0:T(8,128)(2,1)}, bf16[4,4,4,72,640]{4,3,2,1,0:T(8,128)(2,1)}, bf16[320,1152]{1,0:T(8,128)(2,1)S(1)}) custom-call(bf16[320,1152]{1,0:T(8,128)(2,1)S(1)} %fusion.16.grad_ref, f32[4,320,640]{2,1,0:T(8,128)} %get-tuple-element.288.inner_ref, bf16[4,320,576]{2,1,0:T(8,128)(2,1)S(1)} %copy-done.38, ...), custom_call_target="tpu_custom_call" | custom-call | tf_op jit(solution)/shard_map/pallas_call | solution.py:297
  762.5 13.7 %collective-permute-done.55 = bf16[4,4,72,640]{3,2,0,1:T(8,128)(2,1)} collective-permute-done((bf16[4,4,72,640]{3,2,0,1:T(8,128)(2,1)}, bf16[4,4,72,640]{3,2,0,1:T(8,128)(2,1)}, u32[]{:S(2)}, u32[]{:S(2)}) %collective-permute-start.55) | collective-permute-done | bytes 1474592 | tf_op jit(solution)/shard_map/ppermute | solution.py:35
  786.3 35.3 %collective-permute-done.56 = bf16[4,4,72,640]{3,2,0,1:T(8,128)(2,1)} collective-permute-done((bf16[4,4,72,640]{3,2,0,1:T(8,128)(2,1)}, bf16[4,4,72,640]{3,2,0,1:T(8,128)(2,1)}, u32[]{:S(2)}, u32[]{:S(2)}) %collective-permute-start.56) | collective-permute-done | bytes 1474592 | tf_op jit(solution)/shard_map/ppermute | solution.py:35
  827.9 20.0 %shard_map.373 = (bf16[4,1152,640]{2,1,0:T(8,128)(2,1)}, bf16[320,1152]{1,0:T(8,128)(2,1)S(1)}) custom-call(bf16[4,320,640]{2,1,0:T(8,128)(2,1)S(1)} %copy-done.36, bf16[4,320,144]{2,1,0:T(8,128)(2,1)S(1)} %fusion.19.refs_1_, bf16[4,1152,640]{2,1,0:T(8,128)(2,1)} %bitcast.543, bf16[320,1152]{1,0:T(8,128)(2,1)S(1)} %copy-done.50, ...), custom_call_target="tpu_custom_call" | custom-call | tf_op jit(solution)/shard_map/pallas_call | solution.py:297
  921.6 16.2 %collective-permute-start.62 = (f32[4,1728]{1,0:T(4,128)S(1)}, f32[4,1728]{1,0:T(4,128)}, u32[]{:S(2)}, u32[]{:S(2)}) collective-permute-start(f32[4,1728]{1,0:T(4,128)S(1)} %add.653), channel_id=1, source_target_pairs={{0,2},{2,0},{1,3},{3,1},{4,6},{6,4},{5,7},{7,5},{8,10},{10,8},{9,1... | collective-permute-start | bytes 82952 | tf_op jit(solution)/shard_map/ppermute | solution.py:39
  945.2 12.8 %all-to-all-start.3 = ((f32[128,1,1920]{2,1,0:T(1,128)}), f32[128,1,1920]{2,1,0:T(1,128)}, u32[]{:S(2)}, u32[]{:S(2)}) async-start(f32[128,1,1920]{2,1,0:T(1,128)} %all_to_all.43), calls=%async_computation.3 | async-start | bytes 1966080 | tf_op jit(solution)/shard_map/all_to_all | solution.py:204
  970.9 32.4 %collective-permute-done.75 = bf16[4,72,768]{2,1,0:T(8,128)(2,1)S(1)} collective-permute-done((bf16[4,72,768]{2,1,0:T(8,128)(2,1)S(1)}, bf16[4,72,768]{2,1,0:T(8,128)(2,1)S(1)}, u32[]{:S(2)}, u32[]{:S(2)}) %collective-permute-start.75) | collective-permute-done | bytes 442400 | tf_op jit(solution)/shard_map/ppermute | solution.py:35
  1020.7 9.9 all-to-all-start.4
  1037.1 18.3 %all-to-all-done.4 = f32[128,1,384]{2,1,0:T(1,128)S(1)} async-done(((f32[128,1,384]{2,1,0:T(1,128)}), f32[128,1,384]{2,1,0:T(1,128)S(1)}, u32[]{:S(2)}, u32[]{:S(2)}) %all-to-all-start.4) | async-done | bytes 196640 | tf_op jit(solution)/shard_map/all_to_all | solution.py:204
  1114.4 10.9 all-to-all-done.5
  (998 shorter events, 700.3 us)
Async XLA Ops:
  117.2 69.8 %collective-permute-start.10 = (bf16[4,72,1536]{2,1,0:T(8,128)(2,1)S(1)}, bf16[4,72,1536]{2,1,0:T(8,128)(2,1)}, u32[]{:S(2)}, u32[]{:S(2)}) collective-permute-start(bf16[4,72,1536]{2,1,0:T(8,128)(2,1)S(1)} %bitcast.568), channel_id=1, source_target_pairs={{8,0},{16,8},{24,16},{0,24},{9,1},{17,9},{25,17},{1,25},{10,2},{18... | collective-permute-start | bytes 2654216 | tf_op jit(solution)/shard_map/ppermute | solution.py:35
  117.2 69.8 %collective-permute-start.11 = (bf16[4,72,1536]{2,1,0:T(8,128)(2,1)S(1)}, bf16[4,72,1536]{2,1,0:T(8,128)(2,1)}, u32[]{:S(2)}, u32[]{:S(2)}) collective-permute-start(bf16[4,72,1536]{2,1,0:T(8,128)(2,1)S(1)} %bitcast.569), channel_id=1, source_target_pairs={{24,0},{0,8},{8,16},{16,24},{25,1},{1,9},{9,17},{17,25},{26,2},{2,... | collective-permute-start | bytes 2654216 | tf_op jit(solution)/shard_map/ppermute | solution.py:35
  143.1 295.2 %all-gather.5.cloned.1.call-start = ((), (), s32[]{:S(2)}) async-start(), calls=%async_computation.12 | async-start | bytes 10321920 | tf_op jit(solution)/shard_map/all_gather | solution.py:811
  193.1 260.4 %all-gather.7.cloned.1.call-start = ((), (), s32[]{:S(2)}) async-start(), calls=%async_computation.13 | async-start | bytes 6553600 | tf_op jit(solution)/shard_map/all_gather | solution.py:812
  197.7 341.6 %all-gather.9.cloned.1.call-start = ((), (), s32[]{:S(2)}) async-start(), calls=%async_computation.14 | async-start | bytes 7372800 | tf_op jit(solution)/shard_map/all_gather | solution.py:813
  202.2 337.2 %all-gather.11.cloned.1.call-start = ((), (), s32[]{:S(2)}) async-start(), calls=%async_computation.15 | async-start | bytes 7372800 | tf_op jit(solution)/shard_map/all_gather | solution.py:814
  206.4 66.7 %collective-permute-start.24 = (bf16[4,4,72,640]{3,2,1,0:T(8,128)(2,1)}, bf16[4,4,72,640]{3,2,1,0:T(8,128)(2,1)}, u32[]{:S(2)}, u32[]{:S(2)}) collective-permute-start(bf16[4,4,72,640]{3,2,1,0:T(8,128)(2,1)} %bitcast.55.refs_0_), channel_id=1, source_target_pairs={{8,0},{16,8},{24,16},{0,24},{9,1},{17,9},{25,17},{1,25},{10,2},{18... | collective-permute-start | bytes 4423688 | tf_op jit(solution)/shard_map/ppermute | solution.py:35
  209.8 67.0 %collective-permute-start.25 = (bf16[4,4,72,640]{3,2,1,0:T(8,128)(2,1)}, bf16[4,4,72,640]{3,2,1,0:T(8,128)(2,1)}, u32[]{:S(2)}, u32[]{:S(2)}) collective-permute-start(bf16[4,4,72,640]{3,2,1,0:T(8,128)(2,1)} %bitcast.55.refs_0_), channel_id=1, source_target_pairs={{24,0},{0,8},{8,16},{16,24},{25,1},{1,9},{9,17},{17,25},{26,2},{2,... | collective-permute-start | bytes 4423688 | tf_op jit(solution)/shard_map/ppermute | solution.py:35
  210.2 69.7 %collective-permute-start.26 = (bf16[4,4,72,640]{3,2,1,0:T(8,128)(2,1)}, bf16[4,4,72,640]{3,2,1,0:T(8,128)(2,1)}, u32[]{:S(2)}, u32[]{:S(2)}) collective-permute-start(bf16[4,4,72,640]{3,2,1,0:T(8,128)(2,1)} %bitcast.55.refs_0_), channel_id=1, source_target_pairs={{16,0},{24,8},{0,16},{8,24},{17,1},{25,9},{1,17},{9,25},{18,2},{26... | collective-permute-start | bytes 4423688 | tf_op jit(solution)/shard_map/ppermute | solution.py:35
  212.3 67.6 %collective-permute-start.27 = (bf16[4,4,72,640]{3,2,1,0:T(8,128)(2,1)}, bf16[4,4,72,640]{3,2,1,0:T(8,128)(2,1)S(1)}, u32[]{:S(2)}, u32[]{:S(2)}) collective-permute-start(bf16[4,4,72,640]{3,2,1,0:T(8,128)(2,1)} %bitcast.56), channel_id=1, source_target_pairs={{32,0},{64,32},{96,64},{0,96},{33,1},{65,33},{97,65},{1,97},{34,2}... | collective-permute-start | bytes 4423688 | tf_op jit(solution)/shard_map/ppermute | solution.py:35
  242.9 67.0 %collective-permute-start.28 = (bf16[4,4,72,640]{3,2,1,0:T(8,128)(2,1)}, bf16[4,4,72,640]{3,2,1,0:T(8,128)(2,1)}, u32[]{:S(2)}, u32[]{:S(2)}) collective-permute-start(bf16[4,4,72,640]{3,2,1,0:T(8,128)(2,1)} %bitcast.56), channel_id=1, source_target_pairs={{96,0},{0,32},{32,64},{64,96},{97,1},{1,33},{33,65},{65,97},{98,2}... | collective-permute-start | bytes 4423688 | tf_op jit(solution)/shard_map/ppermute | solution.py:35
  276.9 61.6 %collective-permute-start.30 = (bf16[4,4,72,640]{3,2,1,0:T(8,128)(2,1)S(1)}, bf16[4,4,72,640]{3,2,1,0:T(8,128)(2,1)}, u32[]{:S(2)}, u32[]{:S(2)}) collective-permute-start(bf16[4,4,72,640]{3,2,1,0:T(8,128)(2,1)S(1)} %bitcast.558), channel_id=1, source_target_pairs={{4,0},{2,4},{6,2},{0,6},{5,1},{3,5},{7,3},{1,7},{12,8},{10,12},{14... | collective-permute-start | bytes 4423688 | tf_op jit(solution)/shard_map/ppermute | solution.py:34
  280.0 62.8 %collective-permute-start.32 = (bf16[4,4,72,640]{3,2,1,0:T(8,128)(2,1)S(1)}, bf16[4,4,72,640]{3,2,1,0:T(8,128)(2,1)}, u32[]{:S(2)}, u32[]{:S(2)}) collective-permute-start(bf16[4,4,72,640]{3,2,1,0:T(8,128)(2,1)S(1)} %bitcast.560), channel_id=1, source_target_pairs={{2,0},{6,4},{0,2},{4,6},{3,1},{7,5},{1,3},{5,7},{10,8},{14,12},{8,... | collective-permute-start | bytes 4423688 | tf_op jit(solution)/shard_map/ppermute | solution.py:34
  388.9 549.1 %reduce-scatter.12.cloned.1.call-start = ((), (), s32[]{:S(2)}) async-start(), calls=%async_computation.19 | async-start | bytes 6553600 | tf_op jit(solution)/shard_map/reduce_scatter | solution.py:916
  422.6 76.6 %collective-permute-start.45 = (bf16[2,80,1152]{2,1,0:T(8,128)(2,1)}, bf16[2,80,1152]{2,1,0:T(8,128)(2,1)}, u32[]{:S(2)}, u32[]{:S(2)}) collective-permute-start(bf16[2,80,1152]{2,1,0:T(8,128)(2,1)} %get-tuple-element.482), channel_id=1, source_target_pairs={{0,2},{2,0},{1,3},{3,1},{4,6},{6,4},{5,7},{7,5},{8,10},{10,8},{9,1... | collective-permute-start | bytes 1105928 | tf_op jit(solution)/shard_map/ppermute | solution.py:39
  635.8 322.2 %reduce-scatter.10.cloned.1.call-start = ((), (), s32[]{:S(2)}) async-start(), calls=%async_computation.18 | async-start | bytes 7372800 | tf_op jit(solution)/shard_map/reduce_scatter | solution.py:699
  636.4 323.9 %reduce-scatter.6.cloned.1.call-start = ((), (), s32[]{:S(2)}) async-start(), calls=%async_computation.16 | async-start | bytes 7372800 | tf_op jit(solution)/shard_map/reduce_scatter | solution.py:699
  637.1 323.1 %reduce-scatter.8.cloned.1.call-start = ((), (), s32[]{:S(2)}) async-start(), calls=%async_computation.17 | async-start | bytes 10321920 | tf_op jit(solution)/shard_map/reduce_scatter | solution.py:699
  684.7 372.3 %reduce-scatter.14.cloned.1.call-start = ((), (), s32[]{:S(2)}) async-start(), calls=%async_computation.20 | async-start | bytes 1638400 | tf_op jit(solution)/shard_map/reduce_scatter | solution.py:918
  755.6 66.0 %collective-permute-start.56 = (bf16[4,4,72,640]{3,2,0,1:T(8,128)(2,1)}, bf16[4,4,72,640]{3,2,0,1:T(8,128)(2,1)}, u32[]{:S(2)}, u32[]{:S(2)}) collective-permute-start(bf16[4,4,72,640]{3,2,0,1:T(8,128)(2,1)} %bitcast.622), channel_id=1, source_target_pairs={{8,0},{16,8},{24,16},{0,24},{9,1},{17,9},{25,17},{1,25},{10,2},{18... | collective-permute-start | bytes 4423688 | tf_op jit(solution)/shard_map/ppermute | solution.py:35
  757.6 68.1 %collective-permute-start.57 = (bf16[4,4,72,640]{3,2,0,1:T(8,128)(2,1)}, bf16[4,4,72,640]{3,2,0,1:T(8,128)(2,1)}, u32[]{:S(2)}, u32[]{:S(2)}) collective-permute-start(bf16[4,4,72,640]{3,2,0,1:T(8,128)(2,1)} %bitcast.621), channel_id=1, source_target_pairs={{16,0},{24,8},{0,16},{8,24},{17,1},{25,9},{1,17},{9,25},{18,2},{26... | collective-permute-start | bytes 4423688 | tf_op jit(solution)/shard_map/ppermute | solution.py:35
  759.3 66.5 %collective-permute-start.58 = (bf16[4,4,72,640]{3,2,1,0:T(8,128)(2,1)}, bf16[4,4,72,640]{3,2,1,0:T(8,128)(2,1)}, u32[]{:S(2)}, u32[]{:S(2)}) collective-permute-start(bf16[4,4,72,640]{3,2,1,0:T(8,128)(2,1)} %get-tuple-element.298), channel_id=1, source_target_pairs={{96,0},{0,32},{32,64},{64,96},{97,1},{1,33},{33,65},{65,97},{98,2}... | collective-permute-start | bytes 4423688 | tf_op jit(solution)/shard_map/ppermute | solution.py:35
  760.3 65.4 %collective-permute-start.59 = (bf16[4,4,72,640]{3,2,1,0:T(8,128)(2,1)}, bf16[4,4,72,640]{3,2,1,0:T(8,128)(2,1)}, u32[]{:S(2)}, u32[]{:S(2)}) collective-permute-start(bf16[4,4,72,640]{3,2,1,0:T(8,128)(2,1)} %get-tuple-element.299), channel_id=1, source_target_pairs={{32,0},{64,32},{96,64},{0,96},{33,1},{65,33},{97,65},{1,97},{34,2}... | collective-permute-start | bytes 4423688 | tf_op jit(solution)/shard_map/ppermute | solution.py:35
  945.2 66.8 %all-to-all-start.3 = ((f32[128,1,1920]{2,1,0:T(1,128)}), f32[128,1,1920]{2,1,0:T(1,128)}, u32[]{:S(2)}, u32[]{:S(2)}) async-start(f32[128,1,1920]{2,1,0:T(1,128)} %all_to_all.43), calls=%async_computation.3 | async-start | bytes 1966080 | tf_op jit(solution)/shard_map/all_to_all | solution.py:204
  (286 other events, 3698.1 us)
Sparse Core Ops, SparseCore 0:
  193.2 81.4 all-gather.4
  276.4 88.5 all-gather.6
  366.7 68.7 all-gather.8
  437.0 69.5 all-gather.10
  635.9 57.2 reduce-scatter.11
  695.5 61.1 reduce-scatter.9
  759.1 63.6 reduce-scatter.5
  825.3 92.3 reduce-scatter.7
  938.1 37.9 reduce-scatter.13

commit v3 on v2

--- a/solution.py
+++ b/solution.py
@@ -107,6 +107,22 @@
     return lax.optimization_barrier((values, earlier))[0]
 
 
+def tie_kernel(*refs):
+    pass
+
+
+def tie(value, *earlier):
+    anywhere = pl.BlockSpec(memory_space=pl.ANY)
+    return pl.pallas_call(
+        tie_kernel,
+        out_shape=jax.ShapeDtypeStruct(value.shape, value.dtype),
+        in_specs=[anywhere] * (1 + len(earlier)),
+        out_specs=anywhere,
+        input_output_aliases={0: 0},
+        cost_estimate=pl.CostEstimate(flops=0, bytes_accessed=0, transcendentals=0),
+    )(value, *earlier)
+
+
 def fetch_rings(jobs, earlier):
     values = after([value for value, _ in jobs], earlier)
     blocks = [[value] for value, _ in jobs]
@@ -117,23 +133,68 @@
     return [in_order(own) for own in blocks], [own[1] for own in blocks]
 
 
+def gather_rings(jobs, earlier):
+    values = after([value for value, _ in jobs], earlier)
+    near = [(fetch(v, axis, 1), fetch(v, axis, 3)) for v, (_, axis) in zip(values, jobs)]
+    near = lax.optimization_barrier(near)
+    half = [value.shape[0] // 2 for value in values]
+    across = [
+        (fetch(up[:h], axis, 1), fetch(down[h:], axis, 3))
+        for (up, down), h, (_, axis) in zip(near, half, jobs)
+    ]
+    near, across = lax.optimization_barrier((near, across))
+    blocks = [
+        [value, up, jnp.concatenate(pair, axis=0), down]
+        for (value, _), (up, down), pair in zip(jobs, near, across)
+    ]
+    return blocks, [pair[0] for pair in across]
+
+
+def ring_block(parts, axis, step):
+    blocks = [pick(value, axis, step, pos) for value, pos in parts]
+    return blocks[0] if len(blocks) == 1 else jnp.concatenate(blocks, axis=-1)
+
+
+def add(*values):
+    total = values[0].astype(f32)
+    for value in values[1:]:
+        total = total + value.astype(f32)
+    return total.astype(bf16)
+
+
 def sum_rings(jobs, earlier):
-    sent = [
-        [pick(value, axis, step, pos) for step in (1, 3, 2)] for value, axis, pos in jobs
-    ]
+    sent = [[ring_block(parts, axis, step) for step in (1, 3, 2)] for parts, axis in jobs]
     sent = after(sent, earlier)
     arrived = [
         [fetch(own[k], axis, 4 - step) for k, step in enumerate((1, 3, 2))]
-        for own, (_, axis, _) in zip(sent, jobs)
+        for own, (_, axis) in zip(sent, jobs)
     ]
     arrived = lax.optimization_barrier(arrived)
-    totals = []
-    for own, (value, axis, pos) in zip(arrived, jobs):
-        total = pick(value, axis, 0, pos).astype(f32)
-        for block in own:
-            total = total + block.astype(f32)
-        totals.append(total.astype(bf16))
+    totals = [add(ring_block(parts, axis, 0), *own) for own, (parts, axis) in zip(arrived, jobs)]
     return totals, [own[0] for own in arrived]
+
+
+def scatter_rings(jobs, earlier):
+    sent = after([ring_block(parts, axis, 2) for parts, axis in jobs], earlier)
+    half = [value.shape[0] // 2 for value in sent]
+    across = [
+        (fetch(value[:h], axis, 3), fetch(value[h:], axis, 1))
+        for value, h, (_, axis) in zip(sent, half, jobs)
+    ]
+    across = lax.optimization_barrier(across)
+    near = []
+    for (low, high), h, (parts, axis) in zip(across, half, jobs):
+        up, down = ring_block(parts, axis, 1), ring_block(parts, axis, 3)
+        up = jnp.concatenate([add(up[:h], low), up[h:]], axis=0)
+        down = jnp.concatenate([down[:h], add(down[h:], high)], axis=0)
+        near.append((up, down))
+    near = lax.optimization_barrier(near)
+    near = [
+        (fetch(up, axis, 3), fetch(down, axis, 1)) for (up, down), (_, axis) in zip(near, jobs)
+    ]
+    near = lax.optimization_barrier(near)
+    totals = [add(ring_block(parts, axis, 0), *pair) for pair, (parts, axis) in zip(near, jobs)]
+    return totals, [pair[0] for pair in across], [pair[0] for pair in near]
 
 
 def pick(value, axis, step, pos):
@@ -357,11 +418,12 @@
     )
 
 
-def self_back_kernel(groups, extras, *refs):
+def self_back_kernel(groups, extras, cuts, *refs):
     packed_ref, mixed_grad_ref, weight_ref, normed_ref = refs[:4]
     pairs = refs[4 : 4 + 2 * extras]
     bias_ref = refs[4 + 2 * extras] if groups == 1 else None
-    grad_ref, normed_grad_ref, total_ref = refs[-3:]
+    normed_grad_ref, total_ref = refs[-2:]
+    grad_refs = refs[-2 - len(cuts) : -2]
     packed, mixed_grad = packed_ref[0], mixed_grad_ref[0]
     rows = 320 // groups
     strips = []
@@ -389,7 +451,10 @@
         own = outer_sum(pairs[2 * n][...], pairs[2 * n + 1][0])
         lines = [grad[:, :start], grad[:, start : start + 256] + own, grad[:, start + 256 :]]
         grad = jnp.concatenate([line for line in lines if line.shape[1] > 0], axis=1)
-    grad_ref[0] = grad.astype(bf16)
+    start = 0
+    for cut, grad_ref in zip(cuts, grad_refs):
+        grad_ref[0] = grad[:, start : start + cut].astype(bf16)
+        start += cut
     back = product_back(packed_grad, weight_ref[0, :, :640])
 
     @first_piece
@@ -405,7 +470,7 @@
         normed_grad_ref[...] = total_ref[...].astype(bf16)
 
 
-def self_back(groups, packed, mixed_grad, weights, normed, pairs, bias):
+def self_back(groups, packed, mixed_grad, weights, normed, pairs, bias, cuts):
     width = weights.shape[-1]
     specs = [part((320, 640)), part((320, 144)), part((D, width)), whole((320, D))]
     args = [packed, mixed_grad, weights, normed]
@@ -415,14 +480,15 @@
     if groups == 1:
         specs.append(whole((320, 320)))
         args.append(bias)
-    return by_piece(
-        partial(self_back_kernel, groups, len(pairs)),
-        [shaped((4, D, width)), shaped((320, D))],
+    results = by_piece(
+        partial(self_back_kernel, groups, len(pairs), cuts),
+        [shaped((4, D, cut)) for cut in cuts] + [shaped((320, D))],
         specs,
-        [part((D, width)), whole((320, D))],
+        [part((D, cut)) for cut in cuts] + [whole((320, D))],
         [pltpu.VMEM((320, D), f32)],
         args,
     )
+    return results[:-1], results[-1]
 
 
 def out_kernel(start, mixed_ref, weight_ref, out_ref):
@@ -479,7 +545,7 @@
     def _():
         normed_ref[...] = (norm_value(x_ref[...]) * gain_ref[...]).astype(bf16)
 
-    queries = product(normed_ref[...], weight_ref[0, :, :256]).astype(bf16)[:, 64:208]
+    queries = product(normed_ref[...], weight_ref[0, :, 512:768]).astype(bf16)[:, 64:208]
     query_ref[0] = queries
     keys, values = key_ref[0], value_ref[0]
     mixed = []
@@ -494,7 +560,7 @@
     return by_piece(
         cross_kernel,
         [shaped((320, D)), shaped((4, 320, 144)), shaped((4, 320, 144))],
-        [whole((320, D)), whole((1, D)), part((D, 384))]
+        [whole((320, D)), whole((1, D)), part((D, 896))]
         + [part((128, 144)), part((128, 144)), whole((1, 128))],
         [whole((320, D)), part((320, 144)), part((320, 144))],
         [],
@@ -519,7 +585,7 @@
     window_ref[0] = window
     key_out[0] = jnp.concatenate([parts[0][1], parts[1][1]], axis=1).astype(bf16)
     value_out[0] = jnp.concatenate([parts[0][2], parts[1][2]], axis=1).astype(bf16)
-    back = product_back(window, weight_ref[0, :, :256])
+    back = product_back(window, weight_ref[0, :, 512:768])
 
     @first_piece
     def _():
@@ -538,7 +604,7 @@
     return by_piece(
         cross_back_kernel,
         [shaped((4, 320, 256)), shaped((4, 128, 144)), shaped((4, 128, 144)), shaped((320, D))],
-        [part((320, 144)), part((128, 144)), part((128, 144)), part((320, 144)), part((D, 384)), whole((1, 128))],
+        [part((320, 144)), part((128, 144)), part((128, 144)), part((320, 144)), part((D, 896)), whole((1, 128))],
         [part((320, 256)), part((128, 144)), part((128, 144)), whole((320, D))],
         [pltpu.VMEM((320, D), f32)],
         [queries, keys, values, mixed_grad, weights, bias],
@@ -643,6 +709,25 @@
     )
 
 
+def words_kernel(text_ref, grad_ref, out_ref):
+    out_ref[...] = outer_sum(text_ref[...], grad_ref[...]).astype(bf16)
+
+
+def words_back(text, grad):
+    return pl.pallas_call(
+        words_kernel,
+        out_shape=shaped((4096, 640)),
+        grid=(8,),
+        in_specs=[
+            pl.BlockSpec((120, 512), lambda j: (0, j)),
+            pl.BlockSpec((120, 640), lambda j: (0, 0)),
+        ],
+        out_specs=pl.BlockSpec((512, 640), lambda j: (j, 0)),
+        compiler_params=pltpu.CompilerParams(vmem_limit_bytes=40 * 2**20),
+        cost_estimate=pl.CostEstimate(flops=0, bytes_accessed=0, transcendentals=0),
+    )(text, grad)
+
+
 def both_cores(partial_rows):
     return partial_rows.astype(f32) + swap(partial_rows, "c").astype(f32)
 
@@ -657,14 +742,14 @@
     return (hidden_state + modulation[2] * branch, stored)
 
 
-def attention_block_back(groups, incoming, stored, modulation, weights, pairs, bias, earlier):
+def attention_block_back(groups, incoming, stored, modulation, weights, pairs, bias, earlier, cuts):
     hidden_state, normed, packed, mixed_rows, branch = stored
     gate_grad = jnp.sum(incoming * branch, axis=0)
     branch_grad = (modulation[2] * incoming).astype(bf16)
     window = windows(own_columns(branch_grad), 48)
     mixed_grad = after(out_back(window, weights, 384), earlier)
     weight_grad, normed_grad = self_back(
-        groups, packed, mixed_grad, weights, normed, [(mixed_rows, window)] + pairs, bias
+        groups, packed, mixed_grad, weights, normed, [(mixed_rows, window)] + pairs, bias, cuts
     )
     normed_grad = both_cores(normed_grad)
     normal_rows, inverse_std = normalize(hidden_state)
@@ -749,9 +834,15 @@
     words = jnp.pad(words, ((0, 0), (0, 1), (0, 0)))
     near = lax.axis_index("xl")
     words = jnp.stack([jnp.where(near == 0, words, 0), jnp.where(near == 1, words, 0)])
-    sent = jnp.concatenate([sent, words.reshape(8, 9, 2304)], axis=2)
+    split_steps = jnp.stack([timesteps // 32, timesteps % 32], axis=1).reshape(-1).astype(bf16)
+    note = [spatial_table.reshape(-1), temporal_table.reshape(-1), cross_gain, split_steps]
+    note = jnp.pad(jnp.concatenate(note), (0, 9))[None]
+    note = jnp.concatenate([time_input.reshape(9, 256), jnp.pad(note, ((0, 8), (0, 0)))], axis=1)
+    note = jnp.broadcast_to(note, (8, 9, 384))
+    sent = jnp.concatenate([sent, words.reshape(8, 9, 2304), note], axis=2)
     mine = swap_group(sent, GROUP)
-    words = lax.dynamic_slice_in_dim(mine[:, :8, 2592:], near * 4, 4, 0)
+    note = mine[..., 4896:].reshape(72, 384)
+    words = lax.dynamic_slice_in_dim(mine[:, :8, 2592:4896], near * 4, 4, 0)
     words = words.reshape(4, 8, 4, 576).transpose(0, 2, 1, 3).reshape(128, 576)
     words = widen(words, 640)
     mine = mine[..., :2592].reshape(72, 2592)
@@ -762,69 +853,52 @@
     t_att = widen(mine[:, 1728:2592], 896)
     downs = send_down(shards)
 
-    split_steps = jnp.stack([timesteps // 32, timesteps % 32], axis=1).reshape(-1).astype(bf16)
-    note = jnp.concatenate(
-        [
-            time_input.reshape(-1),
-            spatial_table.reshape(-1),
-            temporal_table.reshape(-1),
-            cross_gain,
-            split_steps,
-            jnp.zeros((9,), bf16),
-        ]
-    )
-    notes = swap_group(jnp.broadcast_to(note, (128, 2432)), ALL)
-    full_time_input = notes[:, :2304].reshape(FREQ, D)
-
     near_words = by_core(words, swap(words, "xl"), "xl", 0)
     rings, first_done = fetch_rings(
         [
-            (jnp.concatenate([s_up, t_att, s_att], axis=1), "y"),
-            (jnp.concatenate([downs[0], downs[1], t_up], axis=1), "z"),
+            (jnp.concatenate([t_up, s_att, downs[1], note], axis=1), "y"),
+            (jnp.concatenate([s_up, t_att, downs[0]], axis=1), "z"),
         ],
         (),
     )
-    up_att, s_att = place(rings[0], "y", 0, (1536, 640))
-    s_down, down_up = place(rings[1], "z", 0, (640, 1280))
-    rings, second_done = fetch_rings(
-        [
-            (up_att, "z"),
-            (jnp.concatenate([s_att, s_down], axis=2), "x"),
-            (down_up, "y"),
-            (near_words, "y"),
-        ],
-        (first_done, full_time_input),
-    )
-    steps = notes[::4, 2421:2423].astype(f32)
+    t_up, att_down, note = place(rings[0], "y", 0, (640, 1280, 384))
+    up_att, s_down = place(rings[1], "z", 0, (1536, 640))
+    across = lax.all_gather(
+        jnp.concatenate([att_down, s_down], axis=2), RING, axis=0, tiled=False
+    )
+    s_att, t_down, s_down = across[..., :640], across[..., 640:1280], across[..., 1280:]
+    up_words = jnp.concatenate([t_up, near_words.reshape(4, 64, 640), widen(note, 640)], axis=1)
+    rings, second_done = gather_rings([(up_att, "y"), (up_words, "z")], first_done)
+    s_up, t_att = place(rings[0], "y", 0, (640, 896))
+    (up_words,) = place(rings[1], "z", 1, (640,))
+    t_up, words = up_words[:, :, :72], jnp.swapaxes(up_words[:, :, 72:136], 0, 1)
+    notes = up_words[:, :, 136:, :384].reshape(16, 8, 9, 384)
+    full_time_input = notes[..., :256].reshape(FREQ, D)
+    notes = notes[:, :, 0, 256:].reshape(128, 128)
+    steps = notes[::4, 117:119].astype(f32)
     steps = (steps[:, 0] * 32.0 + steps[:, 1]).astype(jnp.int32)
     embedded = time_features(steps, FREQ).astype(bf16)
     pre_time = product(embedded, full_time_input)
     lifted = jax.nn.silu(pre_time).astype(bf16)
     own_lifted = lax.dynamic_slice_in_dim(lifted, me * 9, 9, 1)
-    shares = after(product(own_lifted, time_output), first_done)
+    shares = product(own_lifted, time_output)
     shares = swap_group(shares.reshape(128, 1728), ALL)
-    shares, rings = lax.optimization_barrier((shares, rings))
-    s_up, t_att = place(rings[0], "z", 1, (640, 896))
-    s_att, s_down = place(rings[1], "x", 0, (640, 640))
-    t_down, t_up = place(rings[2], "y", 0, (640, 640))
-    (words,) = place(rings[3], "y", 0, (640,))
+    s_up = lax.all_gather(s_up.reshape(D, 640), RING, axis=0, tiled=False)
     t_att = lax.all_gather(t_att.reshape(D, 896), RING, axis=0, tiled=False)
-    words = lax.all_gather(words.reshape(1024, 640), "z", axis=0, tiled=False).reshape(4096, 640)
+    words = lax.all_gather(words.reshape(1024, 640), "y", axis=0, tiled=False).reshape(4096, 640)
     t_up = lax.all_gather(t_up.reshape(D, 640), RING, axis=0, tiled=False)
-    t_down = lax.all_gather(t_down.reshape(D, 640), RING, axis=0, tiled=False)
-    t_down = t_down.reshape(4, 4, 4, 72, 640)
-
-    tables = notes[:, 2304:2412].reshape(128, 12, 9).transpose(1, 0, 2).reshape(2, 6, D)
-    full_gain = notes[:, 2412:2421].reshape(D).astype(f32)
+
+    tables = notes[:, :108].reshape(128, 12, 9).transpose(1, 0, 2).reshape(2, 6, D)
+    full_gain = notes[:, 108:117].reshape(D).astype(f32)
     shared = jnp.sum(shares, axis=0)
     shared = by_core(shared, swap(shared, "c"), "c", 0)
     shared = by_core(shared, swap(shared, "xh"), "xh", 0).reshape(6, D)
-    rings, _ = fetch_rings([(s_att, "z"), (s_down, "y"), (s_up, "x")], (second_done, shared))
+    rings, third_done = gather_rings([(s_att, "z"), (s_down, "y")], second_done)
     (s_att,) = place(rings[0], "z", 2, (640,))
     s_att = s_att.reshape(4, D, 640)
     (s_down,) = place(rings[1], "y", 1, (640,))
-    (s_up,) = place(rings[2], "x", 0, (640,))
-    s_up = s_up.reshape(4, D, 640)
+    rings, _ = gather_rings([(t_down, "z")], third_done)
+    (t_down,) = place(rings[0], "z", 2, (640,))
 
     spatial_mod = tables[0].astype(f32) + shared
     temporal_mod = tables[1].astype(f32) + shared
@@ -854,8 +928,7 @@
     own_cotangent = cotangent[0, 0]
     incoming = to_patches(by_core(own_cotangent, swap(own_cotangent, "c"), "c", 0)).astype(f32)
 
-    text_order = text_states[0].reshape(120, 4, 4, 2, 128).transpose(0, 2, 1, 3, 4)
-    text_order = text_order.reshape(120, 4096)
+    text_order = text_states[0]
     text_rows = product(text_order, words)[:, :576].astype(bf16)
     other_text = swap(text_rows, "xh")
     def text_pieces(value):
@@ -868,17 +941,16 @@
     row = jnp.arange(320) % 80
     patch_bias = jnp.where(row[:, None] == row[None], 0.0, MASK_FILL)
 
-    t_cross = t_att[..., 512:]
     hidden_state = patch_rows.astype(f32)
     hidden_state, temporal_attention = attention_block(
         1, hidden_state, temporal_mod, t_att, patch_bias
     )
     cross_state = hidden_state
     cross_normed, cross_queries, cross_mixed = cross_forward(
-        cross_state, full_gain, t_cross, text_keys, text_values, text_bias
+        cross_state, full_gain, t_att, text_keys, text_values, text_bias
     )
     cross_mixed = apart(cross_mixed)
-    hidden_state = cross_state + apart(out_forward(cross_mixed, t_cross, 208)).astype(f32)
+    hidden_state = cross_state + apart(out_forward(cross_mixed, t_att, 720)).astype(f32)
     hidden_state, temporal_mlp = feed_block(hidden_state, temporal_mod, t_up, t_down)
 
     finished = hidden_state.astype(bf16).reshape(4, 80, D)
@@ -889,13 +961,13 @@
     incoming, t_up_grad, t_down_grad, t_mlp_mod = feed_block_back(
         incoming, temporal_mlp, temporal_mod, t_up, t_down
     )
-    t_up_grad = scatter_ring(t_up_grad).reshape(4, 4, 72, 640)
-    t_down_grad = scatter_ring(t_down_grad.reshape(4, D, 640)).reshape(4, 4, 72, 640)
+    t_up_grad = scatter_ring(t_up_grad)
+    t_down_grad = scatter_ring(t_down_grad.reshape(4, D, 640))
     cross_grad = incoming.astype(bf16)
     out_window = windows(own_columns(cross_grad), 80)
-    cross_mixed_grad = out_back(out_window, t_cross, 128)
+    cross_mixed_grad = out_back(out_window, t_att, 640)
     query_window, key_grad, value_grad, normed_grad = cross_back(
-        cross_queries, text_keys, text_values, cross_mixed_grad, t_cross, text_bias
+        cross_queries, text_keys, text_values, cross_mixed_grad, t_att, text_bias
     )
     normed_grad = both_cores(normed_grad)
     normal_rows, inverse_std = normalize(cross_state)
@@ -911,17 +983,7 @@
         return jnp.concatenate([half(key_grad), half(value_grad)], axis=1)
 
     text_grad = text_half(far).astype(f32) + swap(text_half(1 - far), "xh").astype(f32)
-    words_grad = outer_sum(text_order, widen(text_grad.astype(bf16), 640)).astype(bf16)
-    words_grad = words_grad.reshape(4, 1024, 640)
-    words_grad = lax.psum_scatter(words_grad, "z", scatter_dimension=0, tiled=False)
-    words_grad = words_grad.reshape(4, 256, 640)
-    words_grad = lax.psum_scatter(words_grad, "y", scatter_dimension=0, tiled=False)
-    words_grad = words_grad.reshape(2, 128, 640)
-    words_grad = lax.dynamic_index_in_dim(words_grad, near, 0, keepdims=False).astype(f32) + swap(
-        lax.dynamic_index_in_dim(words_grad, 1 - near, 0, keepdims=False), "xl"
-    ).astype(f32)
-    words_grad = words_grad.astype(bf16)
-
+    words_grad = words_back(text_order, widen(text_grad.astype(bf16), 640))
     incoming, t_att_grad, t_att_mod = attention_block_back(
         1,
         incoming,
@@ -930,61 +992,64 @@
         t_att,
         [(cross_normed, query_window), (cross_mixed, out_window)],
         patch_bias,
-        text_grad,
+        (text_grad, t_up_grad),
+        (896,),
     )
     t_mod_grad = jnp.stack(t_att_mod + t_mlp_mod)
 
     back = incoming.astype(bf16).reshape(4, 80, D)
     theirs = swap(back[2:], "xh")
-    t_att_grad = scatter_ring(t_att_grad).reshape(4, 4, 72, 896)
+    t_att_grad = scatter_ring(tie(t_att_grad[0], t_down_grad))
 
 
     frame_grad = by_core(back[:2], theirs, "xh", 1).reshape(320, D).astype(f32)
+    words_grad = tie(words_grad, t_att_grad).reshape(4, 1024, 640)
+    words_grad = lax.psum_scatter(words_grad, "y", scatter_dimension=0, tiled=False)
+    words_grad = words_grad.reshape(4, 256, 640)
+    words_grad = lax.psum_scatter(words_grad, "z", scatter_dimension=0, tiled=False)
+    words_grad = words_grad.reshape(2, 128, 640)
+    words_grad = lax.dynamic_index_in_dim(words_grad, near, 0, keepdims=False).astype(f32) + swap(
+        lax.dynamic_index_in_dim(words_grad, 1 - near, 0, keepdims=False), "xl"
+    ).astype(f32)
+    words_grad = words_grad.astype(bf16)
     frame_grad, s_up_grad, s_down_grad, s_mlp_mod = feed_block_back(
         frame_grad, spatial_mlp, spatial_mod, s_up, s_down
     )
     s_up_grad = s_up_grad.reshape(4, 4, 4, 72, 640)
-    (s_up_grad, s_down_grad), s_done = sum_rings(
-        [(s_up_grad, "z", 2), (s_down_grad, "y", 1)], ()
+    (s_up_grad, s_down_grad), s_done, _ = scatter_rings(
+        [([(s_up_grad, 2)], "z"), ([(s_down_grad, 1)], "y")], ()
     )
     frame_grad, s_att_grad, s_att_mod = attention_block_back(
-        2, frame_grad, spatial_attention, spatial_mod, s_att, [], None, s_done
-    )
+        2, frame_grad, spatial_attention, spatial_mod, s_att, [], None, (s_done, t_down_grad), (384, 256)
+    )
+    t_up_grad = tie(t_up_grad, s_att_grad[0])
+    t_grads = jnp.concatenate([t_up_grad, t_att_grad, t_down_grad], axis=1)
+    t_grads = t_grads.reshape(4, 288, 2176)
+    t_grads = lax.psum_scatter(t_grads, "y", scatter_dimension=0, tiled=False)
+    t_grads = t_grads.reshape(4, 72, 2176)
+    t_grads = lax.psum_scatter(t_grads, "z", scatter_dimension=0, tiled=False)
     latent_grad = signal_scale * lax.dynamic_index_in_dim(frame_grad.reshape(2, 160, D), core, 0)
     s_mod_grad = jnp.stack(s_att_mod + s_mlp_mod)
-    s_att_grad = s_att_grad.reshape(4, 4, 4, 72, 640)
-    (att_x_y, att_x_z, att_y_z), done = sum_rings(
-        [
-            (s_att_grad[..., :256], "z", 2),
-            (s_att_grad[..., 256:512], "y", 1),
-            (s_att_grad[..., 512:], "x", 0),
-        ],
-        (),
-    )
-    up_att = jnp.concatenate([t_up_grad, t_att_grad], axis=3)
-    down_att = jnp.concatenate([t_down_grad, att_y_z], axis=3)
-    up_x_y = jnp.concatenate([s_up_grad, att_x_y], axis=3)
-    down_x_z = jnp.concatenate([s_down_grad, att_x_z], axis=3)
-    (up_att, down_att, up_x_y, down_x_z), done = sum_rings(
-        [(up_att, "z", 1), (down_att, "y", 0), (up_x_y, "y", 1), (down_x_z, "x", 0)], done
-    )
-    down = jnp.concatenate([down_att, down_x_z], axis=2)
-    (up_att, down, up_x), done = sum_rings(
-        [(up_att, "y", 0), (down, "z", 0), (up_x_y, "x", 0)], done
-    )
-    downs = return_down(jnp.stack([down[:, 768:1408], down[:, :640]])).astype(f32)
+    s_att_grad = [grad.reshape(4, 4, 4, 72, -1) for grad in s_att_grad]
+    (att_x_y, att_x_z), _, done = scatter_rings(
+        [([(s_att_grad[0], 2)], "z"), ([(s_att_grad[1], 1)], "y")], ()
+    )
+    (up, down), done = sum_rings(
+        [([(s_up_grad, 1), (att_x_y, 1)], "y"), ([(s_down_grad, 0), (att_x_z, 0)], "x")], done
+    )
+    (up, down), done = sum_rings([([(up, 0)], "x"), ([(down, 0)], "z")], done)
+    downs = return_down(jnp.stack([down[:, :640], t_grads[:, 1536:]])).astype(f32)
     s_down_done, t_down_done = downs[0], downs[1]
     words_grad = swap_group(words_grad[:, :576].reshape(4, 32, 576), SEQ)
     words_grad = words_grad.reshape(2, 2, 32, 2, 288).transpose(2, 3, 1, 0, 4).reshape(32, 2304)
 
     returned = jnp.concatenate(
         [
-            up_x[:, :576],
-            up_x[:, 640:],
-            down[:, 1408:],
-            down[:, 640:704],
-            up_att[:, :576],
-            up_att[:, 640:1504],
+            up[:, :576],
+            up[:, 640:],
+            down[:, 640:832],
+            t_grads[:, :576],
+            t_grads[:, 640:1504],
         ],
         axis=1,
     )

time: 1160 us -> 1020 us (0.88)
  starting transfers between devices: 224 us -> 146 us
  waiting for transfers between devices: 338 us -> 301 us
  local copies, waits for them, and re-layouts: 243 us -> 218 us
    ppermute x15 -> x6, waiting for transfers between devices: 53.8 us -> 0.26 us  [fetch(): return lax.ppermute(value, ('xl', 'xh'), pairs)]
    concatenate x3 -> x22, other arithmetic: 0.11 us -> 24.2 us  [the longest x1 5.57 us: local(): t_grads = jnp.concatenate([t_up_grad, t_att_grad, t_down_grad], axis=1)]
    ppermute x29, starting transfers between devices: 42.8 us -> 19 us  [swap(): return lax.ppermute(value, axis, [(0, 1), (1, 0)])]
    ppermute x15 -> x6, starting transfers between devices: 30.3 us -> 6.93 us  [fetch(): return lax.ppermute(value, ('xl', 'xh'), pairs)]
    all_to_all x7 -> x6, starting transfers between devices: 59 us -> 37.2 us  [swap_group(): return lax.all_to_all(value, axes, split_axis=0, concat_axis=0, tiled=True)]
    all_to_all x7 -> x6, waiting for transfers between devices: 55.4 us -> 36.2 us  [swap_group(): return lax.all_to_all(value, axes, split_axis=0, concat_axis=0, tiled=True)]
    all_gather x2 -> x3, waiting for transfers between devices: 0.02 us -> 17.6 us  [the longest x1 17.6 us: local(): lax.all_gather(words.reshape(1024, 640), 'y', axis=0, tiled=False)]
    slice x15 -> x38, local copies, waits for them, and re-layouts: 14.9 us -> 30 us  [the longest x5 6.25 us: gather_rings(): up[:h]]
  transfers between devices with their start and end apart: 112 -> 105, of which waited for: 38 -> 40; matrix products, arithmetic and copies ran while one was open for 23% -> 27% of each run, Pallas kernels for 12% -> 16%
where the time goes in v3:
time: 1020 us; the launch traced here: 1000 us
  waiting for transfers between devices  301 us (30%)
  local copies, waits for them, and re-layouts  218 us (21%)
  Pallas kernels  189 us (19%)
  starting transfers between devices  146 us (14%)
  other arithmetic  121 us (12%)
  between operations  20.2 us (2%)
    ppermute x48, waiting for transfers between devices, fetch(): return lax.ppermute(value, axis, [((i + step) % 4, i) for i in range(4)])  192 us
    pallas_call x16, Pallas kernels, by_piece(): pl.pallas_call(kernel, out_shape=out_shape, grid=(4,), in_specs=in_specs,...  167 us
    ppermute x48, starting transfers between devices, fetch(): return lax.ppermute(value, axis, [((i + step) % 4, i) for i in range(4)])  71.3 us
    unnamed x293, local copies, waits for them, and re-layouts  55.9 us
    ppermute x29, waiting for transfers between devices, swap(): return lax.ppermute(value, axis, [(0, 1), (1, 0)])  45.6 us
    all_to_all x6, starting transfers between devices, swap_group(): return lax.all_to_all(value, axes, split_axis=0, concat_axis=0, tiled=True)  37.2 us
    all_to_all x6, waiting for transfers between devices, swap_group(): return lax.all_to_all(value, axes, split_axis=0, concat_axis=0, tiled=True)  36.2 us
  transfers between devices with their start and end apart: 105, of which 40 were waited for; matrix products, arithmetic and copies ran while one was open for 27% of the time, Pallas kernels for 16%

profile of v3, /device:TPU:0, one launch (start us, length us, event | category | flops | bytes accessed | tf_op | source)
XLA Modules:
  0.0 1004.1 jit_solution(18352800330225563296)
XLA Ops:
  31.3 14.5 %all-to-all-done = bf16[8,9,5280]{2,1,0:T(8,128)(2,1)S(1)} async-done(((bf16[8,9,5280]{2,1,0:T(8,128)(2,1)}), bf16[8,9,5280]{2,1,0:T(8,128)(2,1)S(1)}, u32[]{:S(2)}, u32[]{:S(2)}) %all-to-all-start) | async-done | bytes 760352 | tf_op jit(solution)/shard_map/all_to_all | solution.py:265
  50.1 8.1 collective-permute-start.3
  61.4 15.2 %collective-permute-done.7 = bf16[72,2176]{1,0:T(8,128)(2,1)S(1)} collective-permute-done((bf16[72,2176]{1,0:T(8,128)(2,1)S(1)}, bf16[72,2176]{1,0:T(8,128)(2,1)S(1)}, u32[]{:S(2)}, u32[]{:S(2)}) %collective-permute-start.7) | collective-permute-done | bytes 313376 | tf_op jit(solution)/shard_map/ppermute | solution.py:35
  90.7 16.1 %collective-permute-done.10 = bf16[4,72,1536]{2,1,0:T(8,128)(2,1)S(1)} collective-permute-done((bf16[4,72,1536]{2,1,0:T(8,128)(2,1)S(1)}, bf16[4,72,1536]{2,1,0:T(8,128)(2,1)S(1)}, u32[]{:S(2)}, u32[]{:S(2)}) %collective-permute-start.10) | collective-permute-done | bytes 884768 | tf_op jit(solution)/shard_map/ppermute | solution.py:35
  164.2 10.7 %all-to-all-done.1 = f32[128,1,1728]{2,1,0:T(1,128)S(1)} async-done(((f32[128,1,1728]{2,1,0:T(1,128)}), f32[128,1,1728]{2,1,0:T(1,128)S(1)}, u32[]{:S(2)}, u32[]{:S(2)}) %all-to-all-start.1) | async-done | bytes 884768 | tf_op jit(solution)/shard_map/all_to_all | solution.py:265
  184.5 9.1 collective-permute-done.20.refs_1_
  240.3 10.8 %shard_map.353 = (bf16[320,1152]{1,0:T(8,128)(2,1)S(1)}, bf16[4,320,640]{2,1,0:T(8,128)(2,1)S(1)}, bf16[4,320,144]{2,1,0:T(8,128)(2,1)S(1)}) custom-call(f32[320,1152]{1,0:T(8,128)S(1)} %get-tuple-element.369.x_ref, f32[1,1152]{1,0:T(1,128)S(1)} %get-tuple-element.540.shift_ref, f32[1,1152]{1,0:T(1,128)S(1)} %get-tuple-element.539.scale_ref, ...), custom_call_target="tpu_custom_call" | custom-call | tf_op jit(solution)/shard_map/pallas_call | solution.py:358
  282.9 10.6 %shard_map.357 = (bf16[320,1152]{1,0:T(8,128)(2,1)S(1)}, f32[4,320,640]{2,1,0:T(8,128)}, bf16[4,320,576]{2,1,0:T(8,128)(2,1)S(1)}, bf16[320,1152]{1,0:T(8,128)(2,1)S(1)}) custom-call(f32[320,1152]{1,0:T(8,128)S(1)} %get-tuple-element.332.x_ref, f32[1,1152]{1,0:T(1,128)S(1)} %get-tuple-element.534.shift_ref, f32[1,1152]{1,0:T(1,128)S(1)} %get-tuple-element.533.scale_ref, ...), custom_call_target="tpu_custom_call" | custom-call | tf_op jit(solution)/shard_map/pallas_call | solution.py:358
  313.1 9.3 shard_map.358
  326.8 17.6 %all-gather.11.cloned.1.call-done = bf16[4,1024,640]{2,1,0:T(8,128)(2,1)} async-done(((bf16[1,1024,640]{2,1,0:T(8,128)(2,1)}), bf16[4,1024,640]{2,1,0:T(8,128)(2,1)}) %all-gather.11.cloned.1.call-update) | async-done | bytes 5242896 | tf_op jit(solution)/shard_map/all_gather | solution.py:888
  378.3 7.8 shard_map.360
  450.8 10.7 %shard_map.363 = (bf16[320,1152]{1,0:T(8,128)(2,1)S(1)}, f32[4,320,640]{2,1,0:T(8,128)}, bf16[4,320,576]{2,1,0:T(8,128)(2,1)S(1)}, bf16[320,1152]{1,0:T(8,128)(2,1)S(1)}) custom-call(f32[320,1152]{1,0:T(8,128)S(1)} %copy-done.5, f32[1,1152]{1,0:T(1,128)S(1)} %get-tuple-element.522.shift_ref, f32[1,1152]{1,0:T(1,128)S(1)} %get-tuple-element.521.scale_ref, ...), custom_call_target="tpu_custom_call" | custom-call | tf_op jit(solution)/shard_map/pallas_call | solution.py:358
  461.5 17.8 %shard_map.364 = (bf16[4,1152,640]{2,1,0:T(8,128)(2,1)}, bf16[4,4,4,72,640]{4,3,2,1,0:T(8,128)(2,1)}, bf16[320,1152]{1,0:T(8,128)(2,1)S(1)}) custom-call(bf16[320,1152]{1,0:T(8,128)(2,1)S(1)} %copy-done.31, f32[4,320,640]{2,1,0:T(8,128)} %get-tuple-element.213.inner_ref, bf16[4,320,576]{2,1,0:T(8,128)(2,1)S(1)} %get-tuple-element.214.active_ref, ...), custom_call_target="tpu_custom_call" | custom-call | tf_op jit(solution)/shard_map/pallas_call | solution.py:358
  525.3 9.6 shard_map.366
  574.2 21.3 %shard_map.368 = (bf16[4,1152,896]{2,1,0:T(8,128)(2,1)}, bf16[320,1152]{1,0:T(8,128)(2,1)S(1)}) custom-call(bf16[4,320,640]{2,1,0:T(8,128)(2,1)} %copy-done.45, bf16[4,320,144]{2,1,0:T(8,128)(2,1)S(1)} %copy-done.32, bf16[4,1152,896]{2,1,0:T(8,128)(2,1)} %all-gather.9.cloned.1.call-done.weight_ref.refs_2_, bf16[320,1152]{1,0:T(8,128)(2,1)S(1)} %copy-done.55, ...), custom_call_target="tpu_custom_call" | custom-call | tf_op jit(solution)/shard_map/pallas_call | solution.py:358
  613.8 18.1 %collective-permute-done.51 = bf16[2,80,1152]{2,1,0:T(8,128)(2,1)S(1)} collective-permute-done((bf16[2,80,1152]{2,1,0:T(8,128)(2,1)S(1)}, bf16[2,80,1152]{2,1,0:T(8,128)(2,1)S(1)}, u32[]{:S(2)}, u32[]{:S(2)}) %collective-permute-start.51) | collective-permute-done | bytes 368672 | tf_op jit(solution)/shard_map/ppermute | solution.py:39
  633.6 17.6 %shard_map.369 = (bf16[4,1152,640]{2,1,0:T(8,128)(2,1)}, bf16[4,4,4,72,640]{4,3,2,1,0:T(8,128)(2,1)}, bf16[320,1152]{1,0:T(8,128)(2,1)S(1)}) custom-call(bf16[320,1152]{1,0:T(8,128)(2,1)S(1)} %fusion.13.grad_ref, f32[4,320,640]{2,1,0:T(8,128)} %get-tuple-element.228.inner_ref, bf16[4,320,576]{2,1,0:T(8,128)(2,1)S(1)} %copy-done.44, ...), custom_call_target="tpu_custom_call" | custom-call | tf_op jit(solution)/shard_map/pallas_call | solution.py:358
  687.1 20.0 %shard_map.371 = (bf16[4,1152,384]{2,1,0:T(8,128)(2,1)}, bf16[4,1152,256]{2,1,0:T(8,128)(2,1)}, bf16[320,1152]{1,0:T(8,128)(2,1)S(1)}) custom-call(bf16[4,320,640]{2,1,0:T(8,128)(2,1)S(1)} %copy-done.42, bf16[4,320,144]{2,1,0:T(8,128)(2,1)S(1)} %fusion.20.refs_1_, bf16[4,1152,640]{2,1,0:T(8,128)(2,1)} %bitcast.553, bf16[320,1152]{1,0:T(8,128)(2,1)S(1)} %copy-done.51, ...), custom_call_target="tpu_custom_call" | custom-call | tf_op jit(solution)/shard_map/pallas_call | solution.py:358
  751.3 13.1 %collective-permute-done.66 = bf16[2,4,72,256]{3,2,1,0:T(8,128)(2,1)S(1)} collective-permute-done((bf16[2,4,72,256]{3,2,1,0:T(8,128)(2,1)S(1)}, bf16[2,4,72,256]{3,2,1,0:T(8,128)(2,1)S(1)}, u32[]{:S(2)}, u32[]{:S(2)}) %collective-permute-start.66) | collective-permute-done | bytes 294944 | tf_op jit(solution)/shard_map/ppermute | solution.py:35
  765.3 20.8 %collective-permute-done.64 = bf16[2,4,72,384]{3,2,1,0:T(8,128)(2,1)S(1)} collective-permute-done((bf16[2,4,72,384]{3,2,1,0:T(8,128)(2,1)S(1)}, bf16[2,4,72,384]{3,2,1,0:T(8,128)(2,1)S(1)}, u32[]{:S(2)}, u32[]{:S(2)}) %collective-permute-start.64) | collective-permute-done | bytes 442400 | tf_op jit(solution)/shard_map/ppermute | solution.py:35
  821.9 39.2 %collective-permute-done.63 = bf16[4,4,72,640]{3,2,1,0:T(8,128)(2,1)} collective-permute-done((bf16[4,4,72,640]{3,2,1,0:T(8,128)(2,1)}, bf16[4,4,72,640]{3,2,1,0:T(8,128)(2,1)}, u32[]{:S(2)}, u32[]{:S(2)}) %collective-permute-start.63) | collective-permute-done | bytes 1474592 | tf_op jit(solution)/shard_map/ppermute | solution.py:35
  867.9 15.3 %collective-permute-done.71 = bf16[4,4,72,256]{3,2,1,0:T(8,128)(2,1)S(1)} collective-permute-done((bf16[4,4,72,256]{3,2,1,0:T(8,128)(2,1)S(1)}, bf16[4,4,72,256]{3,2,1,0:T(8,128)(2,1)S(1)}, u32[]{:S(2)}, u32[]{:S(2)}) %collective-permute-start.71) | collective-permute-done | bytes 589856 | tf_op jit(solution)/shard_map/ppermute | solution.py:35
  908.6 9.6 all-to-all-start.3
  964.8 11.0 %all-to-all-done.4 = bf16[8,9,2592]{2,1,0:T(8,128)(2,1)S(1)} async-done(((bf16[8,9,2592]{2,1,0:T(8,128)(2,1)}), bf16[8,9,2592]{2,1,0:T(8,128)(2,1)S(1)}, u32[]{:S(2)}, u32[]{:S(2)}) %all-to-all-start.4) | async-done | bytes 373280 | tf_op jit(solution)/shard_map/all_to_all | solution.py:265
  (917 shorter events, 629.9 us)
Async XLA Ops:
  21.8 126.8 %all-gather.15.cloned.1.call-start = ((), (), s32[]{:S(2)}) async-start(), calls=%async_computation.23 | async-start | bytes 5529600 | tf_op jit(solution)/shard_map/all_gather | solution.py:866
  79.1 203.8 %all-gather.7.cloned.1.call-start = ((), (), s32[]{:S(2)}) async-start(), calls=%async_computation.13 | async-start | bytes 7372800 | tf_op jit(solution)/shard_map/all_gather | solution.py:886
  128.9 182.8 %all-gather.9.cloned.1.call-start = ((), (), s32[]{:S(2)}) async-start(), calls=%async_computation.14 | async-start | bytes 10321920 | tf_op jit(solution)/shard_map/all_gather | solution.py:887
  129.7 214.7 %all-gather.11.cloned.1.call-start = ((), (), s32[]{:S(2)}) async-start(), calls=%async_computation.15 | async-start | bytes 6553600 | tf_op jit(solution)/shard_map/all_gather | solution.py:888
  148.5 300.9 %all-gather.13.cloned.1.call-start = ((), (), s32[]{:S(2)}) async-start(), calls=%async_computation.16 | async-start | bytes 7372800 | tf_op jit(solution)/shard_map/all_gather | solution.py:889
  193.7 101.1 %collective-permute-start.43 = (bf16[160,1152]{1,0:T(8,128)(2,1)}, bf16[160,1152]{1,0:T(8,128)(2,1)}, u32[]{:S(2)}, u32[]{:S(2)}) collective-permute-start(bf16[160,1152]{1,0:T(8,128)(2,1)} %bitcast.137), channel_id=1, source_target_pairs={{0,1},{1,0},{2,3},{3,2},{4,5},{5,4},{6,7},{7,6},{8,9},{9,8},{10,11... | collective-permute-start | bytes 1105928 | tf_op jit(solution)/shard_map/ppermute | solution.py:39
  271.7 295.9 %reduce-scatter.10.cloned.1.call-start = ((), (), s32[]{:S(2)}) async-start(), calls=%async_computation.17 | async-start | bytes 7372800 | tf_op jit(solution)/shard_map/reduce_scatter | solution.py:784
  301.0 90.0 %collective-permute-start.44 = (bf16[2,80,1152]{2,1,0:T(8,128)(2,1)}, bf16[2,80,1152]{2,1,0:T(8,128)(2,1)}, u32[]{:S(2)}, u32[]{:S(2)}) collective-permute-start(bf16[2,80,1152]{2,1,0:T(8,128)(2,1)} %get-tuple-element.406), channel_id=1, source_target_pairs={{0,2},{2,0},{1,3},{3,1},{4,6},{6,4},{5,7},{7,5},{8,10},{10,8},{9,1... | collective-permute-start | bytes 1105928 | tf_op jit(solution)/shard_map/ppermute | solution.py:39
  480.3 121.8 %reduce-scatter.12.cloned.1.call-start = ((), (), s32[]{:S(2)}) async-start(), calls=%async_computation.18 | async-start | bytes 7372800 | tf_op jit(solution)/shard_map/reduce_scatter | solution.py:784
  481.0 226.2 %reduce-scatter.14.cloned.1.call-start = ((), (), s32[]{:S(2)}) async-start(), calls=%async_computation.19 | async-start | bytes 10321920 | tf_op jit(solution)/shard_map/reduce_scatter | solution.py:784
  602.1 292.1 %reduce-scatter.16.cloned.1.call-start = ((), (), s32[]{:S(2)}) async-start(), calls=%async_computation.20 | async-start | bytes 6266880 | tf_op jit(solution)/shard_map/reduce_scatter | solution.py:1028
  712.8 230.5 %reduce-scatter.18.cloned.1.call-start = ((), (), s32[]{:S(2)}) async-start(), calls=%async_computation.21 | async-start | bytes 6553600 | tf_op jit(solution)/shard_map/reduce_scatter | solution.py:1007
  742.8 72.9 %collective-permute-start.60 = (bf16[4,4,72,640]{3,2,1,0:T(8,128)(2,1)}, bf16[4,4,72,640]{3,2,1,0:T(8,128)(2,1)}, u32[]{:S(2)}, u32[]{:S(2)}) collective-permute-start(bf16[4,4,72,640]{3,2,1,0:T(8,128)(2,1)} %pad_maximum_fusion.4), channel_id=1, source_target_pairs={{24,0},{0,8},{8,16},{16,24},{25,1},{1,9},{9,17},{17,25},{26,2},{2,... | collective-permute-start | bytes 4423688 | tf_op jit(solution)/shard_map/ppermute | solution.py:35
  744.6 43.9 %collective-permute-start.65 = (bf16[2,4,72,384]{3,2,1,0:T(8,128)(2,1)S(1)}, bf16[2,4,72,384]{3,2,1,0:T(8,128)(2,1)S(1)}, u32[]{:S(2)}, u32[]{:S(2)}) collective-permute-start(bf16[2,4,72,384]{3,2,1,0:T(8,128)(2,1)S(1)} %get-tuple-element.398), channel_id=1, source_target_pairs={{8,0},{16,8},{24,16},{0,24},{9,1},{17,9},{25,17},{1,25},{10,2},{18... | collective-permute-start | bytes 1327112 | tf_op jit(solution)/shard_map/ppermute | solution.py:35
  764.4 54.1 %collective-permute-start.61 = (bf16[4,4,72,640]{3,2,1,0:T(8,128)(2,1)}, bf16[4,4,72,640]{3,2,1,0:T(8,128)(2,1)}, u32[]{:S(2)}, u32[]{:S(2)}) collective-permute-start(bf16[4,4,72,640]{3,2,1,0:T(8,128)(2,1)} %pad_maximum_fusion.5), channel_id=1, source_target_pairs={{8,0},{16,8},{24,16},{0,24},{9,1},{17,9},{25,17},{1,25},{10,2},{18... | collective-permute-start | bytes 4423688 | tf_op jit(solution)/shard_map/ppermute | solution.py:35
  765.0 55.0 %collective-permute-start.62 = (bf16[4,4,72,640]{3,2,1,0:T(8,128)(2,1)}, bf16[4,4,72,640]{3,2,1,0:T(8,128)(2,1)}, u32[]{:S(2)}, u32[]{:S(2)}) collective-permute-start(bf16[4,4,72,640]{3,2,1,0:T(8,128)(2,1)} %pad_maximum_fusion.6), channel_id=1, source_target_pairs={{96,0},{0,32},{32,64},{64,96},{97,1},{1,33},{33,65},{65,97},{98,2}... | collective-permute-start | bytes 4423688 | tf_op jit(solution)/shard_map/ppermute | solution.py:35
  786.1 75.1 %collective-permute-start.63 = (bf16[4,4,72,640]{3,2,1,0:T(8,128)(2,1)}, bf16[4,4,72,640]{3,2,1,0:T(8,128)(2,1)}, u32[]{:S(2)}, u32[]{:S(2)}) collective-permute-start(bf16[4,4,72,640]{3,2,1,0:T(8,128)(2,1)} %pad_maximum_fusion.7), channel_id=1, source_target_pairs={{32,0},{64,32},{96,64},{0,96},{33,1},{65,33},{97,65},{1,97},{34,2}... | collective-permute-start | bytes 4423688 | tf_op jit(solution)/shard_map/ppermute | solution.py:35
  802.2 81.0 %collective-permute-start.68 = (bf16[4,4,72,384]{3,2,1,0:T(8,128)(2,1)}, bf16[4,4,72,384]{3,2,1,0:T(8,128)(2,1)}, u32[]{:S(2)}, u32[]{:S(2)}) collective-permute-start(bf16[4,4,72,384]{3,2,1,0:T(8,128)(2,1)} %pad_maximum_fusion.9), channel_id=1, source_target_pairs={{24,0},{0,8},{8,16},{16,24},{25,1},{1,9},{9,17},{17,25},{26,2},{2,... | collective-permute-start | bytes 2654216 | tf_op jit(solution)/shard_map/ppermute | solution.py:35
  808.4 95.6 %all-to-all-start.2 = ((f32[128,1,1920]{2,1,0:T(1,128)}), f32[128,1,1920]{2,1,0:T(1,128)}, u32[]{:S(2)}, u32[]{:S(2)}) async-start(f32[128,1,1920]{2,1,0:T(1,128)} %all_to_all.32), calls=%async_computation.4 | async-start | bytes 1966080 | tf_op jit(solution)/shard_map/all_to_all | solution.py:265
  815.6 135.6 %reduce-scatter.22.cloned.1.call-start = ((), (), s32[]{:S(2)}) async-start(), calls=%async_computation.24 | async-start | bytes 1566720
  815.7 67.5 %collective-permute-start.69 = (bf16[4,4,72,384]{3,2,1,0:T(8,128)(2,1)}, bf16[4,4,72,384]{3,2,1,0:T(8,128)(2,1)S(1)}, u32[]{:S(2)}, u32[]{:S(2)}) collective-permute-start(bf16[4,4,72,384]{3,2,1,0:T(8,128)(2,1)} %pad_maximum_fusion.10), channel_id=1, source_target_pairs={{8,0},{16,8},{24,16},{0,24},{9,1},{17,9},{25,17},{1,25},{10,2},{18... | collective-permute-start | bytes 2654216 | tf_op jit(solution)/shard_map/ppermute | solution.py:35
  818.5 49.4 %collective-permute-start.70 = (bf16[4,4,72,256]{3,2,1,0:T(8,128)(2,1)}, bf16[4,4,72,256]{3,2,1,0:T(8,128)(2,1)S(1)}, u32[]{:S(2)}, u32[]{:S(2)}) collective-permute-start(bf16[4,4,72,256]{3,2,1,0:T(8,128)(2,1)} %pad_maximum_fusion.17), channel_id=1, source_target_pairs={{96,0},{0,32},{32,64},{64,96},{97,1},{1,33},{33,65},{65,97},{98,2}... | collective-permute-start | bytes 1769480 | tf_op jit(solution)/shard_map/ppermute | solution.py:35
  820.0 63.2 %collective-permute-start.71 = (bf16[4,4,72,256]{3,2,1,0:T(8,128)(2,1)S(1)}, bf16[4,4,72,256]{3,2,1,0:T(8,128)(2,1)S(1)}, u32[]{:S(2)}, u32[]{:S(2)}) collective-permute-start(bf16[4,4,72,256]{3,2,1,0:T(8,128)(2,1)S(1)} %copy-done.93), channel_id=1, source_target_pairs={{32,0},{64,32},{96,64},{0,96},{33,1},{65,33},{97,65},{1,97},{34,2}... | collective-permute-start | bytes 1769480 | tf_op jit(solution)/shard_map/ppermute | solution.py:35
  918.2 57.6 %reduce-scatter.20.cloned.1.call-start = ((), (), s32[]{:S(2)}) async-start(), calls=%async_computation.22 | async-start | bytes 1638400 | tf_op jit(solution)/shard_map/reduce_scatter | solution.py:1009
  (224 other events, 2117.3 us)
Sparse Core Ops, SparseCore 0:
  79.2 46.6 all-gather.14
  129.1 71.4 all-gather.6
  202.3 82.6 all-gather.8
  286.4 57.9 all-gather.10
  345.9 62.8 all-gather.12
  480.4 57.9 reduce-scatter.9
  540.8 61.2 reduce-scatter.11
  604.5 86.2 reduce-scatter.13
  712.9 59.1 reduce-scatter.15
  774.4 107.2 reduce-scatter.17
  894.3 23.0 reduce-scatter.21
  943.5 26.3 reduce-scatter.19

commit v4 on v3

--- a/solution.py
+++ b/solution.py
@@ -928,8 +928,15 @@
     own_cotangent = cotangent[0, 0]
     incoming = to_patches(by_core(own_cotangent, swap(own_cotangent, "c"), "c", 0)).astype(f32)
 
+    row = jnp.arange(320) % 80
+    patch_bias = jnp.where(row[:, None] == row[None], 0.0, MASK_FILL)
+
+    hidden_state = patch_rows.astype(f32)
+    hidden_state, temporal_attention = attention_block(
+        1, hidden_state, temporal_mod, t_att, patch_bias
+    )
     text_order = text_states[0]
-    text_rows = product(text_order, words)[:, :576].astype(bf16)
+    text_rows = product(text_order, tie(words, temporal_attention[3]))[:, :576].astype(bf16)
     other_text = swap(text_rows, "xh")
     def text_pieces(value):
         pieces = jnp.swapaxes(value.reshape(120, 4, 144), 0, 1)
@@ -938,13 +945,6 @@
     text_keys = text_pieces(by_core(text_rows[:, :288], other_text[:, :288], "xh", 1))
     text_values = text_pieces(by_core(text_rows[:, 288:], other_text[:, 288:], "xh", 1))
     text_bias = jnp.where(jnp.arange(128) < text_lengths[0], 0.0, MASK_FILL)[None]
-    row = jnp.arange(320) % 80
-    patch_bias = jnp.where(row[:, None] == row[None], 0.0, MASK_FILL)
-
-    hidden_state = patch_rows.astype(f32)
-    hidden_state, temporal_attention = attention_block(
-        1, hidden_state, temporal_mod, t_att, patch_bias
-    )
     cross_state = hidden_state
     cross_normed, cross_queries, cross_mixed = cross_forward(
         cross_state, full_gain, t_att, text_keys, text_values, text_bias

time: 1020 us -> 1010 us (level)
  waiting for transfers between devices: 301 us -> 287 us
    ppermute x48, waiting for transfers between devices: 192 us -> 179 us  [fetch(): return lax.ppermute(value, axis, [((i + step) % 4, i) for i in range(4)])]
    unnamed x293 -> x295, local copies, waits for them, and re-layouts: 55.9 us -> 54.9 us
  transfers between devices with their start and end apart: 105 -> 105, of which waited for: 40 -> 38; matrix products, arithmetic and copies ran while one was open for 27% -> 28% of each run, Pallas kernels for 16% -> 16%
where the time goes in v4:
time: 1010 us; the launch traced here: 992 us
  waiting for transfers between devices  287 us (28%)
  local copies, waits for them, and re-layouts  220 us (22%)
  Pallas kernels  189 us (19%)
  starting transfers between devices  146 us (14%)
  other arithmetic  122 us (12%)
  between operations  20.2 us (2%)
    ppermute x48, waiting for transfers between devices, fetch(): return lax.ppermute(value, axis, [((i + step) % 4, i) for i in range(4)])  179 us
    pallas_call x16, Pallas kernels, by_piece(): pl.pallas_call(kernel, out_shape=out_shape, grid=(4,), in_specs=in_specs,...  167 us
    ppermute x48, starting transfers between devices, fetch(): return lax.ppermute(value, axis, [((i + step) % 4, i) for i in range(4)])  71 us
    unnamed x295, local copies, waits for them, and re-layouts  54.9 us
    ppermute x29, waiting for transfers between devices, swap(): return lax.ppermute(value, axis, [(0, 1), (1, 0)])  48.8 us
    all_to_all x6, starting transfers between devices, swap_group(): return lax.all_to_all(value, axes, split_axis=0, concat_axis=0, tiled=True)  37.3 us
    all_to_all x6, waiting for transfers between devices, swap_group(): return lax.all_to_all(value, axes, split_axis=0, concat_axis=0, tiled=True)  36.8 us
  transfers between devices with their start and end apart: 105, of which 38 were waited for; matrix products, arithmetic and copies ran while one was open for 28% of the time, Pallas kernels for 16%

profile of v4, /device:TPU:0, one launch (start us, length us, event | category | flops | bytes accessed | tf_op | source)
XLA Modules:
  0.0 991.6 jit_solution(7452326662144256283)
XLA Ops:
  31.3 14.5 %all-to-all-done = bf16[8,9,5280]{2,1,0:T(8,128)(2,1)S(1)} async-done(((bf16[8,9,5280]{2,1,0:T(8,128)(2,1)}), bf16[8,9,5280]{2,1,0:T(8,128)(2,1)S(1)}, u32[]{:S(2)}, u32[]{:S(2)}) %all-to-all-start) | async-done | bytes 760352 | tf_op jit(solution)/shard_map/all_to_all | solution.py:265
  50.1 8.1 collective-permute-start.3
  61.4 15.2 %collective-permute-done.7 = bf16[72,2176]{1,0:T(8,128)(2,1)S(1)} collective-permute-done((bf16[72,2176]{1,0:T(8,128)(2,1)S(1)}, bf16[72,2176]{1,0:T(8,128)(2,1)S(1)}, u32[]{:S(2)}, u32[]{:S(2)}) %collective-permute-start.7) | collective-permute-done | bytes 313376 | tf_op jit(solution)/shard_map/ppermute | solution.py:35
  90.7 16.1 %collective-permute-done.10 = bf16[4,72,1536]{2,1,0:T(8,128)(2,1)S(1)} collective-permute-done((bf16[4,72,1536]{2,1,0:T(8,128)(2,1)S(1)}, bf16[4,72,1536]{2,1,0:T(8,128)(2,1)S(1)}, u32[]{:S(2)}, u32[]{:S(2)}) %collective-permute-start.10) | collective-permute-done | bytes 884768 | tf_op jit(solution)/shard_map/ppermute | solution.py:35
  163.6 11.3 %all-to-all-done.1 = f32[128,1,1728]{2,1,0:T(1,128)S(1)} async-done(((f32[128,1,1728]{2,1,0:T(1,128)}), f32[128,1,1728]{2,1,0:T(1,128)S(1)}, u32[]{:S(2)}, u32[]{:S(2)}) %all-to-all-start.1) | async-done | bytes 884768 | tf_op jit(solution)/shard_map/all_to_all | solution.py:265
  184.5 9.2 collective-permute-done.20.refs_1_
  230.0 7.8 shard_map.352
  240.4 10.8 %shard_map.353 = (bf16[320,1152]{1,0:T(8,128)(2,1)S(1)}, bf16[4,320,640]{2,1,0:T(8,128)(2,1)S(1)}, bf16[4,320,144]{2,1,0:T(8,128)(2,1)S(1)}) custom-call(f32[320,1152]{1,0:T(8,128)S(1)} %get-tuple-element.369.x_ref, f32[1,1152]{1,0:T(1,128)S(1)} %get-tuple-element.540.shift_ref, f32[1,1152]{1,0:T(1,128)S(1)} %get-tuple-element.539.scale_ref, ...), custom_call_target="tpu_custom_call" | custom-call | tf_op jit(solution)/shard_map/pallas_call | solution.py:358
  280.1 10.6 %shard_map.357 = (bf16[320,1152]{1,0:T(8,128)(2,1)S(1)}, f32[4,320,640]{2,1,0:T(8,128)}, bf16[4,320,576]{2,1,0:T(8,128)(2,1)S(1)}, bf16[320,1152]{1,0:T(8,128)(2,1)S(1)}) custom-call(f32[320,1152]{1,0:T(8,128)S(1)} %get-tuple-element.332.x_ref, f32[1,1152]{1,0:T(1,128)S(1)} %get-tuple-element.534.shift_ref, f32[1,1152]{1,0:T(1,128)S(1)} %get-tuple-element.533.scale_ref, ...), custom_call_target="tpu_custom_call" | custom-call | tf_op jit(solution)/shard_map/pallas_call | solution.py:358
  311.9 9.2 shard_map.358
  372.4 7.8 shard_map.361
  438.1 10.7 %shard_map.364 = (bf16[320,1152]{1,0:T(8,128)(2,1)S(1)}, f32[4,320,640]{2,1,0:T(8,128)}, bf16[4,320,576]{2,1,0:T(8,128)(2,1)S(1)}, bf16[320,1152]{1,0:T(8,128)(2,1)S(1)}) custom-call(f32[320,1152]{1,0:T(8,128)S(1)} %copy-done.5, f32[1,1152]{1,0:T(1,128)S(1)} %get-tuple-element.522.shift_ref, f32[1,1152]{1,0:T(1,128)S(1)} %get-tuple-element.521.scale_ref, ...), custom_call_target="tpu_custom_call" | custom-call | tf_op jit(solution)/shard_map/pallas_call | solution.py:358
  448.7 17.8 %shard_map.365 = (bf16[4,1152,640]{2,1,0:T(8,128)(2,1)}, bf16[4,4,4,72,640]{4,3,2,1,0:T(8,128)(2,1)}, bf16[320,1152]{1,0:T(8,128)(2,1)S(1)}) custom-call(bf16[320,1152]{1,0:T(8,128)(2,1)S(1)} %copy-done.31, f32[4,320,640]{2,1,0:T(8,128)} %get-tuple-element.213.inner_ref, bf16[4,320,576]{2,1,0:T(8,128)(2,1)S(1)} %get-tuple-element.214.active_ref, ...), custom_call_target="tpu_custom_call" | custom-call | tf_op jit(solution)/shard_map/pallas_call | solution.py:358
  512.5 9.6 shard_map.367
  561.4 21.2 %shard_map.369 = (bf16[4,1152,896]{2,1,0:T(8,128)(2,1)}, bf16[320,1152]{1,0:T(8,128)(2,1)S(1)}) custom-call(bf16[4,320,640]{2,1,0:T(8,128)(2,1)} %copy-done.45, bf16[4,320,144]{2,1,0:T(8,128)(2,1)S(1)} %copy-done.32, bf16[4,1152,896]{2,1,0:T(8,128)(2,1)} %all-gather.9.cloned.1.call-done.weight_ref.refs_2_, bf16[320,1152]{1,0:T(8,128)(2,1)S(1)} %copy-done.55, ...), custom_call_target="tpu_custom_call" | custom-call | tf_op jit(solution)/shard_map/pallas_call | solution.py:358
  600.7 18.4 %collective-permute-done.51 = bf16[2,80,1152]{2,1,0:T(8,128)(2,1)S(1)} collective-permute-done((bf16[2,80,1152]{2,1,0:T(8,128)(2,1)S(1)}, bf16[2,80,1152]{2,1,0:T(8,128)(2,1)S(1)}, u32[]{:S(2)}, u32[]{:S(2)}) %collective-permute-start.51) | collective-permute-done | bytes 368672 | tf_op jit(solution)/shard_map/ppermute | solution.py:39
  620.8 17.6 %shard_map.370 = (bf16[4,1152,640]{2,1,0:T(8,128)(2,1)}, bf16[4,4,4,72,640]{4,3,2,1,0:T(8,128)(2,1)}, bf16[320,1152]{1,0:T(8,128)(2,1)S(1)}) custom-call(bf16[320,1152]{1,0:T(8,128)(2,1)S(1)} %fusion.13.grad_ref, f32[4,320,640]{2,1,0:T(8,128)} %get-tuple-element.228.inner_ref, bf16[4,320,576]{2,1,0:T(8,128)(2,1)S(1)} %copy-done.44, ...), custom_call_target="tpu_custom_call" | custom-call | tf_op jit(solution)/shard_map/pallas_call | solution.py:358
  674.3 20.0 %shard_map.372 = (bf16[4,1152,384]{2,1,0:T(8,128)(2,1)}, bf16[4,1152,256]{2,1,0:T(8,128)(2,1)}, bf16[320,1152]{1,0:T(8,128)(2,1)S(1)}) custom-call(bf16[4,320,640]{2,1,0:T(8,128)(2,1)S(1)} %copy-done.42, bf16[4,320,144]{2,1,0:T(8,128)(2,1)S(1)} %fusion.20.refs_1_, bf16[4,1152,640]{2,1,0:T(8,128)(2,1)} %bitcast.553, bf16[320,1152]{1,0:T(8,128)(2,1)S(1)} %copy-done.51, ...), custom_call_target="tpu_custom_call" | custom-call | tf_op jit(solution)/shard_map/pallas_call | solution.py:358
  738.6 13.1 %collective-permute-done.66 = bf16[2,4,72,256]{3,2,1,0:T(8,128)(2,1)S(1)} collective-permute-done((bf16[2,4,72,256]{3,2,1,0:T(8,128)(2,1)S(1)}, bf16[2,4,72,256]{3,2,1,0:T(8,128)(2,1)S(1)}, u32[]{:S(2)}, u32[]{:S(2)}) %collective-permute-start.66) | collective-permute-done | bytes 294944 | tf_op jit(solution)/shard_map/ppermute | solution.py:35
  752.5 20.9 %collective-permute-done.64 = bf16[2,4,72,384]{3,2,1,0:T(8,128)(2,1)S(1)} collective-permute-done((bf16[2,4,72,384]{3,2,1,0:T(8,128)(2,1)S(1)}, bf16[2,4,72,384]{3,2,1,0:T(8,128)(2,1)S(1)}, u32[]{:S(2)}, u32[]{:S(2)}) %collective-permute-start.64) | collective-permute-done | bytes 442400 | tf_op jit(solution)/shard_map/ppermute | solution.py:35
  808.4 40.0 %collective-permute-done.63 = bf16[4,4,72,640]{3,2,1,0:T(8,128)(2,1)} collective-permute-done((bf16[4,4,72,640]{3,2,1,0:T(8,128)(2,1)}, bf16[4,4,72,640]{3,2,1,0:T(8,128)(2,1)}, u32[]{:S(2)}, u32[]{:S(2)}) %collective-permute-start.63) | collective-permute-done | bytes 1474592 | tf_op jit(solution)/shard_map/ppermute | solution.py:35
  855.2 15.5 %collective-permute-done.71 = bf16[4,4,72,256]{3,2,1,0:T(8,128)(2,1)S(1)} collective-permute-done((bf16[4,4,72,256]{3,2,1,0:T(8,128)(2,1)S(1)}, bf16[4,4,72,256]{3,2,1,0:T(8,128)(2,1)S(1)}, u32[]{:S(2)}, u32[]{:S(2)}) %collective-permute-start.71) | collective-permute-done | bytes 589856 | tf_op jit(solution)/shard_map/ppermute | solution.py:35
  894.9 10.4 %all-to-all-start.3 = ((f32[128,1,384]{2,1,0:T(1,128)}), f32[128,1,384]{2,1,0:T(1,128)}, u32[]{:S(2)}, u32[]{:S(2)}) async-start(f32[128,1,384]{2,1,0:T(1,128)} %broadcast_in_dim.96), calls=%async_computation.5 | async-start | bytes 393216 | tf_op jit(solution)/shard_map/all_to_all | solution.py:265
  952.3 11.0 %all-to-all-done.4 = bf16[8,9,2592]{2,1,0:T(8,128)(2,1)S(1)} async-done(((bf16[8,9,2592]{2,1,0:T(8,128)(2,1)}), bf16[8,9,2592]{2,1,0:T(8,128)(2,1)S(1)}, u32[]{:S(2)}, u32[]{:S(2)}) %all-to-all-start.4) | async-done | bytes 373280 | tf_op jit(solution)/shard_map/all_to_all | solution.py:265
  (921 shorter events, 624.4 us)
Async XLA Ops:
  21.8 126.8 %all-gather.15.cloned.1.call-start = ((), (), s32[]{:S(2)}) async-start(), calls=%async_computation.23 | async-start | bytes 5529600 | tf_op jit(solution)/shard_map/all_gather | solution.py:866
  79.1 201.0 %all-gather.7.cloned.1.call-start = ((), (), s32[]{:S(2)}) async-start(), calls=%async_computation.13 | async-start | bytes 7372800 | tf_op jit(solution)/shard_map/all_gather | solution.py:886
  128.9 181.6 %all-gather.9.cloned.1.call-start = ((), (), s32[]{:S(2)}) async-start(), calls=%async_computation.14 | async-start | bytes 10321920 | tf_op jit(solution)/shard_map/all_gather | solution.py:887
  129.6 214.8 %all-gather.11.cloned.1.call-start = ((), (), s32[]{:S(2)}) async-start(), calls=%async_computation.15 | async-start | bytes 6553600 | tf_op jit(solution)/shard_map/all_gather | solution.py:888
  148.5 288.2 %all-gather.13.cloned.1.call-start = ((), (), s32[]{:S(2)}) async-start(), calls=%async_computation.16 | async-start | bytes 7372800 | tf_op jit(solution)/shard_map/all_gather | solution.py:889
  295.6 259.2 %reduce-scatter.10.cloned.1.call-start = ((), (), s32[]{:S(2)}) async-start(), calls=%async_computation.17 | async-start | bytes 7372800 | tf_op jit(solution)/shard_map/reduce_scatter | solution.py:784
  328.3 56.7 %collective-permute-start.44 = (bf16[2,80,1152]{2,1,0:T(8,128)(2,1)}, bf16[2,80,1152]{2,1,0:T(8,128)(2,1)}, u32[]{:S(2)}, u32[]{:S(2)}) collective-permute-start(bf16[2,80,1152]{2,1,0:T(8,128)(2,1)} %get-tuple-element.406), channel_id=1, source_target_pairs={{0,2},{2,0},{1,3},{3,1},{4,6},{6,4},{5,7},{7,5},{8,10},{10,8},{9,1... | collective-permute-start | bytes 1105928 | tf_op jit(solution)/shard_map/ppermute | solution.py:39
  467.5 121.8 %reduce-scatter.12.cloned.1.call-start = ((), (), s32[]{:S(2)}) async-start(), calls=%async_computation.18 | async-start | bytes 7372800 | tf_op jit(solution)/shard_map/reduce_scatter | solution.py:784
  468.2 226.1 %reduce-scatter.14.cloned.1.call-start = ((), (), s32[]{:S(2)}) async-start(), calls=%async_computation.19 | async-start | bytes 10321920 | tf_op jit(solution)/shard_map/reduce_scatter | solution.py:784
  589.3 291.2 %reduce-scatter.16.cloned.1.call-start = ((), (), s32[]{:S(2)}) async-start(), calls=%async_computation.20 | async-start | bytes 6266880 | tf_op jit(solution)/shard_map/reduce_scatter | solution.py:1028
  699.9 229.9 %reduce-scatter.18.cloned.1.call-start = ((), (), s32[]{:S(2)}) async-start(), calls=%async_computation.21 | async-start | bytes 6553600 | tf_op jit(solution)/shard_map/reduce_scatter | solution.py:1007
  730.0 72.1 %collective-permute-start.60 = (bf16[4,4,72,640]{3,2,1,0:T(8,128)(2,1)}, bf16[4,4,72,640]{3,2,1,0:T(8,128)(2,1)}, u32[]{:S(2)}, u32[]{:S(2)}) collective-permute-start(bf16[4,4,72,640]{3,2,1,0:T(8,128)(2,1)} %pad_maximum_fusion.4), channel_id=1, source_target_pairs={{24,0},{0,8},{8,16},{16,24},{25,1},{1,9},{9,17},{17,25},{26,2},{2,... | collective-permute-start | bytes 4423688 | tf_op jit(solution)/shard_map/ppermute | solution.py:35
  731.8 41.7 %collective-permute-start.64 = (bf16[2,4,72,384]{3,2,1,0:T(8,128)(2,1)S(1)}, bf16[2,4,72,384]{3,2,1,0:T(8,128)(2,1)S(1)}, u32[]{:S(2)}, u32[]{:S(2)}) collective-permute-start(bf16[2,4,72,384]{3,2,1,0:T(8,128)(2,1)S(1)} %get-tuple-element.399), channel_id=1, source_target_pairs={{24,0},{0,8},{8,16},{16,24},{25,1},{1,9},{9,17},{17,25},{26,2},{2,... | collective-permute-start | bytes 1327112 | tf_op jit(solution)/shard_map/ppermute | solution.py:35
  731.8 43.9 %collective-permute-start.65 = (bf16[2,4,72,384]{3,2,1,0:T(8,128)(2,1)S(1)}, bf16[2,4,72,384]{3,2,1,0:T(8,128)(2,1)S(1)}, u32[]{:S(2)}, u32[]{:S(2)}) collective-permute-start(bf16[2,4,72,384]{3,2,1,0:T(8,128)(2,1)S(1)} %get-tuple-element.398), channel_id=1, source_target_pairs={{8,0},{16,8},{24,16},{0,24},{9,1},{17,9},{25,17},{1,25},{10,2},{18... | collective-permute-start | bytes 1327112 | tf_op jit(solution)/shard_map/ppermute | solution.py:35
  751.7 53.2 %collective-permute-start.61 = (bf16[4,4,72,640]{3,2,1,0:T(8,128)(2,1)}, bf16[4,4,72,640]{3,2,1,0:T(8,128)(2,1)}, u32[]{:S(2)}, u32[]{:S(2)}) collective-permute-start(bf16[4,4,72,640]{3,2,1,0:T(8,128)(2,1)} %pad_maximum_fusion.5), channel_id=1, source_target_pairs={{8,0},{16,8},{24,16},{0,24},{9,1},{17,9},{25,17},{1,25},{10,2},{18... | collective-permute-start | bytes 4423688 | tf_op jit(solution)/shard_map/ppermute | solution.py:35
  752.3 54.2 %collective-permute-start.62 = (bf16[4,4,72,640]{3,2,1,0:T(8,128)(2,1)}, bf16[4,4,72,640]{3,2,1,0:T(8,128)(2,1)}, u32[]{:S(2)}, u32[]{:S(2)}) collective-permute-start(bf16[4,4,72,640]{3,2,1,0:T(8,128)(2,1)} %pad_maximum_fusion.6), channel_id=1, source_target_pairs={{96,0},{0,32},{32,64},{64,96},{97,1},{1,33},{33,65},{65,97},{98,2}... | collective-permute-start | bytes 4423688 | tf_op jit(solution)/shard_map/ppermute | solution.py:35
  773.4 75.0 %collective-permute-start.63 = (bf16[4,4,72,640]{3,2,1,0:T(8,128)(2,1)}, bf16[4,4,72,640]{3,2,1,0:T(8,128)(2,1)}, u32[]{:S(2)}, u32[]{:S(2)}) collective-permute-start(bf16[4,4,72,640]{3,2,1,0:T(8,128)(2,1)} %pad_maximum_fusion.7), channel_id=1, source_target_pairs={{32,0},{64,32},{96,64},{0,96},{33,1},{65,33},{97,65},{1,97},{34,2}... | collective-permute-start | bytes 4423688 | tf_op jit(solution)/shard_map/ppermute | solution.py:35
  789.4 81.2 %collective-permute-start.68 = (bf16[4,4,72,384]{3,2,1,0:T(8,128)(2,1)}, bf16[4,4,72,384]{3,2,1,0:T(8,128)(2,1)}, u32[]{:S(2)}, u32[]{:S(2)}) collective-permute-start(bf16[4,4,72,384]{3,2,1,0:T(8,128)(2,1)} %pad_maximum_fusion.9), channel_id=1, source_target_pairs={{24,0},{0,8},{8,16},{16,24},{25,1},{1,9},{9,17},{17,25},{26,2},{2,... | collective-permute-start | bytes 2654216 | tf_op jit(solution)/shard_map/ppermute | solution.py:35
  795.7 95.6 %all-to-all-start.2 = ((f32[128,1,1920]{2,1,0:T(1,128)}), f32[128,1,1920]{2,1,0:T(1,128)}, u32[]{:S(2)}, u32[]{:S(2)}) async-start(f32[128,1,1920]{2,1,0:T(1,128)} %all_to_all.32), calls=%async_computation.4 | async-start | bytes 1966080 | tf_op jit(solution)/shard_map/all_to_all | solution.py:265
  802.0 135.7 %reduce-scatter.22.cloned.1.call-start = ((), (), s32[]{:S(2)}) async-start(), calls=%async_computation.24 | async-start | bytes 1566720
  802.1 68.5 %collective-permute-start.69 = (bf16[4,4,72,384]{3,2,1,0:T(8,128)(2,1)}, bf16[4,4,72,384]{3,2,1,0:T(8,128)(2,1)S(1)}, u32[]{:S(2)}, u32[]{:S(2)}) collective-permute-start(bf16[4,4,72,384]{3,2,1,0:T(8,128)(2,1)} %pad_maximum_fusion.10), channel_id=1, source_target_pairs={{8,0},{16,8},{24,16},{0,24},{9,1},{17,9},{25,17},{1,25},{10,2},{18... | collective-permute-start | bytes 2654216 | tf_op jit(solution)/shard_map/ppermute | solution.py:35
  804.9 50.2 %collective-permute-start.70 = (bf16[4,4,72,256]{3,2,1,0:T(8,128)(2,1)}, bf16[4,4,72,256]{3,2,1,0:T(8,128)(2,1)S(1)}, u32[]{:S(2)}, u32[]{:S(2)}) collective-permute-start(bf16[4,4,72,256]{3,2,1,0:T(8,128)(2,1)} %pad_maximum_fusion.17), channel_id=1, source_target_pairs={{96,0},{0,32},{32,64},{64,96},{97,1},{1,33},{33,65},{65,97},{98,2}... | collective-permute-start | bytes 1769480 | tf_op jit(solution)/shard_map/ppermute | solution.py:35
  806.5 64.1 %collective-permute-start.71 = (bf16[4,4,72,256]{3,2,1,0:T(8,128)(2,1)S(1)}, bf16[4,4,72,256]{3,2,1,0:T(8,128)(2,1)S(1)}, u32[]{:S(2)}, u32[]{:S(2)}) collective-permute-start(bf16[4,4,72,256]{3,2,1,0:T(8,128)(2,1)S(1)} %copy-done.93), channel_id=1, source_target_pairs={{32,0},{64,32},{96,64},{0,96},{33,1},{65,33},{97,65},{1,97},{34,2}... | collective-permute-start | bytes 1769480 | tf_op jit(solution)/shard_map/ppermute | solution.py:35
  905.4 58.0 %reduce-scatter.20.cloned.1.call-start = ((), (), s32[]{:S(2)}) async-start(), calls=%async_computation.22 | async-start | bytes 1638400 | tf_op jit(solution)/shard_map/reduce_scatter | solution.py:1009
  (225 other events, 2072.7 us)
Sparse Core Ops, SparseCore 0:
  79.2 46.6 all-gather.14
  129.0 71.5 all-gather.6
  202.3 82.6 all-gather.8
  286.4 57.9 all-gather.10
  346.0 62.8 all-gather.12
  467.6 58.0 reduce-scatter.9
  528.1 61.1 reduce-scatter.11
  591.8 86.3 reduce-scatter.13
  700.1 59.2 reduce-scatter.15
  761.7 107.8 reduce-scatter.17
  880.7 23.9 reduce-scatter.21
  930.0 25.9 reduce-scatter.19
